TPU v7x, 32 devices: a whole 2x2x4 slice. The times are simulated.
32 devices in a mesh: dp: 8 (over z, core), tensor: 4 (over y, x).
Axes of the slice: x: 2, y: 2, z: 4, core: 2. Of those that a mesh axis runs over, the one named last changes fastest.
Arguments:
- history: bfloat16 [4, 1536, 4096], P(None, 'dp'), may hold values from -6 to 6
- depth_weights: float32 [4], replicated, may hold values from 0.2 to 1
- depth_index: int32 [4], replicated, may hold values from 0 to 3
- gain: float32 [4096], replicated, may hold values from 0.1 to 1.9
- gate_blocks: bfloat16 [896, 128, 128], P(('tensor', 'dp')), may hold values from -0.1875 to 0.1875
- up_blocks: bfloat16 [896, 128, 128], P(('tensor', 'dp')), may hold values from -0.1875 to 0.1875
- down_blocks: bfloat16 [896, 128, 128], P(('tensor', 'dp')), may hold values from -0.09375 to 0.09375
- block_ids: int32 [896, 2], P('tensor'), may hold values from 0 to 31, as said below
- grad_out: bfloat16 [1536, 4096], P('dp'), may hold values from -16 to 16
Outputs:
- layer_out: bfloat16 [1536, 4096], P('dp', 'tensor')
- grad_mixed: float32 [1536, 4096], P('dp', 'tensor')
- grad_gate: float32 [896, 128, 128], P(('tensor', 'dp'))
- grad_up: float32 [896, 128, 128], P(('tensor', 'dp'))
- grad_down: float32 [896, 128, 128], P(('tensor', 'dp'))
- grad_depth: float32 [4], replicated
- grad_gain: float32 [4096], P('tensor')
Inputs may be any that keep to these rules, and one draw needn't show every extreme that they name: `block_ids`: within the 224 rows of one index of tensor the pairs are distinct; column 0 is a row block below 32, column 1 a column block below 28 counted within that index's hidden units.
All inputs are finite; a program needn't handle non-finite values.
Results may differ from a plain program's by a relative error of at most 0.025.
Values may be sent and summed in bfloat16 or wider, within the bound.
A program may use at most 192 MiB of HBM per device.

v0:
```python
import jax
import jax.numpy as jnp
from jax import lax
from jax.sharding import PartitionSpec as P

FF = 14336


EPSILON = 1e-05


def norm_rows(mixed, gain):
    scale_inv = lax.rsqrt(jnp.mean(mixed * mixed, axis=-1, keepdims=True) + EPSILON)
    return mixed * scale_inv * gain


def per_device(
    history,
    depth_weights,
    depth_index,
    gain,
    gate_blocks,
    up_blocks,
    down_blocks,
    block_ids,
    grad_out,
):
    tok_rows = history.shape[1]
    width = history.shape[2]
    block_size = gate_blocks.shape[1]
    row_blocks = width // block_size
    tensor_count = lax.axis_size("tensor")
    col_blocks = FF // block_size // tensor_count
    share_width = width // tensor_count
    share_start = lax.axis_index("tensor") * share_width
    mixed = jnp.zeros((tok_rows, width), jnp.float32)
    for layer_slot in range(depth_index.shape[0]):
        earlier = lax.dynamic_index_in_dim(history, depth_index[layer_slot], 0, keepdims=False)
        mixed = mixed + depth_weights[layer_slot] * earlier.astype(jnp.float32)
    scale_inv = lax.rsqrt(jnp.mean(mixed * mixed, axis=-1, keepdims=True) + EPSILON)
    normed = (mixed * scale_inv * gain).astype(jnp.bfloat16)
    normed3 = normed.reshape(tok_rows, row_blocks, block_size)
    out3 = grad_out.reshape(tok_rows, row_blocks, block_size)
    row_ids = block_ids[:, 0]
    col_ids = block_ids[:, 1]
    zero_cols = jnp.zeros((tok_rows, col_blocks, block_size), jnp.float32)
    zero_rows = jnp.zeros((tok_rows, row_blocks, block_size), jnp.float32)

    def select():
        return (row_ids, col_ids)

    gate_all, up_all, down_all = (
        lax.all_gather(gate_blocks, "dp", axis=0, tiled=True),
        lax.all_gather(up_blocks, "dp", axis=0, tiled=True),
        lax.all_gather(down_blocks, "dp", axis=0, tiled=True),
    )
    pieces = (gate_all, up_all)
    rows_here, cols_here = select()
    picked = jnp.take(normed3, rows_here, axis=1)
    gate_part = jnp.einsum("tbi,bij->tbj", picked, pieces[0], preferred_element_type=jnp.float32)
    up_part = jnp.einsum("tbi,bij->tbj", picked, pieces[1], preferred_element_type=jnp.float32)
    gate_pre = zero_cols.at[:, cols_here].add(gate_part)
    up_pre = zero_cols.at[:, cols_here].add(up_part)
    hidden = (jax.nn.silu(gate_pre) * up_pre).astype(jnp.bfloat16)
    rows_here, cols_here = select()
    picked = jnp.take(hidden, cols_here, axis=1)
    product = jnp.einsum("tbi,bij->tbj", picked, down_all, preferred_element_type=jnp.float32)
    ffn3 = zero_rows.at[:, rows_here].add(product)
    ffn_share = lax.psum_scatter(
        ffn3.reshape(tok_rows, width).astype(jnp.bfloat16),
        "tensor",
        scatter_dimension=1,
        tiled=True,
    ).astype(jnp.float32)
    mixed_share = lax.dynamic_slice_in_dim(mixed, share_start, share_width, 1)
    layer_out = (mixed_share + ffn_share).astype(jnp.bfloat16)
    rows_here, cols_here = select()
    picked = jnp.take(out3, rows_here, axis=1)
    product = jnp.einsum("tbj,bij->tbi", picked, down_all, preferred_element_type=jnp.float32)
    grad_hidden = zero_cols.at[:, cols_here].add(product)
    sigmoid_gate = jax.nn.sigmoid(gate_pre)
    grad_gate_pre = (
        grad_hidden * up_pre * sigmoid_gate * (1.0 + gate_pre * (1.0 - sigmoid_gate))
    ).astype(jnp.bfloat16)
    grad_up_pre = (grad_hidden * gate_pre * sigmoid_gate).astype(jnp.bfloat16)
    pieces = (gate_all, up_all)
    rows_here, cols_here = select()
    picked_gate = jnp.take(grad_gate_pre, cols_here, axis=1)
    picked_up = jnp.take(grad_up_pre, cols_here, axis=1)
    contrib = jnp.einsum("tbj,bij->tbi", picked_gate, pieces[0], preferred_element_type=jnp.float32)
    contrib = contrib + jnp.einsum(
        "tbj,bij->tbi", picked_up, pieces[1], preferred_element_type=jnp.float32
    )
    grad_normed3 = zero_rows.at[:, rows_here].add(contrib)
    rows_here, cols_here = select()
    picked_in = jnp.take(normed3, rows_here, axis=1)
    picked_out = jnp.take(out3, rows_here, axis=1)
    picked_gate = jnp.take(grad_gate_pre, cols_here, axis=1)
    picked_up = jnp.take(grad_up_pre, cols_here, axis=1)
    picked_hidden = jnp.take(hidden, cols_here, axis=1)
    gate_term = jnp.einsum(
        "tbi,tbj->bij", picked_in, picked_gate, preferred_element_type=jnp.float32
    )
    up_term = jnp.einsum("tbi,tbj->bij", picked_in, picked_up, preferred_element_type=jnp.float32)
    down_term = jnp.einsum(
        "tbi,tbj->bij", picked_hidden, picked_out, preferred_element_type=jnp.float32
    )
    block_grads = lax.psum_scatter(
        jnp.stack([gate_term, up_term, down_term], axis=1).astype(jnp.bfloat16),
        "dp",
        scatter_dimension=0,
        tiled=True,
    ).astype(jnp.float32)
    grad_normed = grad_normed3.reshape(tok_rows, width)
    full_grad = lax.psum(grad_normed.astype(jnp.bfloat16), "tensor").astype(jnp.float32)
    ignored, pull_back = jax.vjp(norm_rows, mixed, gain)
    grad_x, gain_rows = pull_back(full_grad)
    grad_full = grad_out.astype(jnp.float32) + grad_x
    grad_mixed = lax.dynamic_slice_in_dim(grad_full, share_start, share_width, 1)
    gain_part = lax.dynamic_slice_in_dim(gain_rows, share_start, share_width, 0)
    depth_list = []
    for layer_slot in range(depth_index.shape[0]):
        earlier = lax.dynamic_index_in_dim(history, depth_index[layer_slot], 0, keepdims=False)
        depth_list.append(jnp.sum(grad_full * earlier.astype(jnp.float32)))
    gain_sum, depth_sum = lax.psum((gain_part, jnp.stack(depth_list)), "dp")
    return (
        layer_out,
        grad_mixed,
        block_grads[:, 0],
        block_grads[:, 1],
        block_grads[:, 2],
        depth_sum,
        gain_sum,
    )


def solution(mesh):
    placed = (
        P(None, "dp", None),
        P(),
        P(),
        P(),
        P(("tensor", "dp"), None, None),
        P(("tensor", "dp"), None, None),
        P(("tensor", "dp"), None, None),
        P("tensor", None),
        P("dp", None),
    )
    return jax.shard_map(
        per_device,
        mesh=mesh,
        in_specs=placed,
        out_specs=(
            P("dp", "tensor"),
            P("dp", "tensor"),
            P(("tensor", "dp"), None, None),
            P(("tensor", "dp"), None, None),
            P(("tensor", "dp"), None, None),
            P(),
            P("tensor"),
        ),
        check_vma=False,
    )
```

profile of v0, /device:TPU:0, one launch (start us, length us, event | category | flops | bytes accessed | tf_op | source)
XLA Modules:
  0.0 960.3 jit_solution(14865432137281903188)
XLA Ops:
  20.0 7.3 fusion.55
  28.6 5.6 multiply_reduce_fusion
  36.8 10.8 %gather_fusion = bf16[224,192,128]{2,1,0:T(8,128)(2,1)} fusion(bf16[192,32,128]{2,0,1:T(8,128)(2,1)S(1)} %fusion.61, s32[1024]{0:T(1024)S(1)} %pad_clamp_fusion.1), kind=kCustom, calls=%fused_computation.clone | custom fusion | bytes 22020992 | tf_op jit(solution)/shard_map/jit(_take)/gather | solution.py:59
  48.0 10.2 %gather_fusion.2 = bf16[224,192,128]{2,1,0:T(8,128)(2,1)} fusion(bf16[192,32,128]{2,0,1:T(8,128)(2,1)S(1)} %copy_bitcast_fusion.2, s32[1024]{0:T(1024)S(1)} %pad_clamp_fusion.1), kind=kCustom, calls=%fused_computation.2.clone | custom fusion | bytes 22020992 | tf_op jit(solution)/shard_map/jit(_take)/gather | solution.py:78
  58.2 27.6 %all-gather.4.cloned.1.call-done = bf16[224,128,128]{2,1,0:T(8,128)(2,1)} async-done(((bf16[28,128,128]{2,1,0:T(8,128)(2,1)}), bf16[224,128,128]{2,1,0:T(8,128)(2,1)}) %all-gather.4.cloned.1.call-update) | async-done | bytes 7340048 | tf_op jit(solution)/shard_map/all_gather | solution.py:53
  85.8 14.8 %fusion.19 = f32[224,192,128]{2,1,0:T(8,128)} fusion(bf16[224,128,128]{2,1,0:T(8,128)(2,1)} %all-gather.4.cloned.1.call-done, bf16[224,192,128]{2,1,0:T(8,128)(2,1)} %gather_fusion, pred[224]{0:T(512)(128)(4,1)S(1)} %get-tuple-element.41), kind=kOutput, calls=%fused_computation.30 | convolution fusion | flops 1414791168 | bytes 40370400 | tf_op jit(solution)/shard_map/tbi,bij->tbj/dot_general | solution.py:60
  100.9 36.1 %scatter_fusion = f32[192,28,128]{2,0,1:T(8,128)S(1)} fusion(f32[192,28,128]{2,0,1:T(8,128)S(1)} %broadcast_in_dim.37.clone, s32[224]{0:T(256)S(1)} %bitcast.156, f32[224,192,128]{2,1,0:T(8,128)} %fusion.19), kind=kCustom, calls=%fused_computation.5 | custom fusion | flops 5505024 | bytes 66061184 | tf_op jit(solution)/shard_map/scatter-add | solution.py:62
  137.0 22.4 %all-gather.6.cloned.1.call-done = bf16[224,128,128]{2,1,0:T(8,128)(2,1)} async-done(((bf16[28,128,128]{2,1,0:T(8,128)(2,1)}), bf16[224,128,128]{2,1,0:T(8,128)(2,1)}) %all-gather.6.cloned.1.call-update) | async-done | bytes 7340048 | tf_op jit(solution)/shard_map/all_gather | solution.py:54
  159.4 14.8 %fusion.17 = f32[224,192,128]{2,1,0:T(8,128)} fusion(bf16[224,128,128]{2,1,0:T(8,128)(2,1)} %all-gather.6.cloned.1.call-done, bf16[224,192,128]{2,1,0:T(8,128)(2,1)} %gather_fusion, pred[224]{0:T(512)(128)(4,1)S(1)} %get-tuple-element.41), kind=kOutput, calls=%fused_computation.28 | convolution fusion | flops 1414791168 | bytes 40370400 | tf_op jit(solution)/shard_map/tbi,bij->tbj/dot_general | solution.py:61
  176.2 56.3 %scatter_fusion.1 = f32[192,28,128]{2,0,1:T(8,128)} fusion(f32[192,28,128]{2,0,1:T(8,128)} %broadcast_in_dim.37.clone.2, s32[224]{0:T(256)S(1)} %bitcast.157, f32[224,192,128]{2,1,0:T(8,128)} %fusion.17), kind=kCustom, calls=%fused_computation.6 | custom fusion | flops 5505024 | bytes 66061184 | tf_op jit(solution)/shard_map/scatter-add | solution.py:63
  233.1 19.3 %fusion.10 = f32[224,192,128]{2,1,0:T(8,128)} fusion(bf16[224,128,128]{2,1,0:T(8,128)(2,1)} %all-gather.8.cloned.1.call-done, bf16[224,192,128]{2,1,0:T(8,128)(2,1)} %gather_fusion.2, pred[224]{0:T(512)(128)(4,1)S(1)} %get-tuple-element.41), kind=kOutput, calls=%fused_computation.21 | convolution fusion | flops 1414791168 | bytes 40370400 | tf_op jit(solution)/shard_map/tbj,bij->tbi/dot_general | solution.py:79
  252.7 35.9 %scatter_fusion.3 = f32[192,28,128]{2,0,1:T(8,128)S(1)} fusion(f32[192,28,128]{2,0,1:T(8,128)S(1)} %broadcast_in_dim.37.clone.1, s32[224]{0:T(256)S(1)} %bitcast.158, f32[224,192,128]{2,1,0:T(8,128)} %fusion.10), kind=kCustom, calls=%fused_computation.8 | custom fusion | flops 5505024 | bytes 66061184 | tf_op jit(solution)/shard_map/scatter-add | solution.py:80
  288.7 4.8 multiply_convert_fusion.1
  293.5 11.5 %gather_fusion.4 = bf16[224,192,128]{2,1,0:T(8,128)(2,1)} fusion(bf16[192,28,128]{2,0,1:T(8,128)(2,1)} %get-tuple-element.25, s32[1024]{0:T(1024)S(1)} %pad_clamp_fusion), kind=kCustom, calls=%fused_computation.4.clone | custom fusion | bytes 22020992 | tf_op jit(solution)/shard_map/jit(_take)/gather | solution.py:89
  305.0 10.3 %gather_fusion.3 = bf16[224,192,128]{2,1,0:T(8,128)(2,1)} fusion(bf16[192,28,128]{2,0,1:T(8,128)(2,1)S(1)} %copy-done.2, s32[1024]{0:T(1024)S(1)} %pad_clamp_fusion), kind=kCustom, calls=%fused_computation.3.clone | custom fusion | bytes 22020992 | tf_op jit(solution)/shard_map/jit(_take)/gather | solution.py:88
  315.3 12.0 %convert_bitcast_fusion.1 = bf16[224,1,128,128]{3,2,0,1:T(8,128)(2,1)} fusion(bf16[224,192,128]{2,1,0:T(8,128)(2,1)} %gather_fusion.4, pred[224]{0:T(512)(128)(4,1)S(1)} %get-tuple-element.40, bf16[224,192,128]{2,1,0:T(8,128)(2,1)} %gather_fusion, pred[224]{0:T(512)(128)(4,1)S(1)} %get-tuple-element.41), kind=kOutput, calls=%fused_computation.38 | convolution fusion | flops 1423966208 | bytes 29360576 | tf_op jit(solution)/shard_map/tbi,tbj->bij/dot_general | solution.py:104
  327.4 12.0 %convert_bitcast_fusion.2 = bf16[224,1,128,128]{3,2,0,1:T(8,128)(2,1)} fusion(bf16[224,192,128]{2,1,0:T(8,128)(2,1)} %gather_fusion.3, pred[224]{0:T(512)(128)(4,1)S(1)} %get-tuple-element.40, bf16[224,192,128]{2,1,0:T(8,128)(2,1)} %gather_fusion, pred[224]{0:T(512)(128)(4,1)S(1)} %get-tuple-element.41), kind=kOutput, calls=%fused_computation.39 | convolution fusion | flops 1423966208 | bytes 29360576 | tf_op jit(solution)/shard_map/tbi,tbj->bij/dot_general | solution.py:101
  339.4 19.7 %fusion.2 = f32[224,192,128]{2,1,0:T(8,128)} fusion(bf16[224,128,128]{2,1,0:T(8,128)(2,1)} %all-gather.6.cloned.1.call-done, bf16[224,192,128]{2,1,0:T(8,128)(2,1)} %gather_fusion.4, pred[224]{0:T(512)(128)(4,1)S(1)} %get-tuple-element.40), kind=kOutput, calls=%fused_computation.13 | convolution fusion | flops 1414791168 | bytes 40370400 | tf_op jit(solution)/shard_map/tbj,bij->tbi/dot_general | solution.py:91
  359.1 22.5 %fusion.21 = f32[224,192,128]{2,1,0:T(8,128)} fusion(f32[224,192,128]{2,1,0:T(8,128)} %fusion.2, bf16[224,128,128]{2,1,0:T(8,128)(2,1)} %all-gather.4.cloned.1.call-done, bf16[224,192,128]{2,1,0:T(8,128)(2,1)} %gather_fusion.3, pred[224]{0:T(512)(128)(4,1)S(1)} %get-tuple-element.40), kind=kOutput, calls=%fused_computation.40 | convolution fusion | flops 1420296192 | bytes 62390496 | tf_op jit(solution)/shard_map/tbj,bij->tbi/dot_general | solution.py:90
  381.9 35.9 %scatter_fusion.4 = f32[192,32,128]{2,0,1:T(8,128)S(1)} fusion(f32[192,32,128]{2,0,1:T(8,128)S(1)} %broadcast_in_dim.36.clone.1, s32[224]{0:T(256)S(1)} %bitcast.159, f32[224,192,128]{2,1,0:T(8,128)} %fusion.21), kind=kCustom, calls=%fused_computation.9 | custom fusion | flops 5505024 | bytes 66061184 | tf_op jit(solution)/shard_map/scatter-add | solution.py:94
  420.6 10.2 %gather_fusion.1 = bf16[224,192,128]{2,1,0:T(8,128)(2,1)} fusion(bf16[192,28,128]{2,0,1:T(8,128)(2,1)S(1)} %copy-done.1, s32[1024]{0:T(1024)S(1)} %pad_clamp_fusion), kind=kCustom, calls=%fused_computation.1.clone | custom fusion | bytes 22020992 | tf_op jit(solution)/shard_map/jit(_take)/gather | solution.py:66
  430.8 14.5 %fusion.13 = f32[224,192,128]{2,1,0:T(8,128)} fusion(bf16[224,128,128]{2,1,0:T(8,128)(2,1)} %all-gather.8.cloned.1.call-done, bf16[224,192,128]{2,1,0:T(8,128)(2,1)} %gather_fusion.1, pred[224]{0:T(512)(128)(4,1)S(1)} %get-tuple-element.40), kind=kOutput, calls=%fused_computation.24 | convolution fusion | flops 1414791168 | bytes 40370400 | tf_op jit(solution)/shard_map/tbi,bij->tbj/dot_general | solution.py:67
  445.6 36.3 %scatter_fusion.2 = f32[192,32,128]{2,0,1:T(8,128)S(1)} fusion(f32[192,32,128]{2,0,1:T(8,128)S(1)} %broadcast_in_dim.36.clone, s32[224]{0:T(256)S(1)} %bitcast.160, f32[224,192,128]{2,1,0:T(8,128)} %fusion.13), kind=kCustom, calls=%fused_computation.7 | custom fusion | flops 5505024 | bytes 66061184 | tf_op jit(solution)/shard_map/scatter-add | solution.py:68
  483.3 12.4 %convert_bitcast_fusion = bf16[224,1,128,128]{3,2,0,1:T(8,128)(2,1)} fusion(bf16[224,192,128]{2,1,0:T(8,128)(2,1)} %gather_fusion.2, pred[224]{0:T(512)(128)(4,1)S(1)} %get-tuple-element.41, bf16[224,192,128]{2,1,0:T(8,128)(2,1)} %gather_fusion.1, pred[224]{0:T(512)(128)(4,1)S(1)} %get-tuple-element.40), kind=kOutput, calls=%fused_computation.37 | convolution fusion | flops 1423966208 | bytes 29360576 | tf_op jit(solution)/shard_map/tbi,tbj->bij/dot_general | solution.py:105
  495.8 19.6 %pad_maximum_fusion = bf16[224,3,128,128]{3,2,0,1:T(8,128)(2,1)} fusion(bf16[224,1,128,128]{3,2,0,1:T(8,128)(2,1)} %convert_bitcast_fusion, bf16[224,1,128,128]{3,2,0,1:T(8,128)(2,1)} %convert_bitcast_fusion.1, bf16[224,1,128,128]{3,2,0,1:T(8,128)(2,1)} %convert_bitcast_fusion.2), kind=kLoop, calls=%fused_computation.10 | loop fusion | flops 22020096 | bytes 44040192 | tf_op jit(solution)/shard_map/stack | solution.py:109
  517.3 2.9 fusion.47
  520.2 6.7 fusion.51
  527.0 2.7 pad_maximum_fusion.1
  530.3 15.7 %all-reduce.1 = (f32[4]{0:T(128)}, f32[1024]{0:T(1024)}) all-reduce(f32[4]{0:T(128)S(1)} %pad_maximum_fusion.1, f32[1024]{0:T(1024)S(1)} %dynamic_slice.32), channel_id=1, replica_groups=mesh['dp'=8,'tensor'=4] {'dp'}, use_global_device_ids=true, to_apply=%region_14.17 | all-reduce | flops 1028 | bytes 8224 | tf_op jit(solution)/shard_map/psum | solution.py:125
  549.9 398.2 %all-reduce.7.cloned.1.call-done = bf16[224,3,128,128]{3,2,0,1:T(8,128)(2,1)} async-done(((bf16[224,3,128,128]{3,2,0,1:T(8,128)(2,1)}), bf16[224,3,128,128]{3,2,0,1:T(8,128)(2,1)}) %all-reduce.7.cloned.1.call-update) | async-done | bytes 22020112
  948.1 2.5 dynamic-slice_convert_fusion
  950.6 2.6 slice_bitcast_fusion
  (75 shorter events, 23.2 us)
Async XLA Ops:
  7.2 78.6 %all-gather.4.cloned.1.call-start = ((), (), s32[]{:S(2)}) async-start(), calls=%async_computation.1 | async-start | bytes 8257536 | tf_op jit(solution)/shard_map/all_gather | solution.py:53
  7.9 151.5 %all-gather.6.cloned.1.call-start = ((), (), s32[]{:S(2)}) async-start(), calls=%async_computation.2 | async-start | bytes 8257536 | tf_op jit(solution)/shard_map/all_gather | solution.py:54
  8.6 224.5 %all-gather.8.cloned.1.call-start = ((), (), s32[]{:S(2)}) async-start(), calls=%async_computation.3 | async-start | bytes 8257536 | tf_op jit(solution)/shard_map/all_gather | solution.py:55
  8.7 19.9 %slice-start = ((s8[6291456]{0:T(1024)(128)(4,1)}), s8[2097152]{0:T(1024)(128)(4,1)S(1)}, s32[]{:S(2)}) async-start(s8[6291456]{0:T(1024)(128)(4,1)} %bitcast.152), calls=%async_computation.7 | async-start | bytes 4194304
  9.4 507.2 %all-reduce.5.cloned.1.call-start = ((), (), s32[]{:S(2)}) async-start(), calls=%async_computation.5 | async-start | bytes 3145728 | tf_op jit(solution)/shard_map/psum | solution.py:115
  20.0 8.6 slice-start.1
  27.3 0.7 copy-start.14
  28.0 6.8 copy-start.7
  34.1 13.4 %copy-start.12 = (f32[192]{0:T(256)}, f32[192]{0:T(256)S(1)}, u32[]{:S(2)}) copy-start(f32[192]{0:T(256)S(1)} %get-tuple-element.18) | copy-start | bytes 2308
  34.2 0.6 copy-start.9
  36.8 10.8 %copy-start.4 = (bf16[192,4096]{1,0:T(8,128)(2,1)S(1)}, bf16[192,4096]{1,0:T(8,128)(2,1)}, u32[]{:S(2)}) copy-start(bf16[192,4096]{1,0:T(8,128)(2,1)} %param.21) | copy-start | bytes 4718596
  137.0 37.2 %copy-start = (f32[192,28,128]{2,0,1:T(8,128)}, f32[192,28,128]{2,0,1:T(8,128)S(1)}, u32[]{:S(2)}) copy-start(f32[192,28,128]{2,0,1:T(8,128)S(1)} %scatter_fusion) | copy-start | bytes 8257540
  293.5 11.5 %copy-start.2 = (bf16[192,28,128]{2,0,1:T(8,128)(2,1)S(1)}, bf16[192,28,128]{2,0,1:T(8,128)(2,1)}, u32[]{:S(2)}) copy-start(bf16[192,28,128]{2,0,1:T(8,128)(2,1)} %get-tuple-element.23) | copy-start | bytes 4128772
  359.1 22.8 %copy-start.11 = (s32[224,1]{0,1:T(1,128)S(1)}, s32[224,1]{0,1:T(1,128)}, u32[]{:S(2)}) copy-start(s32[224,1]{0,1:T(1,128)} %get-tuple-element.27) | copy-start | bytes 2692
  419.2 1.3 copy-start.1
  419.2 128.8 %reduce-scatter.5.cloned.1.call-start = ((), (), s32[]{:S(2)}) async-start(), calls=%async_computation.4 | async-start | bytes 1966080 | tf_op jit(solution)/shard_map/reduce_scatter | solution.py:69
  483.3 464.8 %all-reduce.7.cloned.1.call-start = ((), (), s32[]{:S(2)}) async-start(), calls=%async_computation.6 | async-start | bytes 44040192
  515.3 0.7 copy-start.15
  515.3 1.9 copy-start.3
  515.4 1.9 copy-start.8
  515.4 1.9 copy-start.10
  515.4 4.8 copy-start.13
  516.6 3.6 copy-start.5
  516.6 3.6 copy-start.6
Sparse Core Ops, SparseCore 0:
  9.6 76.0 all-gather.3
  87.4 71.9 all-gather.5
  161.1 71.9 all-gather.7
  419.4 59.5 all-reduce.4
  483.4 30.0 reduce-scatter.4
  516.1 431.9 all-reduce.6
where the time goes:
time: 968 us; the launch traced here: 960 us
  waiting for transfers between devices  451 us (47%)
  other arithmetic  260 us (27%)
  matrix products  142 us (15%)
  local copies, waits for them, and re-layouts  68.5 us (7%)
  between operations  23 us (2%)
  blocking collectives  15.7 us (2%)
    unnamed x7, waiting for transfers between devices  400 us
    scatter-add x1, other arithmetic, per_device(): up_pre = zero_cols.at[:, cols_here].add(up_part)  56.3 us
    scatter-add x1, other arithmetic, per_device(): ffn3 = zero_rows.at[:, rows_here].add(product)  36.3 us
    scatter-add x1, other arithmetic, per_device(): gate_pre = zero_cols.at[:, cols_here].add(gate_part)  36.1 us
    scatter-add x1, other arithmetic, per_device(): grad_hidden = zero_cols.at[:, cols_here].add(product)  35.9 us
    scatter-add x1, other arithmetic, per_device(): grad_normed3 = zero_rows.at[:, rows_here].add(contrib)  35.9 us
    all_gather x1, waiting for transfers between devices, per_device(): lax.all_gather(gate_blocks, 'dp', axis=0, tiled=True)  27.6 us
    dot_general x1, matrix products, per_device(): jnp.einsum('tbj,bij->tbi', picked_gate, pieces[0], preferred_element_type...  22.5 us
  transfers between devices with their start and end apart: 6, of which 4 were waited for; matrix products, arithmetic and copies ran while one was open for 29% of the time, Pallas kernels for 0%

commit v1 on v0

v1 whole, which is shorter than its diff:
```python
import functools

import jax
import jax.numpy as jnp
from jax import lax
from jax.experimental import pallas as pl
from jax.experimental.pallas import tpu as pltpu
from jax.sharding import PartitionSpec as P

FF = 14336
EPSILON = 1e-05
CHUNKS = 8
UNROLL = 7
F32 = jnp.float32
BF16 = jnp.bfloat16
NN = (((1,), (0,)), ((), ()))
NT = (((1,), (1,)), ((), ()))
TN = (((0,), (0,)), ((), ()))


def dot(a, b, dims):
    return lax.dot_general(a, b, dims, preferred_element_type=F32)


def lanes(index, size):
    return pl.ds(pl.multiple_of(index * size, size), size)


def for_blocks(ids, first, count, body):
    def step(i, carry):
        for u in range(UNROLL):
            b = i * UNROLL + u
            body(b, ids[2 * (first + b)], ids[2 * (first + b) + 1])
        return carry

    lax.fori_loop(0, count // UNROLL, step, 0)


def for_columns(size, width, body):
    def step(c, carry):
        body(lanes(c, size))
        return carry

    lax.fori_loop(0, width // size, step, 0)


def gate_kernel(ids, x, w, acc):
    n, size = w.shape[0], w.shape[1]

    @pl.when(pl.program_id(0) == 0)
    def _():
        acc[...] = jnp.zeros_like(acc)

    def body(b, r, c):
        acc[:, lanes(c, size)] += dot(x[:, lanes(r, size)], w[b], NN)

    for_blocks(ids, pl.program_id(0) * n, n, body)


def up_kernel(ids, x, w, gate, acc, hidden):
    n, size = w.shape[0], w.shape[1]
    gate_kernel(ids, x, w, acc)

    @pl.when(pl.program_id(0) == pl.num_programs(0) - 1)
    def _():
        def body(cols):
            g = gate[:, cols]
            hidden[:, cols] = (g / (1.0 + jnp.exp(-g)) * acc[:, cols]).astype(BF16)

        for_columns(size, acc.shape[1], body)


def hidden_grad_kernel(ids, gout, w, gate, up, dgate, dup, acc):
    n, size = w.shape[0], w.shape[1]

    @pl.when(pl.program_id(0) == 0)
    def _():
        acc[...] = jnp.zeros_like(acc)

    def body(b, r, c):
        acc[:, lanes(c, size)] += dot(gout[:, lanes(r, size)], w[b], NT)

    for_blocks(ids, pl.program_id(0) * n, n, body)

    @pl.when(pl.program_id(0) == pl.num_programs(0) - 1)
    def _():
        def finish(cols):
            g = gate[:, cols]
            s = 1.0 / (1.0 + jnp.exp(-g))
            gh = acc[:, cols]
            dgate[:, cols] = (gh * up[:, cols] * s * (1.0 + g * (1.0 - s))).astype(BF16)
            dup[:, cols] = (gh * g * s).astype(BF16)

        for_columns(size, acc.shape[1], finish)


def ffn_kernel(ids, hidden, w, out, acc):
    n, size = w.shape[0], w.shape[1]

    @pl.when(pl.program_id(0) == 0)
    def _():
        acc[...] = jnp.zeros_like(acc)

    def body(b, r, c):
        acc[:, lanes(r, size)] += dot(hidden[:, lanes(c, size)], w[b], NN)

    for_blocks(ids, pl.program_id(0) * n, n, body)

    @pl.when(pl.program_id(0) == pl.num_programs(0) - 1)
    def _():
        out[...] = acc[...].astype(BF16)


def normed_grad_kernel(ids, dgate, dup, gate_w, up_w, out, acc):
    n, size = gate_w.shape[0], gate_w.shape[1]

    @pl.when(pl.program_id(0) == 0)
    def _():
        acc[...] = jnp.zeros_like(acc)

    def body(b, r, c):
        left = jnp.concatenate([dgate[:, lanes(c, size)], dup[:, lanes(c, size)]], axis=1)
        right = jnp.concatenate([gate_w[b], up_w[b]], axis=1)
        acc[:, lanes(r, size)] += dot(left, right, NT)

    for_blocks(ids, pl.program_id(0) * n, n, body)

    @pl.when(pl.program_id(0) == pl.num_programs(0) - 1)
    def _():
        out[...] = acc[...].astype(BF16)


def down_grad_kernel(ids, hidden, gout, out):
    n, size = out.shape[0], out.shape[1]

    def body(b, r, c):
        out[b] = dot(hidden[:, lanes(c, size)], gout[:, lanes(r, size)], TN).astype(BF16)

    for_blocks(ids, pl.program_id(0) * n, n, body)


def gate_up_grad_kernel(ids, x, dgate, dup, out_gate, out_up):
    n, size = out_gate.shape[0], out_gate.shape[1]

    def body(b, r, c):
        right = jnp.concatenate([dgate[:, lanes(c, size)], dup[:, lanes(c, size)]], axis=1)
        both = dot(x[:, lanes(r, size)], right, TN).astype(BF16)
        out_gate[b] = both[:, :size]
        out_up[b] = both[:, size:]

    for_blocks(ids, pl.program_id(0) * n, n, body)


def call(kernel, ids, whole, blocks, outs, flops, steps, acc=None, name=None):
    chunked = lambda shape: pl.BlockSpec((shape[0] // steps, *shape[1:]), lambda i, ids: (i, 0, 0))
    resident = lambda shape: pl.BlockSpec(shape, lambda i, ids: (0, 0))
    order = [(a, resident(a.shape)) if a.ndim == 2 else (a, chunked(a.shape)) for a in (*whole, *blocks)]
    out_specs = [chunked(s) if cut else resident(s) for s, _, cut in outs]
    out_shape = [jax.ShapeDtypeStruct(s, d) for s, d, _ in outs]
    moved = sum(a.size * a.dtype.itemsize for a, _ in order)
    moved += sum(s.size * s.dtype.itemsize for s in out_shape)
    return pl.pallas_call(
        kernel,
        out_shape=out_shape,
        grid_spec=pltpu.PrefetchScalarGridSpec(
            num_scalar_prefetch=1,
            grid=(steps,),
            in_specs=[s for _, s in order],
            out_specs=out_specs,
            scratch_shapes=[pltpu.VMEM(acc, F32)] if acc else [],
        ),
        compiler_params=pltpu.CompilerParams(vmem_limit_bytes=40 * 2**20),
        cost_estimate=pl.CostEstimate(flops=4 * flops, bytes_accessed=moved, transcendentals=0),
        name=name,
    )(ids, *[a for a, _ in order])


def per_device(
    history,
    depth_weights,
    depth_index,
    gain,
    gate_blocks,
    up_blocks,
    down_blocks,
    block_ids,
    grad_out,
):
    tokens, width = grad_out.shape
    owned, size = gate_blocks.shape[:2]
    tensor_count = lax.axis_size("tensor")
    dp_count = lax.axis_size("dp")
    chips = dp_count // 2
    hidden_width = FF // tensor_count
    share_width = width // tensor_count
    share_start = lax.axis_index("tensor") * share_width
    dp = lax.axis_index("dp")
    chip, core = dp // 2, dp % 2
    active = block_ids.shape[0]
    ids = block_ids.reshape(-1)
    flops = 2 * active * size * size * tokens

    gate_all = lax.all_gather(gate_blocks, "dp", axis=0, tiled=True)
    up_all = lax.all_gather(up_blocks, "dp", axis=0, tiled=True)
    down_all = lax.all_gather(down_blocks, "dp", axis=0, tiled=True)

    def share(a):
        return lax.dynamic_slice_in_dim(a, share_start, share_width, a.ndim - 1)

    mixed = jnp.zeros((tokens, width), F32)
    for slot in range(depth_index.shape[0]):
        earlier = lax.dynamic_index_in_dim(history, depth_index[slot], 0, keepdims=False)
        mixed = mixed + depth_weights[slot] * earlier.astype(F32)
    scale_inv = lax.rsqrt(jnp.mean(mixed * mixed, axis=-1, keepdims=True) + EPSILON)
    normed = (mixed * scale_inv * gain).astype(BF16)

    acts = (tokens, hidden_width)
    (gate_pre,) = call(gate_kernel, ids, [normed], [gate_all], [(acts, F32, False)], flops, CHUNKS, name="gate")
    up_pre, hidden = call(
        up_kernel, ids, [normed], [up_all, gate_pre], [(acts, F32, False), (acts, BF16, False)],
        flops, CHUNKS, name="up_hidden",
    )

    owner_ids = block_ids.reshape(chips, 2, owned, 2)

    def half_ids(which):
        return lax.dynamic_index_in_dim(owner_ids, which, 1, keepdims=False).reshape(-1)

    other_ids, own_ids = half_ids(1 - core), half_ids(core)
    half = (chips * owned, size, size)
    siblings = [(i, i ^ 1) for i in range(dp_count)]

    def down_grads(which):
        return call(
            down_grad_kernel, which, [hidden, grad_out], [], [(half, BF16, True)],
            flops // 2, chips, name="down_grad",
        )

    def line_sum(own, received):
        parts = own.astype(F32) + received.astype(F32)
        parts = parts.astype(BF16).reshape(chips, owned, size, size)
        from_below = from_above = None
        for step in range(chips - 1):
            reach = chips - 1 - step

            def piece(target, arrived):
                p = lax.dynamic_index_in_dim(parts, jnp.clip(target, 0, chips - 1), 0, keepdims=False)
                if arrived is None:
                    return p
                return (p.astype(F32) + arrived.astype(F32)).astype(BF16)

            upward = piece(chip + reach, from_below)
            downward = piece(chip - reach, from_above)
            pairs = [(z, z + 1) for z in range(min(step + 1, chips - 1))]
            up_pairs = [(2 * a + c, 2 * b + c) for a, b in pairs for c in (0, 1)]
            down_pairs = [
                (2 * (chips - 1 - a) + c, 2 * (chips - 1 - b) + c) for a, b in pairs for c in (0, 1)
            ]
            from_below = lax.ppermute(upward, "dp", up_pairs)
            from_above = lax.ppermute(downward, "dp", down_pairs)
        total = lax.dynamic_index_in_dim(parts, chip, 0, keepdims=False).astype(F32)
        if from_below is not None:
            total = total + from_below.astype(F32) + from_above.astype(F32)
        return total

    (down_other,) = down_grads(other_ids)
    down_received = lax.ppermute(down_other, "dp", siblings)
    (down_own,) = down_grads(own_ids)
    grad_down = line_sum(down_own, down_received)

    dgate, dup = call(
        hidden_grad_kernel, ids, [grad_out], [down_all, gate_pre, up_pre],
        [(acts, BF16, False), (acts, BF16, False)], flops, CHUNKS, acc=acts, name="hidden_grad",
    )

    def gate_up_grads(which):
        return call(
            gate_up_grad_kernel, which, [normed, dgate, dup], [], [(half, BF16, True), (half, BF16, True)],
            flops, chips, name="gate_up_grad",
        )

    gate_other, up_other = gate_up_grads(other_ids)
    gate_received = lax.ppermute(gate_other, "dp", siblings)
    up_received = lax.ppermute(up_other, "dp", siblings)
    gate_own, up_own = gate_up_grads(own_ids)
    grad_gate = line_sum(gate_own, gate_received)
    grad_up = line_sum(up_own, up_received)

    rows = (tokens, width)
    (ffn,) = call(
        ffn_kernel, ids, [hidden], [down_all], [(rows, BF16, False)], flops, CHUNKS, acc=rows, name="ffn"
    )
    (normed_grad,) = call(
        normed_grad_kernel, ids, [dgate, dup], [gate_all, up_all], [(rows, BF16, False)],
        2 * flops, CHUNKS, acc=rows, name="normed_grad",
    )
    ffn_share = lax.psum_scatter(ffn, "tensor", scatter_dimension=1, tiled=True).astype(F32)
    mixed_share = share(mixed)
    layer_out = (mixed_share + ffn_share).astype(BF16)

    grad_share = lax.psum_scatter(normed_grad, "tensor", scatter_dimension=1, tiled=True).astype(F32)
    gain_share = share(gain)
    along = lax.psum(jnp.sum(grad_share * gain_share * mixed_share, axis=-1, keepdims=True), "tensor")
    grad_mixed = (
        share(grad_out).astype(F32)
        + scale_inv * gain_share * grad_share
        - mixed_share * (scale_inv * scale_inv * scale_inv / width) * along
    )
    gain_part = jnp.sum(grad_share * mixed_share * scale_inv, axis=0)
    depth_list = []
    for slot in range(depth_index.shape[0]):
        earlier = lax.dynamic_index_in_dim(history, depth_index[slot], 0, keepdims=False)
        depth_list.append(jnp.sum(grad_mixed * share(earlier).astype(F32)))
    gain_sum = lax.psum(gain_part, "dp")
    depth_sum = lax.psum(jnp.stack(depth_list), ("dp", "tensor"))
    return (layer_out, grad_mixed, grad_gate, grad_up, grad_down, depth_sum, gain_sum)


def solution(mesh):
    placed = (
        P(None, "dp", None),
        P(),
        P(),
        P(),
        P(("tensor", "dp"), None, None),
        P(("tensor", "dp"), None, None),
        P(("tensor", "dp"), None, None),
        P("tensor", None),
        P("dp", None),
    )
    return jax.shard_map(
        per_device,
        mesh=mesh,
        in_specs=placed,
        out_specs=(
            P("dp", "tensor"),
            P("dp", "tensor"),
            P(("tensor", "dp"), None, None),
            P(("tensor", "dp"), None, None),
            P(("tensor", "dp"), None, None),
            P(),
            P("tensor"),
        ),
        check_vma=False,
    )
```

time: 968 us -> 584 us (0.60)
  waiting for transfers between devices: 451 us -> 234 us
  other arithmetic: 260 us -> 68.5 us
  matrix products: 142 us -> 0 us
  Pallas kernels: 0 us -> 91 us
  blocking collectives: 15.7 us -> 88.9 us
  starting transfers between devices: 0.24 us -> 44.8 us
  local copies, waits for them, and re-layouts: 68.5 us -> 32.8 us
    unnamed x7 -> x5, waiting for transfers between devices: 400 us -> 2.09 us
    scatter-add x5 -> x0, other arithmetic: 201 us -> none  [the longest x1 56.3 us: per_device(): up_pre = zero_cols.at[:, cols_here].add(up_part)]
    dot_general x9 -> x0, matrix products: 142 us -> none  [the longest x1 22.5 us: per_device(): jnp.einsum('tbj,bij->tbi', picked_gate, pieces[0], preferred_element_type...]
    all_gather x3, waiting for transfers between devices: 50.7 us -> 172 us  [the longest x1 59.5 us: per_device(): up_all = lax.all_gather(up_blocks, 'dp', axis=0, tiled=True)]
    pallas_call x0 -> x9, Pallas kernels: none -> 91 us  [call(): pl.pallas_call(kernel, out_shape=out_shape, grid_spec=pltpu.PrefetchScala...]
    psum x1 -> x3, blocking collectives: 15.7 us -> 88.9 us  [the longest x1 63.2 us: per_device(): depth_sum = lax.psum(jnp.stack(depth_list), ('dp', 'tensor'))]
    ppermute x0 -> x21, waiting for transfers between devices: none -> 60.3 us  [the longest x9 60.2 us: line_sum(): from_below = lax.ppermute(upward, 'dp', up_pairs)]
    gather x5 -> x0, local copies, waits for them, and re-layouts: 53 us -> none  [the longest x1 11.5 us: per_device(): picked_up = jnp.take(grad_up_pre, cols_here, axis=1)]
  transfers between devices with their start and end apart: 6 -> 26, of which waited for: 4 -> 8; matrix products, arithmetic and copies ran while one was open for 29% -> 13% of each run, Pallas kernels for 0% -> 12%
where the time goes in v1:
time: 584 us; the launch traced here: 582 us
  waiting for transfers between devices  234 us (40%)
  Pallas kernels  91 us (16%)
  blocking collectives  88.9 us (15%)
  other arithmetic  68.5 us (12%)
  starting transfers between devices  44.8 us (8%)
  local copies, waits for them, and re-layouts  32.8 us (6%)
  between operations  22 us (4%)
    pallas_call x9, Pallas kernels, call(): pl.pallas_call(kernel, out_shape=out_shape, grid_spec=pltpu.PrefetchScala...  91 us
    psum x1, blocking collectives, per_device(): depth_sum = lax.psum(jnp.stack(depth_list), ('dp', 'tensor'))  63.2 us
    ppermute x9, waiting for transfers between devices, line_sum(): from_below = lax.ppermute(upward, 'dp', up_pairs)  60.2 us
    all_gather x1, waiting for transfers between devices, per_device(): up_all = lax.all_gather(up_blocks, 'dp', axis=0, tiled=True)  59.5 us
    all_gather x1, waiting for transfers between devices, per_device(): down_all = lax.all_gather(down_blocks, 'dp', axis=0, tiled=True)  56.9 us
    all_gather x1, waiting for transfers between devices, per_device(): gate_all = lax.all_gather(gate_blocks, 'dp', axis=0, tiled=True)  55.5 us
    ppermute x9, starting transfers between devices, line_sum(): from_below = lax.ppermute(upward, 'dp', up_pairs)  30.1 us
    convert_element_type x9, other arithmetic, piece(): return (p.astype(F32) + arrived.astype(F32)).astype(BF16)  25.1 us
  transfers between devices with their start and end apart: 26, of which 8 were waited for; matrix products, arithmetic and copies ran while one was open for 13% of the time, Pallas kernels for 12%

profile of v1, /device:TPU:0, one launch (start us, length us, event | category | flops | bytes accessed | tf_op | source)
XLA Modules:
  0.0 582.3 jit_solution(3222769980416731779)
XLA Ops:
  21.3 6.8 %fusion.2 = (f32[192]{0:T(256)S(1)}, f32[1,192,4096]{2,1,0:T(8,128)S(1)}) fusion(bf16[4,192,4096]{2,1,0:T(8,128)(2,1)} %param.9, s32[]{:T(128)S(6)} %select_n.81, f32[]{:T(128)} %bitcast.6, s32[]{:T(128)S(6)} %select_n.80, f32[]{:T(128)} %bitcast.4, s32[]{:T(128)S(6)} %select_n.79, f32[]{:T(128)} %bitcast.2, s32[]{:T(128)S(6)} %select_n.78, f32[]{:T(128)} %bitcast), kind=kLoop, calls=%fused_computation.7 | loop fusion | flops 10223424 | bytes 9437984 | tf_op jit(solution)/shard_map/reduce_sum | solution.py:214
  30.3 55.5 %all-gather.6.cloned.1.call-done.w.gate_w = bf16[224,128,128]{2,1,0:T(8,128)(2,1)} async-done(((bf16[28,128,128]{2,1,0:T(8,128)(2,1)}), bf16[224,128,128]{2,1,0:T(8,128)(2,1)}) %all-gather.6.cloned.1.call-update) | async-done | bytes 7340048 | tf_op jit(solution)/shard_map/all_gather | solution.py:203
  88.9 9.5 %gate.1 = f32[192,3584]{1,0:T(8,128)S(1)} custom-call(s32[448]{0:T(512)S(1)} %reshape.111.ids, bf16[192,4096]{1,0:T(8,128)(2,1)S(1)} %fusion.1.x, bf16[224,128,128]{2,1,0:T(8,128)(2,1)S(1)} %copy-done.6), custom_call_target="tpu_custom_call" | custom-call | flops 5637144576 | bytes 11665408 | tf_op jit(solution)/shard_map/gate/pallas_call | solution.py:162
  100.0 59.5 %all-gather.4.cloned.1.call-done.w.up_w = bf16[224,128,128]{2,1,0:T(8,128)(2,1)} async-done(((bf16[28,128,128]{2,1,0:T(8,128)(2,1)}), bf16[224,128,128]{2,1,0:T(8,128)(2,1)}) %all-gather.4.cloned.1.call-update) | async-done | bytes 7340048 | tf_op jit(solution)/shard_map/all_gather | solution.py:204
  161.2 12.3 %up_hidden.1 = (f32[192,3584]{1,0:T(8,128)S(1)}, bf16[192,3584]{1,0:T(8,128)(2,1)S(1)}) custom-call(s32[448]{0:T(512)S(1)} %reshape.111.ids, bf16[192,4096]{1,0:T(8,128)(2,1)S(1)} %fusion.1.x, bf16[224,128,128]{2,1,0:T(8,128)(2,1)} %all-gather.4.cloned.1.call-done.w.up_w, f32[192,3584]{1,0:T(8,128)S(1)} %copy-done.12), custom_call_target="tpu_custom_call" | custom-call | flops 5637144576 | bytes 15794176 | tf_op jit(solution)/shard_map/up_hidden/pallas_call | solution.py:162
  176.2 56.9 %all-gather.8.cloned.1.call-done.w = bf16[224,128,128]{2,1,0:T(8,128)(2,1)} async-done(((bf16[28,128,128]{2,1,0:T(8,128)(2,1)}), bf16[224,128,128]{2,1,0:T(8,128)(2,1)}) %all-gather.8.cloned.1.call-update) | async-done | bytes 7340048 | tf_op jit(solution)/shard_map/all_gather | solution.py:205
  236.7 14.0 %hidden_grad.1 = (bf16[192,3584]{1,0:T(8,128)(2,1)S(1)}, bf16[192,3584]{1,0:T(8,128)(2,1)S(1)}) custom-call(s32[448]{0:T(512)S(1)} %reshape.111.ids, bf16[192,4096]{1,0:T(8,128)(2,1)S(1)} %copy-done.4, bf16[224,128,128]{2,1,0:T(8,128)(2,1)} %all-gather.8.cloned.1.call-done.w, f32[192,3584]{1,0:T(8,128)S(1)} %copy-done.13, f32[192,3584]{1,0:T(8,128)S(1)} %copy-done.15), custom_call_target="tpu_custom_call" | custom-call | flops 5637144576 | bytes 17170432 | tf_op jit(solution)/shard_map/hidden_grad/pallas_call | solution.py:162
  250.8 8.0 %gate_up_grad.3 = (bf16[112,128,128]{2,1,0:T(8,128)(2,1)}, bf16[112,128,128]{2,1,0:T(8,128)(2,1)}) custom-call(s32[224]{0:T(256)S(1)} %reshape.114.ids, bf16[192,4096]{1,0:T(8,128)(2,1)S(1)} %fusion.1.x, bf16[192,3584]{1,0:T(8,128)(2,1)S(1)} %get-tuple-element.17.dgate, bf16[192,3584]{1,0:T(8,128)(2,1)S(1)} %get-tuple-element.18.dup), custom_call_target="tpu_custom_call" | custom-call | flops 5637144576 | bytes 11665408 | tf_op jit(solution)/shard_map/gate_up_grad/pallas_call | solution.py:162
  259.3 7.1 %down_grad.3 = bf16[112,128,128]{2,1,0:T(8,128)(2,1)} custom-call(s32[224]{0:T(256)S(1)} %reshape.114.ids, bf16[192,3584]{1,0:T(8,128)(2,1)S(1)} %copy-done.8, bf16[192,4096]{1,0:T(8,128)(2,1)S(1)} %copy-done.4), custom_call_target="tpu_custom_call" | custom-call | flops 2818572288 | bytes 6619136 | tf_op jit(solution)/shard_map/down_grad/pallas_call | solution.py:162
  266.7 15.4 %normed_grad.1 = bf16[192,4096]{1,0:T(8,128)(2,1)} custom-call(s32[448]{0:T(512)S(1)} %reshape.111.ids, bf16[192,3584]{1,0:T(8,128)(2,1)S(1)} %get-tuple-element.17.dgate, bf16[192,3584]{1,0:T(8,128)(2,1)S(1)} %get-tuple-element.18.dup, bf16[224,128,128]{2,1,0:T(8,128)(2,1)S(1)} %bitcast.114, bf16[224,128,128]{2,1,0:T(8,128)(2,1)} %all-gather.4.cloned.1.call-done.w.up_w), custom_call_target="tpu_custom_call" | custom-call | flops 11274289152 | bytes 19005440 | tf_op jit(solution)/shard_map/normed_grad/pallas_call | solution.py:162
  285.2 6.1 %down_grad.2 = bf16[112,128,128]{2,1,0:T(8,128)(2,1)S(1)} custom-call(s32[224]{0:T(256)S(1)} %reshape.113.ids, bf16[192,3584]{1,0:T(8,128)(2,1)S(1)} %copy-done.9, bf16[192,4096]{1,0:T(8,128)(2,1)S(1)} %copy-done.5), custom_call_target="tpu_custom_call" | custom-call | flops 2818572288 | bytes 6619136 | tf_op jit(solution)/shard_map/down_grad/pallas_call | solution.py:162
  291.4 6.7 %gate_up_grad.2 = (bf16[112,128,128]{2,1,0:T(8,128)(2,1)S(1)}, bf16[112,128,128]{2,1,0:T(8,128)(2,1)S(1)}) custom-call(s32[224]{0:T(256)S(1)} %reshape.113.ids, bf16[192,4096]{1,0:T(8,128)(2,1)S(1)} %copy-done.3, bf16[192,3584]{1,0:T(8,128)(2,1)S(1)} %copy-done.17, bf16[192,3584]{1,0:T(8,128)(2,1)S(1)} %copy-done.19), custom_call_target="tpu_custom_call" | custom-call | flops 5637144576 | bytes 11665408 | tf_op jit(solution)/shard_map/gate_up_grad/pallas_call | solution.py:162
  301.8 13.6 %add_convert_fusion.1 = (bf16[112,128,128]{2,1,0:T(8,128)(2,1)}, bf16[112,128,128]{2,1,0:T(8,128)(2,1)}) fusion(bf16[112,128,128]{2,1,0:T(8,128)(2,1)} %collective-permute-done.7, bf16[112,128,128]{2,1,0:T(8,128)(2,1)} %copy-done.1, bf16[112,128,128]{2,1,0:T(8,128)(2,1)} %collective-permute-done, bf16[112,128,128]{2,1,0:T(8,128)(2,1)} %copy-done), kind=kLoop, calls=%fused_computation.1 | loop fusion | flops 14680064 | bytes 22020096 | tf_op jit(solution)/shard_map/convert_element_type | solution.py:241
  325.5 3.7 add_convert_fusion
  334.6 11.8 %ffn.1 = bf16[192,4096]{1,0:T(8,128)(2,1)} custom-call(s32[448]{0:T(512)S(1)} %reshape.111.ids, bf16[192,3584]{1,0:T(8,128)(2,1)S(1)} %copy-done.10, bf16[224,128,128]{2,1,0:T(8,128)(2,1)S(1)} %bitcast.112), custom_call_target="tpu_custom_call" | custom-call | flops 5637144576 | bytes 10289152 | tf_op jit(solution)/shard_map/ffn/pallas_call | solution.py:162
  352.1 8.2 %collective-permute-done.8 = bf16[28,128,128]{2,1,0:T(8,128)(2,1)S(1)} collective-permute-done((bf16[28,128,128]{2,1,0:T(8,128)(2,1)}, bf16[28,128,128]{2,1,0:T(8,128)(2,1)S(1)}, u32[]{:S(2)}, u32[]{:S(2)}) %collective-permute-start.8) | collective-permute-done | bytes 917536 | tf_op jit(solution)/shard_map/ppermute | solution.py:259
  361.8 4.3 collective-permute-start.9
  366.2 13.8 %collective-permute-done.15 = bf16[28,128,128]{2,1,0:T(8,128)(2,1)} collective-permute-done((bf16[28,128,128]{2,1,0:T(8,128)(2,1)}, bf16[28,128,128]{2,1,0:T(8,128)(2,1)}, u32[]{:S(2)}, u32[]{:S(2)}) %collective-permute-start.15) | collective-permute-done | bytes 917536 | tf_op jit(solution)/shard_map/ppermute | solution.py:259
  384.3 5.3 collective-permute-start.16
  389.7 9.9 %collective-permute-done.2 = bf16[28,128,128]{2,1,0:T(8,128)(2,1)} collective-permute-done((bf16[28,128,128]{2,1,0:T(8,128)(2,1)S(1)}, bf16[28,128,128]{2,1,0:T(8,128)(2,1)}, u32[]{:S(2)}, u32[]{:S(2)}) %collective-permute-start.2) | collective-permute-done | bytes 917536 | tf_op jit(solution)/shard_map/ppermute | solution.py:259
  399.6 4.2 fusion.16
  405.5 13.7 %collective-permute-done.9 = bf16[28,128,128]{2,1,0:T(8,128)(2,1)S(1)} collective-permute-done((bf16[28,128,128]{2,1,0:T(8,128)(2,1)S(1)}, bf16[28,128,128]{2,1,0:T(8,128)(2,1)S(1)}, u32[]{:S(2)}, u32[]{:S(2)}) %collective-permute-start.9) | collective-permute-done | bytes 917536 | tf_op jit(solution)/shard_map/ppermute | solution.py:259
  424.1 14.6 %collective-permute-done.16 = bf16[28,128,128]{2,1,0:T(8,128)(2,1)} collective-permute-done((bf16[28,128,128]{2,1,0:T(8,128)(2,1)}, bf16[28,128,128]{2,1,0:T(8,128)(2,1)}, u32[]{:S(2)}, u32[]{:S(2)}) %collective-permute-start.16) | collective-permute-done | bytes 917536 | tf_op jit(solution)/shard_map/ppermute | solution.py:259
  443.7 5.1 collective-permute-start.3
  450.0 10.4 %psum.21 = f32[192]{0:T(256)} all-reduce(f32[192]{0:T(256)S(1)} %get-tuple-element.28), channel_id=1, replica_groups=mesh['dp'=8,'tensor'=4] {'tensor'}, use_global_device_ids=true, to_apply=%region_4.5 | all-reduce | flops 192 | bytes 1536 | tf_op jit(solution)/shard_map/psum | solution.py:303
  460.4 4.6 collective-permute-start.10
  479.6 4.7 fusion.27
  487.0 63.2 %psum.22 = f32[4]{0:T(128)} all-reduce(f32[4]{0:T(128)S(1)} %pad_maximum_fusion), channel_id=1, replica_groups=mesh['dp'=8,'tensor'=4] {'dp','tensor'}, use_global_device_ids=true, to_apply=%region_9.10 | all-reduce | flops 4 | bytes 32 | tf_op jit(solution)/shard_map/psum | solution.py:315
  550.2 15.3 %psum.23 = f32[1024]{0:T(1024)} all-reduce(f32[1024]{0:T(1024)S(1)} %get-tuple-element.27), channel_id=1, replica_groups=mesh['dp'=8,'tensor'=4] {'dp'}, use_global_device_ids=true, to_apply=%region_11.12 | all-reduce | flops 1024 | bytes 8192 | tf_op jit(solution)/shard_map/psum | solution.py:314
  565.5 3.4 fusion.17
  568.9 3.4 fusion.12
  572.4 3.4 fusion.7
  (139 shorter events, 85.7 us)
Async XLA Ops:
  7.2 78.6 %all-gather.6.cloned.1.call-start = ((), (), s32[]{:S(2)}) async-start(), calls=%async_computation.3 | async-start | bytes 8257536 | tf_op jit(solution)/shard_map/all_gather | solution.py:203
  7.9 151.6 %all-gather.4.cloned.1.call-start = ((), (), s32[]{:S(2)}) async-start(), calls=%async_computation.2 | async-start | bytes 8257536 | tf_op jit(solution)/shard_map/all_gather | solution.py:204
  8.7 224.5 %all-gather.8.cloned.1.call-start = ((), (), s32[]{:S(2)}) async-start(), calls=%async_computation.4 | async-start | bytes 8257536 | tf_op jit(solution)/shard_map/all_gather | solution.py:205
  9.4 439.3 %reduce-scatter.5.cloned.1.call-start = ((), (), s32[]{:S(2)}) async-start(), calls=%async_computation.6 | async-start | bytes 1966080 | tf_op jit(solution)/shard_map/reduce_scatter | solution.py:301
  30.3 220.4 %copy-start.2 = (bf16[192,4096]{1,0:T(8,128)(2,1)}, bf16[192,4096]{1,0:T(8,128)(2,1)S(1)}, u32[]{:S(2)}) copy-start(bf16[192,4096]{1,0:T(8,128)(2,1)S(1)} %fusion.1.x) | copy-start | bytes 4718596
  100.0 133.2 %copy-start.4 = (bf16[192,4096]{1,0:T(8,128)(2,1)S(1)}, bf16[192,4096]{1,0:T(8,128)(2,1)}, u32[]{:S(2)}) copy-start(bf16[192,4096]{1,0:T(8,128)(2,1)} %gout.5) | copy-start | bytes 4718596
  236.7 29.9 %slice-start.2 = ((s8[7340032]{0:T(1024)(128)(4,1)}), s8[4194304]{0:T(1024)(128)(4,1)S(1)}, s32[]{:S(2)}) async-start(s8[7340032]{0:T(1024)(128)(4,1)} %bitcast.113), calls=%async_computation.9 | async-start | bytes 8388608
  258.8 43.0 %collective-permute-start.7 = (bf16[112,128,128]{2,1,0:T(8,128)(2,1)}, bf16[112,128,128]{2,1,0:T(8,128)(2,1)}, u32[]{:S(2)}, u32[]{:S(2)}) collective-permute-start(bf16[112,128,128]{2,1,0:T(8,128)(2,1)} %get-tuple-element.22), channel_id=1, source_target_pairs={{0,4},{4,0},{8,12},{12,8},{16,20},{20,16},{24,28},{28,24},{1,5},{5... | collective-permute-start | bytes 11010056 | tf_op jit(solution)/shard_map/ppermute | solution.py:284
  259.0 42.8 %collective-permute-start = (bf16[112,128,128]{2,1,0:T(8,128)(2,1)}, bf16[112,128,128]{2,1,0:T(8,128)(2,1)}, u32[]{:S(2)}, u32[]{:S(2)}) collective-permute-start(bf16[112,128,128]{2,1,0:T(8,128)(2,1)} %get-tuple-element.20), channel_id=1, source_target_pairs={{0,4},{4,0},{8,12},{12,8},{16,20},{20,16},{24,28},{28,24},{1,5},{5... | collective-permute-start | bytes 11010056 | tf_op jit(solution)/shard_map/ppermute | solution.py:283
  266.4 59.1 %collective-permute-start.14 = (bf16[112,128,128]{2,1,0:T(8,128)(2,1)}, bf16[112,128,128]{2,1,0:T(8,128)(2,1)}, u32[]{:S(2)}, u32[]{:S(2)}) collective-permute-start(bf16[112,128,128]{2,1,0:T(8,128)(2,1)} %down_grad.3), channel_id=1, source_target_pairs={{0,4},{4,0},{8,12},{12,8},{16,20},{20,16},{24,28},{28,24},{1,5},{5... | collective-permute-start | bytes 11010056 | tf_op jit(solution)/shard_map/ppermute | solution.py:267
  282.1 197.5 %reduce-scatter.3.cloned.1.call-start = ((), (), s32[]{:S(2)}) async-start(), calls=%async_computation.5 | async-start | bytes 1966080 | tf_op jit(solution)/shard_map/reduce_scatter | solution.py:297
  318.4 28.0 %collective-permute-start.1 = (bf16[28,128,128]{2,1,0:T(8,128)(2,1)}, bf16[28,128,128]{2,1,0:T(8,128)(2,1)}, u32[]{:S(2)}, u32[]{:S(2)}) collective-permute-start(bf16[28,128,128]{2,1,0:T(8,128)(2,1)} %get-tuple-element.42), channel_id=1, source_target_pairs={{0,8},{4,12},{1,9},{5,13},{2,10},{6,14},{3,11},{7,15}} | collective-permute-start | bytes 2752520 | tf_op jit(solution)/shard_map/ppermute | solution.py:259
  320.7 63.7 %collective-permute-start.4 = (bf16[28,128,128]{2,1,0:T(8,128)(2,1)}, bf16[28,128,128]{2,1,0:T(8,128)(2,1)}, u32[]{:S(2)}, u32[]{:S(2)}) collective-permute-start(bf16[28,128,128]{2,1,0:T(8,128)(2,1)} %get-tuple-element.43), channel_id=1, source_target_pairs={{24,16},{28,20},{25,17},{29,21},{26,18},{30,22},{27,19},{31,23}} | collective-permute-start | bytes 2752520 | tf_op jit(solution)/shard_map/ppermute | solution.py:260
  323.7 36.6 %collective-permute-start.8 = (bf16[28,128,128]{2,1,0:T(8,128)(2,1)}, bf16[28,128,128]{2,1,0:T(8,128)(2,1)S(1)}, u32[]{:S(2)}, u32[]{:S(2)}) collective-permute-start(bf16[28,128,128]{2,1,0:T(8,128)(2,1)} %get-tuple-element.38), channel_id=1, source_target_pairs={{0,8},{4,12},{1,9},{5,13},{2,10},{6,14},{3,11},{7,15}} | collective-permute-start | bytes 2752520 | tf_op jit(solution)/shard_map/ppermute | solution.py:259
  332.4 47.6 %collective-permute-start.15 = (bf16[28,128,128]{2,1,0:T(8,128)(2,1)}, bf16[28,128,128]{2,1,0:T(8,128)(2,1)}, u32[]{:S(2)}, u32[]{:S(2)}) collective-permute-start(bf16[28,128,128]{2,1,0:T(8,128)(2,1)} %get-tuple-element.34), channel_id=1, source_target_pairs={{0,8},{4,12},{1,9},{5,13},{2,10},{6,14},{3,11},{7,15}} | collective-permute-start | bytes 2752520 | tf_op jit(solution)/shard_map/ppermute | solution.py:259
  348.3 51.3 %collective-permute-start.2 = (bf16[28,128,128]{2,1,0:T(8,128)(2,1)S(1)}, bf16[28,128,128]{2,1,0:T(8,128)(2,1)}, u32[]{:S(2)}, u32[]{:S(2)}) collective-permute-start(bf16[28,128,128]{2,1,0:T(8,128)(2,1)S(1)} %fusion.15), channel_id=1, source_target_pairs={{0,8},{4,12},{8,16},{12,20},{1,9},{5,13},{9,17},{13,21},{2,10},{6,... | collective-permute-start | bytes 2752520 | tf_op jit(solution)/shard_map/ppermute | solution.py:259
  350.5 55.0 %collective-permute-start.11 = (bf16[28,128,128]{2,1,0:T(8,128)(2,1)}, bf16[28,128,128]{2,1,0:T(8,128)(2,1)}, u32[]{:S(2)}, u32[]{:S(2)}) collective-permute-start(bf16[28,128,128]{2,1,0:T(8,128)(2,1)} %get-tuple-element.39), channel_id=1, source_target_pairs={{24,16},{28,20},{25,17},{29,21},{26,18},{30,22},{27,19},{31,23}} | collective-permute-start | bytes 2752520 | tf_op jit(solution)/shard_map/ppermute | solution.py:260
  361.8 57.4 %collective-permute-start.9 = (bf16[28,128,128]{2,1,0:T(8,128)(2,1)S(1)}, bf16[28,128,128]{2,1,0:T(8,128)(2,1)S(1)}, u32[]{:S(2)}, u32[]{:S(2)}) collective-permute-start(bf16[28,128,128]{2,1,0:T(8,128)(2,1)S(1)} %fusion.10), channel_id=1, source_target_pairs={{0,8},{4,12},{8,16},{12,20},{1,9},{5,13},{9,17},{13,21},{2,10},{6,... | collective-permute-start | bytes 2752520 | tf_op jit(solution)/shard_map/ppermute | solution.py:259
  380.0 44.1 %collective-permute-start.18 = (bf16[28,128,128]{2,1,0:T(8,128)(2,1)}, bf16[28,128,128]{2,1,0:T(8,128)(2,1)}, u32[]{:S(2)}, u32[]{:S(2)}) collective-permute-start(bf16[28,128,128]{2,1,0:T(8,128)(2,1)} %get-tuple-element.35), channel_id=1, source_target_pairs={{24,16},{28,20},{25,17},{29,21},{26,18},{30,22},{27,19},{31,23}} | collective-permute-start | bytes 2752520 | tf_op jit(solution)/shard_map/ppermute | solution.py:260
  384.3 54.3 %collective-permute-start.16 = (bf16[28,128,128]{2,1,0:T(8,128)(2,1)}, bf16[28,128,128]{2,1,0:T(8,128)(2,1)}, u32[]{:S(2)}, u32[]{:S(2)}) collective-permute-start(bf16[28,128,128]{2,1,0:T(8,128)(2,1)} %fusion.5), channel_id=1, source_target_pairs={{0,8},{4,12},{8,16},{12,20},{1,9},{5,13},{9,17},{13,21},{2,10},{6,... | collective-permute-start | bytes 2752520 | tf_op jit(solution)/shard_map/ppermute | solution.py:259
  389.7 29.6 %copy-start.21 = (bf16[112,128,128]{2,1,0:T(8,128)(2,1)S(1)}, bf16[112,128,128]{2,1,0:T(8,128)(2,1)}, u32[]{:S(2)}) copy-start(bf16[112,128,128]{2,1,0:T(8,128)(2,1)} %get-tuple-element.57) | copy-start | bytes 11010052
  403.7 34.9 %copy-start.23 = (bf16[112,128,128]{2,1,0:T(8,128)(2,1)S(1)}, bf16[112,128,128]{2,1,0:T(8,128)(2,1)}, u32[]{:S(2)}) copy-start(bf16[112,128,128]{2,1,0:T(8,128)(2,1)} %copy-done.22) | copy-start | bytes 11010052
  403.7 61.2 %collective-permute-start.5 = (bf16[28,128,128]{2,1,0:T(8,128)(2,1)}, bf16[28,128,128]{2,1,0:T(8,128)(2,1)}, u32[]{:S(2)}, u32[]{:S(2)}) collective-permute-start(bf16[28,128,128]{2,1,0:T(8,128)(2,1)} %get-tuple-element.41), channel_id=1, source_target_pairs={{24,16},{28,20},{16,8},{20,12},{25,17},{29,21},{17,9},{21,13},{26,... | collective-permute-start | bytes 2752520 | tf_op jit(solution)/shard_map/ppermute | solution.py:260
  422.3 26.4 %copy-start.25 = (f32[1,192,4096]{2,1,0:T(8,128)S(1)}, f32[1,192,4096]{2,1,0:T(8,128)}, u32[]{:S(2)}) copy-start(f32[1,192,4096]{2,1,0:T(8,128)} %copy-done.24) | copy-start | bytes 9437188
  422.3 47.7 %collective-permute-start.12 = (bf16[28,128,128]{2,1,0:T(8,128)(2,1)}, bf16[28,128,128]{2,1,0:T(8,128)(2,1)}, u32[]{:S(2)}, u32[]{:S(2)}) collective-permute-start(bf16[28,128,128]{2,1,0:T(8,128)(2,1)} %get-tuple-element.37), channel_id=1, source_target_pairs={{24,16},{28,20},{16,8},{20,12},{25,17},{29,21},{17,9},{21,13},{26,... | collective-permute-start | bytes 2752520 | tf_op jit(solution)/shard_map/ppermute | solution.py:260
  442.1 32.1 %collective-permute-start.19 = (bf16[28,128,128]{2,1,0:T(8,128)(2,1)}, bf16[28,128,128]{2,1,0:T(8,128)(2,1)}, u32[]{:S(2)}, u32[]{:S(2)}) collective-permute-start(bf16[28,128,128]{2,1,0:T(8,128)(2,1)} %get-tuple-element.33), channel_id=1, source_target_pairs={{24,16},{28,20},{16,8},{20,12},{25,17},{29,21},{17,9},{21,13},{26,... | collective-permute-start | bytes 2752520 | tf_op jit(solution)/shard_map/ppermute | solution.py:260
  443.7 34.6 %collective-permute-start.3 = (bf16[28,128,128]{2,1,0:T(8,128)(2,1)}, bf16[28,128,128]{2,1,0:T(8,128)(2,1)}, u32[]{:S(2)}, u32[]{:S(2)}) collective-permute-start(bf16[28,128,128]{2,1,0:T(8,128)(2,1)} %get-tuple-element.40), channel_id=1, source_target_pairs={{0,8},{4,12},{8,16},{12,20},{16,24},{20,28},{1,9},{5,13},{9,17},{1... | collective-permute-start | bytes 2752520 | tf_op jit(solution)/shard_map/ppermute | solution.py:259
  460.4 108.5 %collective-permute-start.10 = (bf16[28,128,128]{2,1,0:T(8,128)(2,1)}, bf16[28,128,128]{2,1,0:T(8,128)(2,1)}, u32[]{:S(2)}, u32[]{:S(2)}) collective-permute-start(bf16[28,128,128]{2,1,0:T(8,128)(2,1)} %get-tuple-element.36), channel_id=1, source_target_pairs={{0,8},{4,12},{8,16},{12,20},{16,24},{20,28},{1,9},{5,13},{9,17},{1... | collective-permute-start | bytes 2752520 | tf_op jit(solution)/shard_map/ppermute | solution.py:259
  465.0 107.4 %collective-permute-start.17 = (bf16[28,128,128]{2,1,0:T(8,128)(2,1)}, bf16[28,128,128]{2,1,0:T(8,128)(2,1)}, u32[]{:S(2)}, u32[]{:S(2)}) collective-permute-start(bf16[28,128,128]{2,1,0:T(8,128)(2,1)} %get-tuple-element.32), channel_id=1, source_target_pairs={{0,8},{4,12},{8,16},{12,20},{16,24},{20,28},{1,9},{5,13},{9,17},{1... | collective-permute-start | bytes 2752520 | tf_op jit(solution)/shard_map/ppermute | solution.py:259
  470.0 95.5 %collective-permute-start.6 = (bf16[28,128,128]{2,1,0:T(8,128)(2,1)}, bf16[28,128,128]{2,1,0:T(8,128)(2,1)}, u32[]{:S(2)}, u32[]{:S(2)}) collective-permute-start(bf16[28,128,128]{2,1,0:T(8,128)(2,1)} %fusion.14), channel_id=1, source_target_pairs={{24,16},{28,20},{16,8},{20,12},{8,0},{12,4},{25,17},{29,21},{17,9}... | collective-permute-start | bytes 2752520 | tf_op jit(solution)/shard_map/ppermute | solution.py:260
  474.2 94.7 %collective-permute-start.13 = (bf16[28,128,128]{2,1,0:T(8,128)(2,1)}, bf16[28,128,128]{2,1,0:T(8,128)(2,1)}, u32[]{:S(2)}, u32[]{:S(2)}) collective-permute-start(bf16[28,128,128]{2,1,0:T(8,128)(2,1)} %fusion.9), channel_id=1, source_target_pairs={{24,16},{28,20},{16,8},{20,12},{8,0},{12,4},{25,17},{29,21},{17,9}... | collective-permute-start | bytes 2752520 | tf_op jit(solution)/shard_map/ppermute | solution.py:260
  478.3 94.1 %collective-permute-start.20 = (bf16[28,128,128]{2,1,0:T(8,128)(2,1)}, bf16[28,128,128]{2,1,0:T(8,128)(2,1)}, u32[]{:S(2)}, u32[]{:S(2)}) collective-permute-start(bf16[28,128,128]{2,1,0:T(8,128)(2,1)} %fusion.4), channel_id=1, source_target_pairs={{24,16},{28,20},{16,8},{20,12},{8,0},{12,4},{25,17},{29,21},{17,9}... | collective-permute-start | bytes 2752520 | tf_op jit(solution)/shard_map/ppermute | solution.py:260
  (27 other events, 164.6 us)
Sparse Core Ops, SparseCore 0:
  9.7 76.0 all-gather.5
  87.4 71.9 all-gather.3
  161.1 71.9 all-gather.7
  282.2 29.4 reduce-scatter.4
  346.6 30.5 reduce-scatter.2

commit v2 on v1

--- a/solution.py
+++ b/solution.py
@@ -1,5 +1,3 @@
-import functools
-
 import jax
 import jax.numpy as jnp
 from jax import lax
@@ -151,7 +149,12 @@
     for_blocks(ids, pl.program_id(0) * n, n, body)
 
 
-def call(kernel, ids, whole, blocks, outs, flops, steps, acc=None, name=None):
+def call(kernel, ids, whole, blocks, outs, flops, steps, acc=None, name=None, after=()):
+    read = 1 + len(whole) + len(blocks)
+
+    def body(*refs):
+        kernel(*refs[:read], *refs[read + len(after) :])
+
     chunked = lambda shape: pl.BlockSpec((shape[0] // steps, *shape[1:]), lambda i, ids: (i, 0, 0))
     resident = lambda shape: pl.BlockSpec(shape, lambda i, ids: (0, 0))
     order = [(a, resident(a.shape)) if a.ndim == 2 else (a, chunked(a.shape)) for a in (*whole, *blocks)]
@@ -160,19 +163,19 @@
     moved = sum(a.size * a.dtype.itemsize for a, _ in order)
     moved += sum(s.size * s.dtype.itemsize for s in out_shape)
     return pl.pallas_call(
-        kernel,
+        body,
         out_shape=out_shape,
         grid_spec=pltpu.PrefetchScalarGridSpec(
             num_scalar_prefetch=1,
             grid=(steps,),
-            in_specs=[s for _, s in order],
+            in_specs=[s for _, s in order] + [pl.BlockSpec(memory_space=pl.ANY)] * len(after),
             out_specs=out_specs,
             scratch_shapes=[pltpu.VMEM(acc, F32)] if acc else [],
         ),
         compiler_params=pltpu.CompilerParams(vmem_limit_bytes=40 * 2**20),
         cost_estimate=pl.CostEstimate(flops=4 * flops, bytes_accessed=moved, transcendentals=0),
         name=name,
-    )(ids, *[a for a, _ in order])
+    )(ids, *[a for a, _ in order], *after)
 
 
 def per_device(
@@ -230,89 +233,106 @@
     half = (chips * owned, size, size)
     siblings = [(i, i ^ 1) for i in range(dp_count)]
 
-    def down_grads(which):
+    def down_grads(which, after=()):
         return call(
             down_grad_kernel, which, [hidden, grad_out], [], [(half, BF16, True)],
-            flops // 2, chips, name="down_grad",
+            flops // 2, chips, name="down_grad", after=after,
         )
 
     def line_sum(own, received):
-        parts = own.astype(F32) + received.astype(F32)
-        parts = parts.astype(BF16).reshape(chips, owned, size, size)
+        own = own.reshape(chips, owned, size, size)
+        received = received.reshape(chips, owned, size, size)
+
+        def part(target):
+            target = jnp.clip(target, 0, chips - 1)
+            a = lax.dynamic_index_in_dim(own, target, 0, keepdims=False)
+            b = lax.dynamic_index_in_dim(received, target, 0, keepdims=False)
+            return a.astype(F32) + b.astype(F32)
+
         from_below = from_above = None
         for step in range(chips - 1):
             reach = chips - 1 - step
-
-            def piece(target, arrived):
-                p = lax.dynamic_index_in_dim(parts, jnp.clip(target, 0, chips - 1), 0, keepdims=False)
-                if arrived is None:
-                    return p
-                return (p.astype(F32) + arrived.astype(F32)).astype(BF16)
-
-            upward = piece(chip + reach, from_below)
-            downward = piece(chip - reach, from_above)
-            pairs = [(z, z + 1) for z in range(min(step + 1, chips - 1))]
+            upward, downward = part(chip + reach), part(chip - reach)
+            if step:
+                upward = upward + from_below.astype(F32)
+                downward = downward + from_above.astype(F32)
+            upward, downward = upward.astype(BF16), downward.astype(BF16)
+            pairs = [(z, z + 1) for z in range(step + 1)]
             up_pairs = [(2 * a + c, 2 * b + c) for a, b in pairs for c in (0, 1)]
             down_pairs = [
                 (2 * (chips - 1 - a) + c, 2 * (chips - 1 - b) + c) for a, b in pairs for c in (0, 1)
             ]
             from_below = lax.ppermute(upward, "dp", up_pairs)
             from_above = lax.ppermute(downward, "dp", down_pairs)
-        total = lax.dynamic_index_in_dim(parts, chip, 0, keepdims=False).astype(F32)
+            yield [upward, downward]
+        total = part(chip)
         if from_below is not None:
             total = total + from_below.astype(F32) + from_above.astype(F32)
-        return total
+        yield total
 
     (down_other,) = down_grads(other_ids)
     down_received = lax.ppermute(down_other, "dp", siblings)
-    (down_own,) = down_grads(own_ids)
-    grad_down = line_sum(down_own, down_received)
+    (down_own,) = down_grads(own_ids, [down_other])
+    down_line = list(line_sum(down_own, down_received))
+    grad_down = down_line[-1]
 
     dgate, dup = call(
         hidden_grad_kernel, ids, [grad_out], [down_all, gate_pre, up_pre],
         [(acts, BF16, False), (acts, BF16, False)], flops, CHUNKS, acc=acts, name="hidden_grad",
-    )
-
-    def gate_up_grads(which):
+        after=down_line[min(1, chips - 2)] if chips > 1 else (),
+    )
+
+    def gate_up_grads(which, after=()):
         return call(
             gate_up_grad_kernel, which, [normed, dgate, dup], [], [(half, BF16, True), (half, BF16, True)],
-            flops, chips, name="gate_up_grad",
+            flops, chips, name="gate_up_grad", after=after,
         )
 
-    gate_other, up_other = gate_up_grads(other_ids)
+    gate_other, up_other = gate_up_grads(other_ids, down_line[-2] if chips > 1 else ())
     gate_received = lax.ppermute(gate_other, "dp", siblings)
     up_received = lax.ppermute(up_other, "dp", siblings)
-    gate_own, up_own = gate_up_grads(own_ids)
-    grad_gate = line_sum(gate_own, gate_received)
-    grad_up = line_sum(up_own, up_received)
+    gate_own, up_own = gate_up_grads(own_ids, [gate_other])
+    gate_line = list(line_sum(gate_own, gate_received))
+    up_line = list(line_sum(up_own, up_received))
+    grad_gate, grad_up = gate_line[-1], up_line[-1]
+    first = (gate_line[0] + up_line[0]) if chips > 1 else []
+    last = (gate_line[-2] + up_line[-2]) if chips > 1 else []
 
     rows = (tokens, width)
-    (ffn,) = call(
-        ffn_kernel, ids, [hidden], [down_all], [(rows, BF16, False)], flops, CHUNKS, acc=rows, name="ffn"
-    )
     (normed_grad,) = call(
         normed_grad_kernel, ids, [dgate, dup], [gate_all, up_all], [(rows, BF16, False)],
-        2 * flops, CHUNKS, acc=rows, name="normed_grad",
-    )
+        2 * flops, CHUNKS, acc=rows, name="normed_grad", after=first,
+    )
+    (ffn,) = call(
+        ffn_kernel, ids, [hidden], [down_all], [(rows, BF16, False)], flops, CHUNKS, acc=rows, name="ffn",
+        after=[normed_grad],
+    )
+    grad_share = lax.psum_scatter(normed_grad, "tensor", scatter_dimension=1, tiled=True).astype(F32)
     ffn_share = lax.psum_scatter(ffn, "tensor", scatter_dimension=1, tiled=True).astype(F32)
     mixed_share = share(mixed)
     layer_out = (mixed_share + ffn_share).astype(BF16)
 
-    grad_share = lax.psum_scatter(normed_grad, "tensor", scatter_dimension=1, tiled=True).astype(F32)
     gain_share = share(gain)
-    along = lax.psum(jnp.sum(grad_share * gain_share * mixed_share, axis=-1, keepdims=True), "tensor")
-    grad_mixed = (
-        share(grad_out).astype(F32)
-        + scale_inv * gain_share * grad_share
-        - mixed_share * (scale_inv * scale_inv * scale_inv / width) * along
-    )
+    cubed = scale_inv * scale_inv * scale_inv / width
+    direct = share(grad_out).astype(F32) + scale_inv * gain_share * grad_share
+    along_part = jnp.sum(grad_share * gain_share * mixed_share, axis=-1)
     gain_part = jnp.sum(grad_share * mixed_share * scale_inv, axis=0)
     depth_list = []
     for slot in range(depth_index.shape[0]):
-        earlier = lax.dynamic_index_in_dim(history, depth_index[slot], 0, keepdims=False)
-        depth_list.append(jnp.sum(grad_mixed * share(earlier).astype(F32)))
-    gain_sum = lax.psum(gain_part, "dp")
-    depth_sum = lax.psum(jnp.stack(depth_list), ("dp", "tensor"))
+        earlier = lax.dynamic_index_in_dim(history, depth_index[slot], 0, keepdims=False).astype(F32)
+        second = jnp.sum(mixed * earlier, axis=-1) * cubed[:, 0]
+        depth_list.append(jnp.sum(direct * share(earlier)) - jnp.sum(along_part * second))
+    slots = depth_index.shape[0]
+    sums = jnp.zeros((slots + width + dp_count * tokens,), F32)
+    sums = lax.dynamic_update_slice_in_dim(sums, jnp.stack(depth_list), 0, 0)
+    sums = lax.dynamic_update_slice_in_dim(sums, gain_part, slots + share_start, 0)
+    sums = lax.dynamic_update_slice_in_dim(sums, along_part, slots + width + dp * tokens, 0)
+    sums = lax.optimization_barrier((sums, *last))[0]
+    sums = lax.psum(sums, ("dp", "tensor"))
+    depth_sum = sums[:slots]
+    gain_sum = lax.dynamic_slice_in_dim(sums, slots + share_start, share_width, 0)
+    along = lax.dynamic_slice_in_dim(sums, slots + width + dp * tokens, tokens, 0)[:, None]
+    grad_mixed = direct - mixed_share * cubed * along
     return (layer_out, grad_mixed, grad_gate, grad_up, grad_down, depth_sum, gain_sum)
 
 

time: 584 us -> 522 us (0.89)
  waiting for transfers between devices: 234 us -> 161 us
  starting transfers between devices: 44.8 us -> 98 us
  blocking collectives: 88.9 us -> 42.3 us
  local copies, waits for them, and re-layouts: 32.8 us -> 26.1 us
  other arithmetic: 68.5 us -> 75.1 us
    all_gather x1, waiting for transfers between devices: 56.9 us -> 1.26 us  [per_device(): down_all = lax.all_gather(down_blocks, 'dp', axis=0, tiled=True)]
    ppermute x9, starting transfers between devices: 30.1 us -> 85.2 us  [line_sum(): from_below = lax.ppermute(upward, 'dp', up_pairs)]
    psum x3 -> x1, blocking collectives: 88.9 us -> 42.3 us  [per_device(): sums = lax.psum(sums, ('dp', 'tensor'))]
    ppermute x9, waiting for transfers between devices: 60.2 us -> 41.9 us  [line_sum(): from_below = lax.ppermute(upward, 'dp', up_pairs)]
    squeeze x3 -> x0, local copies, waits for them, and re-layouts: 5.92 us -> none  [piece(): lax.dynamic_index_in_dim(parts, jnp.clip(target, 0, chips - 1), 0, keepdi...]
    convert_element_type x11 -> x12, other arithmetic: 42.3 us -> 47.9 us  [the longest x11 39.5 us: line_sum(): upward, downward = (upward.astype(BF16), downward.astype(BF16))]
    unnamed x69 -> x63, local copies, waits for them, and re-layouts: 23.7 us -> 22.7 us
  transfers between devices with their start and end apart: 26 -> 26, of which waited for: 8 -> 5; matrix products, arithmetic and copies ran while one was open for 13% -> 13% of each run, Pallas kernels for 12% -> 13%
where the time goes in v2:
time: 522 us; the launch traced here: 520 us
  waiting for transfers between devices  161 us (31%)
  starting transfers between devices  98 us (19%)
  Pallas kernels  90.1 us (17%)
  other arithmetic  75.1 us (14%)
  blocking collectives  42.3 us (8%)
  between operations  27.3 us (5%)
  local copies, waits for them, and re-layouts  26.1 us (5%)
    pallas_call x9, Pallas kernels, call(): pl.pallas_call(body, out_shape=out_shape, grid_spec=pltpu.PrefetchScalarG...  90.1 us
    ppermute x9, starting transfers between devices, line_sum(): from_below = lax.ppermute(upward, 'dp', up_pairs)  85.2 us
    all_gather x1, waiting for transfers between devices, per_device(): up_all = lax.all_gather(up_blocks, 'dp', axis=0, tiled=True)  59.6 us
    all_gather x1, waiting for transfers between devices, per_device(): gate_all = lax.all_gather(gate_blocks, 'dp', axis=0, tiled=True)  56.3 us
    psum x1, blocking collectives, per_device(): sums = lax.psum(sums, ('dp', 'tensor'))  42.3 us
    ppermute x9, waiting for transfers between devices, line_sum(): from_below = lax.ppermute(upward, 'dp', up_pairs)  41.9 us
    convert_element_type x11, other arithmetic, line_sum(): upward, downward = (upward.astype(BF16), downward.astype(BF16))  39.5 us
    unnamed x63, local copies, waits for them, and re-layouts  22.7 us
  transfers between devices with their start and end apart: 26, of which 5 were waited for; matrix products, arithmetic and copies ran while one was open for 13% of the time, Pallas kernels for 13%

profile of v2, /device:TPU:0, one launch (start us, length us, event | category | flops | bytes accessed | tf_op | source)
XLA Modules:
  0.0 520.2 jit_solution(864526211200093790)
XLA Ops:
  19.2 8.1 %fusion.6 = (f32[192]{0:T(256)S(1)}, f32[192]{0:T(256)S(1)}, f32[192]{0:T(256)S(1)}, f32[192]{0:T(256)S(1)}, f32[192]{0:T(256)S(1)}, /*index=5*/f32[192,4096]{1,0:T(8,128)S(1)}) fusion(bf16[4,192,4096]{2,1,0:T(8,128)(2,1)} %param.9, s32[]{:T(128)S(6)} %select_n.95, s32[]{:T(128)S(6)} %select_n.98, s32[]{:T(128)S(6)} %select_n.97, s32[]{:T(128)S(6)} %select_n.96, ...), kind=kLoop, calls=%fused_computation.14 | loop fusion | flops 16514112 | bytes 9441056 | tf_op jit(solution)/shard_map/reduce_sum | solution.py:323
  29.5 56.3 %all-gather.6.cloned.1.call-done.refs_2_.refs_3_ = bf16[224,128,128]{2,1,0:T(8,128)(2,1)} async-done(((bf16[28,128,128]{2,1,0:T(8,128)(2,1)}), bf16[224,128,128]{2,1,0:T(8,128)(2,1)}) %all-gather.6.cloned.1.call-update) | async-done | bytes 7340048 | tf_op jit(solution)/shard_map/all_gather | solution.py:206
  88.9 9.5 %gate.1.refs_3_ = f32[192,3584]{1,0:T(8,128)S(1)} custom-call(s32[448]{0:T(512)S(1)} %reshape.142.refs_0_, bf16[192,4096]{1,0:T(8,128)(2,1)S(1)} %multiply_convert_fusion.refs_1_, bf16[224,128,128]{2,1,0:T(8,128)(2,1)S(1)} %copy-done.12), custom_call_target="tpu_custom_call" | custom-call | flops 5637144576 | bytes 11665408 | tf_op jit(solution)/shard_map/gate/pallas_call | solution.py:165
  99.9 59.6 %all-gather.4.cloned.1.call-done.refs_2_.refs_4_ = bf16[224,128,128]{2,1,0:T(8,128)(2,1)} async-done(((bf16[28,128,128]{2,1,0:T(8,128)(2,1)}), bf16[224,128,128]{2,1,0:T(8,128)(2,1)}) %all-gather.4.cloned.1.call-update) | async-done | bytes 7340048 | tf_op jit(solution)/shard_map/all_gather | solution.py:207
  161.3 12.3 %up_hidden.1 = (f32[192,3584]{1,0:T(8,128)S(1)}, bf16[192,3584]{1,0:T(8,128)(2,1)S(1)}) custom-call(s32[448]{0:T(512)S(1)} %reshape.142.refs_0_, bf16[192,4096]{1,0:T(8,128)(2,1)S(1)} %multiply_convert_fusion.refs_1_, bf16[224,128,128]{2,1,0:T(8,128)(2,1)} %all-gather.4.cloned.1.call-done.refs_2_.refs_4_, f32[192,3584]{1,0:T(8,128)S(1)} %copy-done.18), custom_call_target="tpu_custom_call" | custom-call | flops 5637144576 | bytes 15794176 | tf_op jit(solution)/shard_map/up_hidden/pallas_call | solution.py:165
  175.1 7.1 %down_grad.2.refs_3_ = bf16[112,128,128]{2,1,0:T(8,128)(2,1)} custom-call(s32[224]{0:T(256)S(1)} %reshape.145.refs_0_, bf16[192,3584]{1,0:T(8,128)(2,1)S(1)} %get-tuple-element.16.refs_1_, bf16[192,4096]{1,0:T(8,128)(2,1)S(1)} %copy-done.8), custom_call_target="tpu_custom_call" | custom-call | flops 2818572288 | bytes 6619136 | tf_op jit(solution)/shard_map/down_grad/pallas_call | solution.py:165
  184.2 6.1 %down_grad.3 = bf16[112,128,128]{2,1,0:T(8,128)(2,1)S(1)} custom-call(s32[224]{0:T(256)S(1)} %reshape.144.refs_0_, bf16[192,3584]{1,0:T(8,128)(2,1)S(1)} %copy-done.15, bf16[192,4096]{1,0:T(8,128)(2,1)S(1)} %copy-done.8, bf16[112,128,128]{2,1,0:T(8,128)(2,1)} %down_grad.2.refs_3_), custom_call_target="tpu_custom_call" | custom-call | flops 2818572288 | bytes 6619136 | tf_op jit(solution)/shard_map/down_grad/pallas_call | solution.py:165
  190.3 4.5 fusion.23
  197.7 38.8 %collective-permute-done.1 = bf16[28,128,128]{2,1,0:T(8,128)(2,1)S(1)} collective-permute-done((bf16[28,128,128]{2,1,0:T(8,128)(2,1)}, bf16[28,128,128]{2,1,0:T(8,128)(2,1)S(1)}, u32[]{:S(2)}, u32[]{:S(2)}) %collective-permute-start.1) | collective-permute-done | bytes 917536 | tf_op jit(solution)/shard_map/ppermute | solution.py:265
  237.5 3.5 fusion.20
  241.0 5.3 %collective-permute-start.3 = (bf16[28,128,128]{2,1,0:T(8,128)(2,1)S(1)}, bf16[28,128,128]{2,1,0:T(8,128)(2,1)}, u32[]{:S(2)}, u32[]{:S(2)}) collective-permute-start(bf16[28,128,128]{2,1,0:T(8,128)(2,1)S(1)} %get-tuple-element.54.refs_5_), channel_id=1, source_target_pairs={{0,8},{4,12},{8,16},{12,20},{1,9},{5,13},{9,17},{13,21},{2,10},{6,... | collective-permute-start | bytes 2752520 | tf_op jit(solution)/shard_map/ppermute | solution.py:265
  254.1 14.0 %hidden_grad.1 = (bf16[192,3584]{1,0:T(8,128)(2,1)S(1)}, bf16[192,3584]{1,0:T(8,128)(2,1)S(1)}) custom-call(s32[448]{0:T(512)S(1)} %reshape.142.refs_0_, bf16[192,4096]{1,0:T(8,128)(2,1)S(1)} %copy-done.9, bf16[224,128,128]{2,1,0:T(8,128)(2,1)} %all-gather.8.cloned.1.call-done.refs_2_, f32[192,3584]{1,0:T(8,128)S(1)} %copy-done.19, ...), custom_call_target="tpu_custom_call" | custom-call | flops 5637144576 | bytes 17170432 | tf_op jit(solution)/shard_map/hidden_grad/pallas_call | solution.py:165
  271.2 6.7 %gate_up_grad.2 = (bf16[112,128,128]{2,1,0:T(8,128)(2,1)S(1)}, bf16[112,128,128]{2,1,0:T(8,128)(2,1)S(1)}) custom-call(s32[224]{0:T(256)S(1)} %reshape.145.refs_0_, bf16[192,4096]{1,0:T(8,128)(2,1)S(1)} %multiply_convert_fusion.refs_1_, bf16[192,3584]{1,0:T(8,128)(2,1)S(1)} %get-tuple-element.18.refs_2_.refs_1_, ...), custom_call_target="tpu_custom_call" | custom-call | flops 5637144576 | bytes 11665408 | tf_op jit(solution)/shard_map/gate_up_grad/pallas_call | solution.py:165
  279.8 6.7 %gate_up_grad.3 = (bf16[112,128,128]{2,1,0:T(8,128)(2,1)S(1)}, bf16[112,128,128]{2,1,0:T(8,128)(2,1)S(1)}) custom-call(s32[224]{0:T(256)S(1)} %reshape.144.refs_0_, bf16[192,4096]{1,0:T(8,128)(2,1)S(1)} %multiply_convert_fusion.refs_1_, bf16[192,3584]{1,0:T(8,128)(2,1)S(1)} %get-tuple-element.18.refs_2_.refs_1_, ...), custom_call_target="tpu_custom_call" | custom-call | flops 5637144576 | bytes 11665408 | tf_op jit(solution)/shard_map/gate_up_grad/pallas_call | solution.py:165
  286.5 3.8 fusion.27
  293.2 15.7 %normed_grad.1.refs_3_ = bf16[192,4096]{1,0:T(8,128)(2,1)} custom-call(s32[448]{0:T(512)S(1)} %reshape.142.refs_0_, bf16[192,3584]{1,0:T(8,128)(2,1)S(1)} %get-tuple-element.18.refs_2_.refs_1_, bf16[192,3584]{1,0:T(8,128)(2,1)S(1)} %get-tuple-element.19.refs_3_.refs_2_, bf16[224,128,128]{2,1,0:T(8,128)(2,1)} %all-gather.6.cloned.1.call-done.refs_2_.refs_3_, ...), custom_call_target="tpu_custom_call" | custom-call | flops 11274289152 | bytes 19005440 | tf_op jit(solution)/shard_map/normed_grad/pallas_call | solution.py:165
  311.4 6.9 %collective-permute-start.11 = (bf16[28,128,128]{2,1,0:T(8,128)(2,1)}, bf16[28,128,128]{2,1,0:T(8,128)(2,1)}, u32[]{:S(2)}, u32[]{:S(2)}) collective-permute-start(bf16[28,128,128]{2,1,0:T(8,128)(2,1)} %copy-done.5), channel_id=1, source_target_pairs={{0,8},{4,12},{1,9},{5,13},{2,10},{6,14},{3,11},{7,15}} | collective-permute-start | bytes 2752520 | tf_op jit(solution)/shard_map/ppermute | solution.py:265
  333.0 11.9 %ffn.1 = bf16[192,4096]{1,0:T(8,128)(2,1)} custom-call(s32[448]{0:T(512)S(1)} %reshape.142.refs_0_, bf16[192,3584]{1,0:T(8,128)(2,1)S(1)} %copy-done.16, bf16[224,128,128]{2,1,0:T(8,128)(2,1)S(1)} %copy-done.11, bf16[192,4096]{1,0:T(8,128)(2,1)} %normed_grad.1.refs_3_), custom_call_target="tpu_custom_call" | custom-call | flops 5637144576 | bytes 10289152 | tf_op jit(solution)/shard_map/ffn/pallas_call | solution.py:165
  348.7 5.1 fusion.11
  353.9 39.5 %collective-permute-start.12 = (bf16[28,128,128]{2,1,0:T(8,128)(2,1)}, bf16[28,128,128]{2,1,0:T(8,128)(2,1)}, u32[]{:S(2)}, u32[]{:S(2)}) collective-permute-start(bf16[28,128,128]{2,1,0:T(8,128)(2,1)} %get-tuple-element.44), channel_id=1, source_target_pairs={{0,8},{4,12},{8,16},{12,20},{1,9},{5,13},{9,17},{13,21},{2,10},{6,... | collective-permute-start | bytes 2752520 | tf_op jit(solution)/shard_map/ppermute | solution.py:265
  393.4 4.5 fusion.15
  397.9 5.1 collective-permute-start.8
  403.0 8.4 %dynamic-slice_convert_fusion.2 = (f32[1,192,4096]{2,1,0:T(8,128)}, f32[1,192,4096]{2,1,0:T(8,128)}, f32[1,192,4096]{2,1,0:T(8,128)}, f32[1,192,4096]{2,1,0:T(8,128)}) fusion(bf16[4,192,4096]{2,1,0:T(8,128)(2,1)} %param.9, s32[]{:T(128)S(6)} %select_n.96, s32[]{:T(128)S(6)} %select_n.95, s32[]{:T(128)S(6)} %select_n.98, s32[]{:T(128)S(6)} %select_n.97), kind=kLoop, calls=%fused_computation.55 | loop fusion | flops 3145728 | bytes 18874384 | tf_op jit(solution)/shard_map/convert_element_type | solution.py:216
  411.4 3.9 fusion.7
  417.9 3.2 fusion.13
  421.1 9.0 %collective-permute-start.17 = (bf16[28,128,128]{2,1,0:T(8,128)(2,1)}, bf16[28,128,128]{2,1,0:T(8,128)(2,1)}, u32[]{:S(2)}, u32[]{:S(2)}) collective-permute-start(bf16[28,128,128]{2,1,0:T(8,128)(2,1)} %fusion.13), channel_id=1, source_target_pairs={{0,8},{4,12},{8,16},{12,20},{16,24},{20,28},{1,9},{5,13},{9,17},{1... | collective-permute-start | bytes 2752520 | tf_op jit(solution)/shard_map/ppermute | solution.py:265
  433.2 3.2 fusion.17
  436.5 13.3 %collective-permute-start.15 = (bf16[28,128,128]{2,1,0:T(8,128)(2,1)}, bf16[28,128,128]{2,1,0:T(8,128)(2,1)}, u32[]{:S(2)}, u32[]{:S(2)}) collective-permute-start(bf16[28,128,128]{2,1,0:T(8,128)(2,1)} %fusion.17), channel_id=1, source_target_pairs={{0,8},{4,12},{8,16},{12,20},{16,24},{20,28},{1,9},{5,13},{9,17},{1... | collective-permute-start | bytes 2752520 | tf_op jit(solution)/shard_map/ppermute | solution.py:265
  449.7 3.7 fusion.36
  459.8 42.3 %psum.7 = f32[5636]{0:T(1024)S(1)} all-reduce(f32[5636]{0:T(1024)S(1)} %dynamic_update_slice.11), channel_id=1, replica_groups=mesh['dp'=8,'tensor'=4] {'dp','tensor'}, use_global_device_ids=true, to_apply=%region_17.18 | all-reduce | flops 5636 | bytes 45088 | tf_op jit(solution)/shard_map/psum | solution.py:331
  506.0 3.8 fusion.8
  509.8 3.8 fusion.9
  (133 shorter events, 67.1 us)
Async XLA Ops:
  7.2 11.4 %copy-start.29 = (f32[4]{0:T(128)S(1)}, f32[4]{0:T(128)}, u32[]{:S(2)}) copy-start(f32[4]{0:T(128)} %param.10) | copy-start | bytes 52
  7.2 78.6 %all-gather.6.cloned.1.call-start = ((), (), s32[]{:S(2)}) async-start(), calls=%async_computation.3 | async-start | bytes 8257536 | tf_op jit(solution)/shard_map/all_gather | solution.py:206
  7.9 151.5 %all-gather.4.cloned.1.call-start = ((), (), s32[]{:S(2)}) async-start(), calls=%async_computation.2 | async-start | bytes 8257536 | tf_op jit(solution)/shard_map/all_gather | solution.py:207
  8.7 240.5 %all-gather.8.cloned.1.call-start = ((), (), s32[]{:S(2)}) async-start(), calls=%async_computation.4 | async-start | bytes 8257536 | tf_op jit(solution)/shard_map/all_gather | solution.py:208
  9.4 440.3 %reduce-scatter.5.cloned.1.call-start = ((), (), s32[]{:S(2)}) async-start(), calls=%async_computation.6 | async-start | bytes 1966080 | tf_op jit(solution)/shard_map/reduce_scatter | solution.py:310
  99.9 75.2 %copy-start.8 = (bf16[192,4096]{1,0:T(8,128)(2,1)S(1)}, bf16[192,4096]{1,0:T(8,128)(2,1)}, u32[]{:S(2)}) copy-start(bf16[192,4096]{1,0:T(8,128)(2,1)} %refs_1_.1) | copy-start | bytes 4718596
  182.3 8.0 %collective-permute-start = (bf16[112,128,128]{2,1,0:T(8,128)(2,1)}, bf16[112,128,128]{2,1,0:T(8,128)(2,1)}, u32[]{:S(2)}, u32[]{:S(2)}) collective-permute-start(bf16[112,128,128]{2,1,0:T(8,128)(2,1)} %down_grad.2.refs_3_), channel_id=1, source_target_pairs={{0,4},{4,0},{8,12},{12,8},{16,20},{20,16},{24,28},{28,24},{1,5},{5... | collective-permute-start | bytes 11010056 | tf_op jit(solution)/shard_map/ppermute | solution.py:274
  194.8 41.8 %collective-permute-start.1 = (bf16[28,128,128]{2,1,0:T(8,128)(2,1)}, bf16[28,128,128]{2,1,0:T(8,128)(2,1)S(1)}, u32[]{:S(2)}, u32[]{:S(2)}) collective-permute-start(bf16[28,128,128]{2,1,0:T(8,128)(2,1)} %get-tuple-element.56), channel_id=1, source_target_pairs={{0,8},{4,12},{1,9},{5,13},{2,10},{6,14},{3,11},{7,15}} | collective-permute-start | bytes 2752520 | tf_op jit(solution)/shard_map/ppermute | solution.py:265
  196.1 41.4 %collective-permute-start.2 = (bf16[28,128,128]{2,1,0:T(8,128)(2,1)S(1)}, bf16[28,128,128]{2,1,0:T(8,128)(2,1)}, u32[]{:S(2)}, u32[]{:S(2)}) collective-permute-start(bf16[28,128,128]{2,1,0:T(8,128)(2,1)S(1)} %get-tuple-element.55), channel_id=1, source_target_pairs={{24,16},{28,20},{25,17},{29,21},{26,18},{30,22},{27,19},{31,23}} | collective-permute-start | bytes 2752520 | tf_op jit(solution)/shard_map/ppermute | solution.py:266
  241.0 27.1 %collective-permute-start.3 = (bf16[28,128,128]{2,1,0:T(8,128)(2,1)S(1)}, bf16[28,128,128]{2,1,0:T(8,128)(2,1)}, u32[]{:S(2)}, u32[]{:S(2)}) collective-permute-start(bf16[28,128,128]{2,1,0:T(8,128)(2,1)S(1)} %get-tuple-element.54.refs_5_), channel_id=1, source_target_pairs={{0,8},{4,12},{8,16},{12,20},{1,9},{5,13},{9,17},{13,21},{2,10},{6,... | collective-permute-start | bytes 2752520 | tf_op jit(solution)/shard_map/ppermute | solution.py:265
  246.3 21.9 %collective-permute-start.4 = (bf16[28,128,128]{2,1,0:T(8,128)(2,1)S(1)}, bf16[28,128,128]{2,1,0:T(8,128)(2,1)}, u32[]{:S(2)}, u32[]{:S(2)}) collective-permute-start(bf16[28,128,128]{2,1,0:T(8,128)(2,1)S(1)} %get-tuple-element.53.refs_6_), channel_id=1, source_target_pairs={{24,16},{28,20},{16,8},{20,12},{25,17},{29,21},{17,9},{21,13},{26,... | collective-permute-start | bytes 2752520 | tf_op jit(solution)/shard_map/ppermute | solution.py:266
  254.1 14.0 %copy-start.4 = (bf16[112,128,128]{2,1,0:T(8,128)(2,1)S(1)}, bf16[112,128,128]{2,1,0:T(8,128)(2,1)}, u32[]{:S(2)}) copy-start(bf16[112,128,128]{2,1,0:T(8,128)(2,1)} %copy-done.3) | copy-start | bytes 11010052
  277.9 8.6 %collective-permute-start.6 = (bf16[112,128,128]{2,1,0:T(8,128)(2,1)S(1)}, bf16[112,128,128]{2,1,0:T(8,128)(2,1)}, u32[]{:S(2)}, u32[]{:S(2)}) collective-permute-start(bf16[112,128,128]{2,1,0:T(8,128)(2,1)S(1)} %get-tuple-element.23), channel_id=1, source_target_pairs={{0,4},{4,0},{8,12},{12,8},{16,20},{20,16},{24,28},{28,24},{1,5},{5... | collective-permute-start | bytes 11010056 | tf_op jit(solution)/shard_map/ppermute | solution.py:293
  278.0 12.3 %collective-permute-start.5 = (bf16[112,128,128]{2,1,0:T(8,128)(2,1)S(1)}, bf16[112,128,128]{2,1,0:T(8,128)(2,1)}, u32[]{:S(2)}, u32[]{:S(2)}) collective-permute-start(bf16[112,128,128]{2,1,0:T(8,128)(2,1)S(1)} %get-tuple-element.20.refs_4_), channel_id=1, source_target_pairs={{0,4},{4,0},{8,12},{12,8},{16,20},{20,16},{24,28},{28,24},{1,5},{5... | collective-permute-start | bytes 11010056 | tf_op jit(solution)/shard_map/ppermute | solution.py:292
  309.9 193.5 %reduce-scatter.3.cloned.1.call-start = ((), (), s32[]{:S(2)}) async-start(), calls=%async_computation.5 | async-start | bytes 1966080 | tf_op jit(solution)/shard_map/reduce_scatter | solution.py:311
  310.0 10.6 %collective-permute-start.13 = (bf16[28,128,128]{2,1,0:T(8,128)(2,1)}, bf16[28,128,128]{2,1,0:T(8,128)(2,1)S(1)}, u32[]{:S(2)}, u32[]{:S(2)}) collective-permute-start(bf16[28,128,128]{2,1,0:T(8,128)(2,1)} %copy-done.7), channel_id=1, source_target_pairs={{24,16},{28,20},{25,17},{29,21},{26,18},{30,22},{27,19},{31,23}} | collective-permute-start | bytes 2752520 | tf_op jit(solution)/shard_map/ppermute | solution.py:266
  310.7 14.6 %collective-permute-start.9 = (bf16[28,128,128]{2,1,0:T(8,128)(2,1)}, bf16[28,128,128]{2,1,0:T(8,128)(2,1)S(1)}, u32[]{:S(2)}, u32[]{:S(2)}) collective-permute-start(bf16[28,128,128]{2,1,0:T(8,128)(2,1)} %copy-done.6), channel_id=1, source_target_pairs={{24,16},{28,20},{25,17},{29,21},{26,18},{30,22},{27,19},{31,23}} | collective-permute-start | bytes 2752520 | tf_op jit(solution)/shard_map/ppermute | solution.py:266
  311.4 36.0 %collective-permute-start.11 = (bf16[28,128,128]{2,1,0:T(8,128)(2,1)}, bf16[28,128,128]{2,1,0:T(8,128)(2,1)}, u32[]{:S(2)}, u32[]{:S(2)}) collective-permute-start(bf16[28,128,128]{2,1,0:T(8,128)(2,1)} %copy-done.5), channel_id=1, source_target_pairs={{0,8},{4,12},{1,9},{5,13},{2,10},{6,14},{3,11},{7,15}} | collective-permute-start | bytes 2752520 | tf_op jit(solution)/shard_map/ppermute | solution.py:265
  318.3 75.1 %collective-permute-start.7 = (bf16[28,128,128]{2,1,0:T(8,128)(2,1)S(1)}, bf16[28,128,128]{2,1,0:T(8,128)(2,1)}, u32[]{:S(2)}, u32[]{:S(2)}) collective-permute-start(bf16[28,128,128]{2,1,0:T(8,128)(2,1)S(1)} %get-tuple-element.50.refs_5_), channel_id=1, source_target_pairs={{0,8},{4,12},{1,9},{5,13},{2,10},{6,14},{3,11},{7,15}} | collective-permute-start | bytes 2752520 | tf_op jit(solution)/shard_map/ppermute | solution.py:265
  323.5 25.2 %collective-permute-start.14 = (bf16[28,128,128]{2,1,0:T(8,128)(2,1)}, bf16[28,128,128]{2,1,0:T(8,128)(2,1)}, u32[]{:S(2)}, u32[]{:S(2)}) collective-permute-start(bf16[28,128,128]{2,1,0:T(8,128)(2,1)} %fusion.10), channel_id=1, source_target_pairs={{24,16},{28,20},{16,8},{20,12},{25,17},{29,21},{17,9},{21,13},{26,... | collective-permute-start | bytes 2752520 | tf_op jit(solution)/shard_map/ppermute | solution.py:266
  328.2 65.2 %collective-permute-start.10 = (bf16[28,128,128]{2,1,0:T(8,128)(2,1)}, bf16[28,128,128]{2,1,0:T(8,128)(2,1)}, u32[]{:S(2)}, u32[]{:S(2)}) collective-permute-start(bf16[28,128,128]{2,1,0:T(8,128)(2,1)} %fusion.14), channel_id=1, source_target_pairs={{24,16},{28,20},{16,8},{20,12},{25,17},{29,21},{17,9},{21,13},{26,... | collective-permute-start | bytes 2752520 | tf_op jit(solution)/shard_map/ppermute | solution.py:266
  344.9 48.5 %copy-start.1 = (bf16[112,128,128]{2,1,0:T(8,128)(2,1)S(1)}, bf16[112,128,128]{2,1,0:T(8,128)(2,1)}, u32[]{:S(2)}) copy-start(bf16[112,128,128]{2,1,0:T(8,128)(2,1)} %copy-done) | copy-start | bytes 11010052
  344.9 66.5 %collective-permute-start.19 = (bf16[28,128,128]{2,1,0:T(8,128)(2,1)S(1)}, bf16[28,128,128]{2,1,0:T(8,128)(2,1)}, u32[]{:S(2)}, u32[]{:S(2)}) collective-permute-start(bf16[28,128,128]{2,1,0:T(8,128)(2,1)S(1)} %get-tuple-element.52.refs_4_), channel_id=1, source_target_pairs={{0,8},{4,12},{8,16},{12,20},{16,24},{20,28},{1,9},{5,13},{9,17},{1... | collective-permute-start | bytes 2752520 | tf_op jit(solution)/shard_map/ppermute | solution.py:265
  347.4 63.9 %collective-permute-start.20 = (bf16[28,128,128]{2,1,0:T(8,128)(2,1)S(1)}, bf16[28,128,128]{2,1,0:T(8,128)(2,1)}, u32[]{:S(2)}, u32[]{:S(2)}) collective-permute-start(bf16[28,128,128]{2,1,0:T(8,128)(2,1)S(1)} %get-tuple-element.51.refs_5_), channel_id=1, source_target_pairs={{24,16},{28,20},{16,8},{20,12},{8,0},{12,4},{25,17},{29,21},{17,9}... | collective-permute-start | bytes 2752520 | tf_op jit(solution)/shard_map/ppermute | solution.py:266
  353.9 64.0 %collective-permute-start.12 = (bf16[28,128,128]{2,1,0:T(8,128)(2,1)}, bf16[28,128,128]{2,1,0:T(8,128)(2,1)}, u32[]{:S(2)}, u32[]{:S(2)}) collective-permute-start(bf16[28,128,128]{2,1,0:T(8,128)(2,1)} %get-tuple-element.44), channel_id=1, source_target_pairs={{0,8},{4,12},{8,16},{12,20},{1,9},{5,13},{9,17},{13,21},{2,10},{6,... | collective-permute-start | bytes 2752520 | tf_op jit(solution)/shard_map/ppermute | solution.py:265
  397.9 35.3 %collective-permute-start.8 = (bf16[28,128,128]{2,1,0:T(8,128)(2,1)}, bf16[28,128,128]{2,1,0:T(8,128)(2,1)}, u32[]{:S(2)}, u32[]{:S(2)}) collective-permute-start(bf16[28,128,128]{2,1,0:T(8,128)(2,1)} %get-tuple-element.46), channel_id=1, source_target_pairs={{0,8},{4,12},{8,16},{12,20},{1,9},{5,13},{9,17},{13,21},{2,10},{6,... | collective-permute-start | bytes 2752520 | tf_op jit(solution)/shard_map/ppermute | solution.py:265
  415.3 90.6 %collective-permute-start.18 = (bf16[28,128,128]{2,1,0:T(8,128)(2,1)S(1)}, bf16[28,128,128]{2,1,0:T(8,128)(2,1)}, u32[]{:S(2)}, u32[]{:S(2)}) collective-permute-start(bf16[28,128,128]{2,1,0:T(8,128)(2,1)S(1)} %copy-done.24), channel_id=1, source_target_pairs={{24,16},{28,20},{16,8},{20,12},{8,0},{12,4},{25,17},{29,21},{17,9}... | collective-permute-start | bytes 2752520 | tf_op jit(solution)/shard_map/ppermute | solution.py:266
  416.6 93.2 %collective-permute-start.16 = (bf16[28,128,128]{2,1,0:T(8,128)(2,1)}, bf16[28,128,128]{2,1,0:T(8,128)(2,1)}, u32[]{:S(2)}, u32[]{:S(2)}) collective-permute-start(bf16[28,128,128]{2,1,0:T(8,128)(2,1)} %get-tuple-element.45), channel_id=1, source_target_pairs={{24,16},{28,20},{16,8},{20,12},{8,0},{12,4},{25,17},{29,21},{17,9}... | collective-permute-start | bytes 2752520 | tf_op jit(solution)/shard_map/ppermute | solution.py:266
  421.1 28.6 %copy-start.10 = (bf16[192,4096]{1,0:T(8,128)(2,1)S(1)}, bf16[192,4096]{1,0:T(8,128)(2,1)}, u32[]{:S(2)}) copy-start(bf16[192,4096]{1,0:T(8,128)(2,1)} %refs_1_.1) | copy-start | bytes 4718596
  421.1 84.8 %collective-permute-start.17 = (bf16[28,128,128]{2,1,0:T(8,128)(2,1)}, bf16[28,128,128]{2,1,0:T(8,128)(2,1)}, u32[]{:S(2)}, u32[]{:S(2)}) collective-permute-start(bf16[28,128,128]{2,1,0:T(8,128)(2,1)} %fusion.13), channel_id=1, source_target_pairs={{0,8},{4,12},{8,16},{12,20},{16,24},{20,28},{1,9},{5,13},{9,17},{1... | collective-permute-start | bytes 2752520 | tf_op jit(solution)/shard_map/ppermute | solution.py:265
  436.5 73.4 %collective-permute-start.15 = (bf16[28,128,128]{2,1,0:T(8,128)(2,1)}, bf16[28,128,128]{2,1,0:T(8,128)(2,1)}, u32[]{:S(2)}, u32[]{:S(2)}) collective-permute-start(bf16[28,128,128]{2,1,0:T(8,128)(2,1)} %fusion.17), channel_id=1, source_target_pairs={{0,8},{4,12},{8,16},{12,20},{16,24},{20,28},{1,9},{5,13},{9,17},{1... | collective-permute-start | bytes 2752520 | tf_op jit(solution)/shard_map/ppermute | solution.py:265
  449.7 53.7 %copy-start.23 = (bf16[192,1024]{1,0:T(8,128)(2,1)S(1)}, bf16[192,1024]{1,0:T(8,128)(2,1)}, u32[]{:S(2)}) copy-start(bf16[192,1024]{1,0:T(8,128)(2,1)} %reduce-scatter.5.cloned.1.call-done) | copy-start | bytes 1179652
  (24 other events, 81.4 us)
Sparse Core Ops, SparseCore 0:
  9.7 76.0 all-gather.5
  87.4 71.9 all-gather.3
  161.1 88.0 all-gather.7
  310.0 34.4 reduce-scatter.4
  348.0 63.6 reduce-scatter.2

commit v3 on v2

--- a/solution.py
+++ b/solution.py
@@ -129,24 +129,196 @@
 
 
 def down_grad_kernel(ids, hidden, gout, out):
-    n, size = out.shape[0], out.shape[1]
-
-    def body(b, r, c):
-        out[b] = dot(hidden[:, lanes(c, size)], gout[:, lanes(r, size)], TN).astype(BF16)
-
-    for_blocks(ids, pl.program_id(0) * n, n, body)
-
-
-def gate_up_grad_kernel(ids, x, dgate, dup, out_gate, out_up):
-    n, size = out_gate.shape[0], out_gate.shape[1]
+    n, size = out.shape[2], out.shape[3]
+
+    def body(b, r, c):
+        out[0, 0, b] = dot(hidden[:, lanes(c, size)], gout[:, lanes(r, size)], TN).astype(BF16)
+
+    for_blocks(ids, pl.program_id(0) * n, n, body)
+
+
+def gate_up_grad_kernel(ids, x, dgate, dup, out):
+    n, size = out.shape[2], out.shape[3]
 
     def body(b, r, c):
         right = jnp.concatenate([dgate[:, lanes(c, size)], dup[:, lanes(c, size)]], axis=1)
         both = dot(x[:, lanes(r, size)], right, TN).astype(BF16)
-        out_gate[b] = both[:, :size]
-        out_up[b] = both[:, size:]
-
-    for_blocks(ids, pl.program_id(0) * n, n, body)
+        out[0, 0, b] = both[:, :size]
+        out[0, 1, b] = both[:, size:]
+
+    for_blocks(ids, pl.program_id(0) * n, n, body)
+
+
+def line_sum_kernel(own, other, out, held, below, above, pair_send, pair_recv, up_send, up_recv, down_send, down_recv):
+    chips, arrays, owned = own.shape[:3]
+    dp = lax.axis_index("dp")
+    tensor = lax.axis_index("tensor")
+    chip, core = dp // 2, dp % 2
+    sibling = (chip * 2 + 1 - core, tensor)
+    upper, lower = (dp + 2, tensor), (dp - 2, tensor)
+    has_upper, has_lower = chip < chips - 1, chip > 0
+    mesh_id = pl.DeviceIdType.MESH
+
+    barrier = pltpu.get_barrier_semaphore()
+    pl.semaphore_signal(barrier, inc=1, device_id=sibling, device_id_type=mesh_id)
+
+    @pl.when(has_upper)
+    def _():
+        pl.semaphore_signal(barrier, inc=1, device_id=upper, device_id_type=mesh_id)
+
+    @pl.when(has_lower)
+    def _():
+        pl.semaphore_signal(barrier, inc=1, device_id=lower, device_id_type=mesh_id)
+
+    pl.semaphore_wait(barrier, 1 + has_upper.astype(jnp.int32) + has_lower.astype(jnp.int32))
+
+    def pair_copy(j, a):
+        return pltpu.make_async_remote_copy(
+            src_ref=other.at[j, a], dst_ref=held.at[j, a],
+            send_sem=pair_send.at[j, a], recv_sem=pair_recv.at[j, a],
+            device_id=sibling, device_id_type=mesh_id,
+        )
+
+    def up_copy(step, a):
+        return pltpu.make_async_remote_copy(
+            src_ref=held.at[lax.rem(chips - 1 - step + chip, chips), a], dst_ref=below.at[step, a],
+            send_sem=up_send.at[step, a], recv_sem=up_recv.at[step, a],
+            device_id=upper, device_id_type=mesh_id,
+        )
+
+    def down_copy(step, a):
+        return pltpu.make_async_remote_copy(
+            src_ref=held.at[lax.rem(chip + 1 + step, chips), a], dst_ref=above.at[step, a],
+            send_sem=down_send.at[step, a], recv_sem=down_recv.at[step, a],
+            device_id=lower, device_id_type=mesh_id,
+        )
+
+    for k in range(chips):
+        j = jnp.where(2 * chip < chips, chips - 1 - k, k)
+        for a in range(arrays):
+            pair_copy(j, a).start()
+
+    def add(j, a, arrived):
+        def body(b, carry):
+            total = own[j, a, b].astype(F32) + held[j, a, b].astype(F32)
+            if arrived is not None:
+                total = total + arrived[b].astype(F32)
+            held[j, a, b] = total.astype(BF16)
+            return carry
+
+        lax.fori_loop(0, owned, body, 0)
+
+    def pass_on(step, a, sends, first, j, copy, arrived):
+        @pl.when(sends)
+        def _():
+            pair_copy(j, a).wait_recv()
+
+            @pl.when(first)
+            def _():
+                add(j, a, None)
+
+            if step:
+
+                @pl.when(jnp.logical_not(first))
+                def _():
+                    copy(step - 1, a).wait_recv()
+                    add(j, a, arrived.at[step - 1, a])
+
+                @pl.when(sends_at(step - 1, first, chip, copy))
+                def _():
+                    copy(step - 1, a).wait_send()
+
+            copy(step, a).start()
+
+    def sends_at(step, first, chip, copy):
+        return chip <= step if copy is up_copy else chips - 1 - chip <= step
+
+    for step in range(chips - 1):
+        for a in range(arrays):
+            pass_on(
+                step, a, jnp.logical_and(has_upper, chip <= step), chip == 0,
+                lax.rem(chips - 1 - step + chip, chips), up_copy, below,
+            )
+            pass_on(
+                step, a, jnp.logical_and(has_lower, chips - 1 - chip <= step), chip == chips - 1,
+                lax.rem(chip + 1 + step, chips), down_copy, above,
+            )
+
+    for a in range(arrays):
+        pair_copy(chip, a).wait_recv()
+
+        @pl.when(has_lower)
+        def _():
+            up_copy(chips - 2, a).wait_recv()
+
+        @pl.when(has_upper)
+        def _():
+            down_copy(chips - 2, a).wait_recv()
+
+        def base(b):
+            return own[chip, a, b].astype(F32) + held[chip, a, b].astype(F32)
+
+        def each(value):
+            def body(b, carry):
+                out[a, b] = value(b)
+                return carry
+
+            lax.fori_loop(0, owned, body, 0)
+
+        inner = jnp.logical_and(has_lower, has_upper)
+
+        @pl.when(inner)
+        def _():
+            each(lambda b: base(b) + below[chips - 2, a, b].astype(F32) + above[chips - 2, a, b].astype(F32))
+
+        @pl.when(jnp.logical_and(has_lower, jnp.logical_not(has_upper)))
+        def _():
+            each(lambda b: base(b) + below[chips - 2, a, b].astype(F32))
+
+        @pl.when(jnp.logical_and(has_upper, jnp.logical_not(has_lower)))
+        def _():
+            each(lambda b: base(b) + above[chips - 2, a, b].astype(F32))
+
+        for j in range(chips):
+            pair_copy(j, a).wait_send()
+
+        @pl.when(has_upper)
+        def _():
+            up_copy(chips - 2, a).wait_send()
+
+        @pl.when(has_lower)
+        def _():
+            down_copy(chips - 2, a).wait_send()
+
+
+def line_sum(own, other, collective_id, name):
+    chips, arrays = own.shape[:2]
+    piece = own.shape[2:]
+    line = (chips - 1, arrays)
+    return pl.pallas_call(
+        line_sum_kernel,
+        out_shape=jax.ShapeDtypeStruct(own.shape[1:], F32),
+        in_specs=[pl.BlockSpec(memory_space=pltpu.VMEM)] * 2,
+        out_specs=pl.BlockSpec(memory_space=pltpu.VMEM),
+        scratch_shapes=[
+            pltpu.VMEM(own.shape, BF16),
+            pltpu.VMEM((*line, *piece), BF16),
+            pltpu.VMEM((*line, *piece), BF16),
+            pltpu.SemaphoreType.DMA((chips, arrays)),
+            pltpu.SemaphoreType.DMA((chips, arrays)),
+            pltpu.SemaphoreType.DMA(line),
+            pltpu.SemaphoreType.DMA(line),
+            pltpu.SemaphoreType.DMA(line),
+            pltpu.SemaphoreType.DMA(line),
+        ],
+        compiler_params=pltpu.CompilerParams(
+            collective_id=collective_id, has_side_effects=True, vmem_limit_bytes=56 * 2**20
+        ),
+        cost_estimate=pl.CostEstimate(
+            flops=own.size, bytes_accessed=64 * own.size, transcendentals=0
+        ),
+        name=name,
+    )(own, other)
 
 
 def call(kernel, ids, whole, blocks, outs, flops, steps, acc=None, name=None, after=()):
@@ -155,7 +327,9 @@
     def body(*refs):
         kernel(*refs[:read], *refs[read + len(after) :])
 
-    chunked = lambda shape: pl.BlockSpec((shape[0] // steps, *shape[1:]), lambda i, ids: (i, 0, 0))
+    chunked = lambda shape: pl.BlockSpec(
+        (shape[0] // steps, *shape[1:]), lambda i, ids: (i, *[0] * (len(shape) - 1))
+    )
     resident = lambda shape: pl.BlockSpec(shape, lambda i, ids: (0, 0))
     order = [(a, resident(a.shape)) if a.ndim == 2 else (a, chunked(a.shape)) for a in (*whole, *blocks)]
     out_specs = [chunked(s) if cut else resident(s) for s, _, cut in outs]
@@ -230,83 +404,41 @@
         return lax.dynamic_index_in_dim(owner_ids, which, 1, keepdims=False).reshape(-1)
 
     other_ids, own_ids = half_ids(1 - core), half_ids(core)
-    half = (chips * owned, size, size)
-    siblings = [(i, i ^ 1) for i in range(dp_count)]
-
-    def down_grads(which, after=()):
-        return call(
-            down_grad_kernel, which, [hidden, grad_out], [], [(half, BF16, True)],
-            flops // 2, chips, name="down_grad", after=after,
+
+    def down_grads(which):
+        (out,) = call(
+            down_grad_kernel, which, [hidden, grad_out], [], [((chips, 1, owned, size, size), BF16, True)],
+            flops // 2, chips, name="down_grad",
         )
-
-    def line_sum(own, received):
-        own = own.reshape(chips, owned, size, size)
-        received = received.reshape(chips, owned, size, size)
-
-        def part(target):
-            target = jnp.clip(target, 0, chips - 1)
-            a = lax.dynamic_index_in_dim(own, target, 0, keepdims=False)
-            b = lax.dynamic_index_in_dim(received, target, 0, keepdims=False)
-            return a.astype(F32) + b.astype(F32)
-
-        from_below = from_above = None
-        for step in range(chips - 1):
-            reach = chips - 1 - step
-            upward, downward = part(chip + reach), part(chip - reach)
-            if step:
-                upward = upward + from_below.astype(F32)
-                downward = downward + from_above.astype(F32)
-            upward, downward = upward.astype(BF16), downward.astype(BF16)
-            pairs = [(z, z + 1) for z in range(step + 1)]
-            up_pairs = [(2 * a + c, 2 * b + c) for a, b in pairs for c in (0, 1)]
-            down_pairs = [
-                (2 * (chips - 1 - a) + c, 2 * (chips - 1 - b) + c) for a, b in pairs for c in (0, 1)
-            ]
-            from_below = lax.ppermute(upward, "dp", up_pairs)
-            from_above = lax.ppermute(downward, "dp", down_pairs)
-            yield [upward, downward]
-        total = part(chip)
-        if from_below is not None:
-            total = total + from_below.astype(F32) + from_above.astype(F32)
-        yield total
-
-    (down_other,) = down_grads(other_ids)
-    down_received = lax.ppermute(down_other, "dp", siblings)
-    (down_own,) = down_grads(own_ids, [down_other])
-    down_line = list(line_sum(down_own, down_received))
-    grad_down = down_line[-1]
+        return out
+
+    (grad_down,) = line_sum(down_grads(own_ids), down_grads(other_ids), 0, "down_line")
 
     dgate, dup = call(
         hidden_grad_kernel, ids, [grad_out], [down_all, gate_pre, up_pre],
         [(acts, BF16, False), (acts, BF16, False)], flops, CHUNKS, acc=acts, name="hidden_grad",
-        after=down_line[min(1, chips - 2)] if chips > 1 else (),
-    )
-
-    def gate_up_grads(which, after=()):
-        return call(
-            gate_up_grad_kernel, which, [normed, dgate, dup], [], [(half, BF16, True), (half, BF16, True)],
-            flops, chips, name="gate_up_grad", after=after,
-        )
-
-    gate_other, up_other = gate_up_grads(other_ids, down_line[-2] if chips > 1 else ())
-    gate_received = lax.ppermute(gate_other, "dp", siblings)
-    up_received = lax.ppermute(up_other, "dp", siblings)
-    gate_own, up_own = gate_up_grads(own_ids, [gate_other])
-    gate_line = list(line_sum(gate_own, gate_received))
-    up_line = list(line_sum(up_own, up_received))
-    grad_gate, grad_up = gate_line[-1], up_line[-1]
-    first = (gate_line[0] + up_line[0]) if chips > 1 else []
-    last = (gate_line[-2] + up_line[-2]) if chips > 1 else []
-
+        after=[grad_down],
+    )
     rows = (tokens, width)
     (normed_grad,) = call(
         normed_grad_kernel, ids, [dgate, dup], [gate_all, up_all], [(rows, BF16, False)],
-        2 * flops, CHUNKS, acc=rows, name="normed_grad", after=first,
+        2 * flops, CHUNKS, acc=rows, name="normed_grad",
     )
     (ffn,) = call(
         ffn_kernel, ids, [hidden], [down_all], [(rows, BF16, False)], flops, CHUNKS, acc=rows, name="ffn",
         after=[normed_grad],
     )
+
+    def gate_up_grads(which):
+        (out,) = call(
+            gate_up_grad_kernel, which, [normed, dgate, dup], [],
+            [((chips, 2, owned, size, size), BF16, True)],
+            flops, chips, name="gate_up_grad", after=[ffn],
+        )
+        return out
+
+    grad_gate, grad_up = line_sum(gate_up_grads(own_ids), gate_up_grads(other_ids), 1, "gate_up_line")
+
     grad_share = lax.psum_scatter(normed_grad, "tensor", scatter_dimension=1, tiled=True).astype(F32)
     ffn_share = lax.psum_scatter(ffn, "tensor", scatter_dimension=1, tiled=True).astype(F32)
     mixed_share = share(mixed)
@@ -327,7 +459,7 @@
     sums = lax.dynamic_update_slice_in_dim(sums, jnp.stack(depth_list), 0, 0)
     sums = lax.dynamic_update_slice_in_dim(sums, gain_part, slots + share_start, 0)
     sums = lax.dynamic_update_slice_in_dim(sums, along_part, slots + width + dp * tokens, 0)
-    sums = lax.optimization_barrier((sums, *last))[0]
+    sums = lax.optimization_barrier((sums, grad_gate))[0]
     sums = lax.psum(sums, ("dp", "tensor"))
     depth_sum = sums[:slots]
     gain_sum = lax.dynamic_slice_in_dim(sums, slots + share_start, share_width, 0)

time: 522 us -> 575 us (1.10)
  Pallas kernels: 90.1 us -> 320 us
  starting transfers between devices: 98 us -> 0.19 us
  other arithmetic: 75.1 us -> 26.2 us
  waiting for transfers between devices: 161 us -> 115 us
  local copies, waits for them, and re-layouts: 26.1 us -> 43.8 us
    pallas_call x0 -> x2, Pallas kernels: none -> 231 us  [line_sum(): pl.pallas_call(line_sum_kernel, out_shape=jax.ShapeDtypeStruct(own.shape[...]
    ppermute x21 -> x0, starting transfers between devices: 97.8 us -> none  [the longest x9 85.2 us: line_sum(): from_below = lax.ppermute(upward, 'dp', up_pairs)]
    ppermute x21 -> x0, waiting for transfers between devices: 42 us -> none  [the longest x9 41.9 us: line_sum(): from_below = lax.ppermute(upward, 'dp', up_pairs)]
    convert_element_type x11 -> x0, other arithmetic: 39.5 us -> none  [line_sum(): upward, downward = (upward.astype(BF16), downward.astype(BF16))]
    unnamed x63 -> x50, local copies, waits for them, and re-layouts: 22.7 us -> 34.5 us
    add x3 -> x0, other arithmetic: 11.6 us -> none  [line_sum(): total = total + from_below.astype(F32) + from_above.astype(F32)]
  transfers between devices with their start and end apart: 26 -> 5, of which waited for: 5 -> 2; matrix products, arithmetic and copies ran while one was open for 13% -> 6% of each run, Pallas kernels for 13% -> 51%
where the time goes in v3:
time: 575 us; the launch traced here: 574 us
  Pallas kernels  320 us (56%)
  waiting for transfers between devices  115 us (20%)
  local copies, waits for them, and re-layouts  43.8 us (8%)
  blocking collectives  41.8 us (7%)
  between operations  27 us (5%)
  other arithmetic  26.2 us (5%)
    pallas_call x2, Pallas kernels, line_sum(): pl.pallas_call(line_sum_kernel, out_shape=jax.ShapeDtypeStruct(own.shape[...  231 us
    pallas_call x9, Pallas kernels, call(): pl.pallas_call(body, out_shape=out_shape, grid_spec=pltpu.PrefetchScalarG...  88.5 us
    all_gather x1, waiting for transfers between devices, per_device(): up_all = lax.all_gather(up_blocks, 'dp', axis=0, tiled=True)  59.6 us
    all_gather x1, waiting for transfers between devices, per_device(): gate_all = lax.all_gather(gate_blocks, 'dp', axis=0, tiled=True)  53.6 us
    psum x1, blocking collectives, per_device(): sums = lax.psum(sums, ('dp', 'tensor'))  41.8 us
    unnamed x50, local copies, waits for them, and re-layouts  34.5 us
  transfers between devices with their start and end apart: 5, of which 2 were waited for; matrix products, arithmetic and copies ran while one was open for 6% of the time, Pallas kernels for 51%

profile of v3, /device:TPU:0, one launch (start us, length us, event | category | flops | bytes accessed | tf_op | source)
XLA Modules:
  0.0 574.1 jit_solution(13263161171654432417)
XLA Ops:
  21.5 8.2 %fusion.6 = (f32[192]{0:T(256)S(1)}, f32[192]{0:T(256)S(1)}, f32[192]{0:T(256)S(1)}, f32[192]{0:T(256)S(1)}, f32[192]{0:T(256)S(1)}, /*index=5*/f32[192,4096]{1,0:T(8,128)}) fusion(bf16[4,192,4096]{2,1,0:T(8,128)(2,1)} %param.9, s32[]{:T(128)S(6)} %select_n.48, s32[]{:T(128)S(6)} %select_n.51, s32[]{:T(128)S(6)} %select_n.50, s32[]{:T(128)S(6)} %select_n.49, ...), kind=kLoop, calls=%fused_computation.14 | loop fusion | flops 16514112 | bytes 9441056 | tf_op jit(solution)/shard_map/reduce_sum | solution.py:455
  29.8 2.4 multiply_convert_fusion.refs_1_
  32.2 53.6 %all-gather.6.cloned.1.call-done.refs_2_.refs_3_ = bf16[224,128,128]{2,1,0:T(8,128)(2,1)} async-done(((bf16[28,128,128]{2,1,0:T(8,128)(2,1)}), bf16[224,128,128]{2,1,0:T(8,128)(2,1)}) %all-gather.6.cloned.1.call-update) | async-done | bytes 7340048 | tf_op jit(solution)/shard_map/all_gather | solution.py:380
  85.8 3.1 copy-done.7
  88.9 9.5 %gate.1.refs_3_ = f32[192,3584]{1,0:T(8,128)S(1)} custom-call(s32[448]{0:T(512)S(1)} %reshape.55.refs_0_, bf16[192,4096]{1,0:T(8,128)(2,1)S(1)} %multiply_convert_fusion.refs_1_, bf16[224,128,128]{2,1,0:T(8,128)(2,1)S(1)} %copy-done.7), custom_call_target="tpu_custom_call" | custom-call | flops 5637144576 | bytes 11665408 | tf_op jit(solution)/shard_map/gate/pallas_call | solution.py:339
  98.4 1.5 copy-done.10
  99.9 59.6 %all-gather.4.cloned.1.call-done.refs_2_.refs_4_ = bf16[224,128,128]{2,1,0:T(8,128)(2,1)} async-done(((bf16[28,128,128]{2,1,0:T(8,128)(2,1)}), bf16[224,128,128]{2,1,0:T(8,128)(2,1)}) %all-gather.4.cloned.1.call-update) | async-done | bytes 7340048 | tf_op jit(solution)/shard_map/all_gather | solution.py:381
  159.5 1.8 copy-done.11
  161.2 12.3 %up_hidden.1 = (f32[192,3584]{1,0:T(8,128)S(1)}, bf16[192,3584]{1,0:T(8,128)(2,1)S(1)}) custom-call(s32[448]{0:T(512)S(1)} %reshape.55.refs_0_, bf16[192,4096]{1,0:T(8,128)(2,1)S(1)} %multiply_convert_fusion.refs_1_, bf16[224,128,128]{2,1,0:T(8,128)(2,1)} %all-gather.4.cloned.1.call-done.refs_2_.refs_4_, f32[192,3584]{1,0:T(8,128)S(1)} %copy-done.11), custom_call_target="tpu_custom_call" | custom-call | flops 5637144576 | bytes 15794176 | tf_op jit(solution)/shard_map/up_hidden/pallas_call | solution.py:339
  173.6 1.6 copy-done.13
  175.1 6.1 %down_grad.2.own = bf16[4,1,28,128,128]{4,3,2,1,0:T(8,128)(2,1)S(1)} custom-call(s32[224]{0:T(256)S(1)} %reshape.57.refs_0_, bf16[192,3584]{1,0:T(8,128)(2,1)S(1)} %get-tuple-element.12.refs_1_, bf16[192,4096]{1,0:T(8,128)(2,1)S(1)} %copy-done.6), custom_call_target="tpu_custom_call" | custom-call | flops 2818572288 | bytes 6619136 | tf_op jit(solution)/shard_map/down_grad/pallas_call | solution.py:339
  181.3 1.9 copy-done.4
  183.1 6.1 %down_grad.3.other = bf16[4,1,28,128,128]{4,3,2,1,0:T(8,128)(2,1)S(1)} custom-call(s32[224]{0:T(256)S(1)} %reshape.58.refs_0_, bf16[192,3584]{1,0:T(8,128)(2,1)S(1)} %get-tuple-element.12.refs_1_, bf16[192,4096]{1,0:T(8,128)(2,1)S(1)} %copy-done.6), custom_call_target="tpu_custom_call" | custom-call | flops 2818572288 | bytes 6619136 | tf_op jit(solution)/shard_map/down_grad/pallas_call | solution.py:339
  189.2 1.8 copy-done.5
  191.0 101.5 %down_line.1 = f32[1,28,128,128]{3,2,1,0:T(8,128)} custom-call(bf16[4,1,28,128,128]{4,3,2,1,0:T(8,128)(2,1)} %copy-done.4, bf16[4,1,28,128,128]{4,3,2,1,0:T(8,128)(2,1)} %copy-done.5), custom_call_target="tpu_custom_call" | custom-call | flops 1835008 | bytes 117440512 | tf_op jit(solution)/shard_map/down_line/pallas_call | solution.py:298
  294.1 1.8 copy-done.12
  295.8 1.8 copy-done.14
  297.6 13.7 %hidden_grad.1 = (bf16[192,3584]{1,0:T(8,128)(2,1)S(1)}, bf16[192,3584]{1,0:T(8,128)(2,1)S(1)}) custom-call(s32[448]{0:T(512)S(1)} %reshape.55.refs_0_, bf16[192,4096]{1,0:T(8,128)(2,1)S(1)} %copy-done.6, bf16[224,128,128]{2,1,0:T(8,128)(2,1)} %all-gather.8.cloned.1.call-done.refs_2_, f32[192,3584]{1,0:T(8,128)S(1)} %copy-done.12, ...), custom_call_target="tpu_custom_call" | custom-call | flops 5637144576 | bytes 17170432 | tf_op jit(solution)/shard_map/hidden_grad/pallas_call | solution.py:339
  311.4 3.1 copy-done.8
  314.4 15.4 %normed_grad.1.refs_3_ = bf16[192,4096]{1,0:T(8,128)(2,1)} custom-call(s32[448]{0:T(512)S(1)} %reshape.55.refs_0_, bf16[192,3584]{1,0:T(8,128)(2,1)S(1)} %get-tuple-element.14.refs_1_.refs_2_, bf16[192,3584]{1,0:T(8,128)(2,1)S(1)} %get-tuple-element.15.refs_2_.refs_3_, bf16[224,128,128]{2,1,0:T(8,128)(2,1)S(1)} %copy-done.8, ...), custom_call_target="tpu_custom_call" | custom-call | flops 11274289152 | bytes 19005440 | tf_op jit(solution)/shard_map/normed_grad/pallas_call | solution.py:339
  332.1 3.1 copy-done.9
  336.5 11.8 %ffn.1.refs_4_ = bf16[192,4096]{1,0:T(8,128)(2,1)} custom-call(s32[448]{0:T(512)S(1)} %reshape.55.refs_0_, bf16[192,3584]{1,0:T(8,128)(2,1)S(1)} %copy-done.16, bf16[224,128,128]{2,1,0:T(8,128)(2,1)S(1)} %copy-done.9, bf16[192,4096]{1,0:T(8,128)(2,1)} %normed_grad.1.refs_3_), custom_call_target="tpu_custom_call" | custom-call | flops 5637144576 | bytes 10289152 | tf_op jit(solution)/shard_map/ffn/pallas_call | solution.py:339
  348.4 8.5 %dynamic-slice_convert_fusion.2 = (f32[1,192,4096]{2,1,0:T(8,128)}, f32[1,192,4096]{2,1,0:T(8,128)}, f32[1,192,4096]{2,1,0:T(8,128)}, f32[1,192,4096]{2,1,0:T(8,128)}) fusion(bf16[4,192,4096]{2,1,0:T(8,128)(2,1)} %param.9, s32[]{:T(128)S(6)} %select_n.49, s32[]{:T(128)S(6)} %select_n.48, s32[]{:T(128)S(6)} %select_n.51, s32[]{:T(128)S(6)} %select_n.50), kind=kLoop, calls=%fused_computation.21 | loop fusion | flops 3145728 | bytes 18874384 | tf_op jit(solution)/shard_map/convert_element_type | solution.py:390
  356.8 6.8 %gate_up_grad.3.other = bf16[4,2,28,128,128]{4,3,2,1,0:T(8,128)(2,1)S(1)} custom-call(s32[224]{0:T(256)S(1)} %reshape.58.refs_0_, bf16[192,4096]{1,0:T(8,128)(2,1)S(1)} %multiply_convert_fusion.refs_1_, bf16[192,3584]{1,0:T(8,128)(2,1)S(1)} %copy-done.18, bf16[192,3584]{1,0:T(8,128)(2,1)S(1)} %copy-done.20, bf16[192,4096]{1,0:T(8,128)(2,1)} %ffn.1.refs_4_), custom_call_target="tpu_custom_call" | custom-call | flops 5637144576 | bytes 11665408 | tf_op jit(solution)/shard_map/gate_up_grad/pallas_call | solution.py:339
  363.6 3.0 copy-done
  366.6 6.8 %gate_up_grad.2.own = bf16[4,2,28,128,128]{4,3,2,1,0:T(8,128)(2,1)S(1)} custom-call(s32[224]{0:T(256)S(1)} %reshape.57.refs_0_, bf16[192,4096]{1,0:T(8,128)(2,1)S(1)} %multiply_convert_fusion.refs_1_, bf16[192,3584]{1,0:T(8,128)(2,1)S(1)} %copy-done.18, bf16[192,3584]{1,0:T(8,128)(2,1)S(1)} %copy-done.20, bf16[192,4096]{1,0:T(8,128)(2,1)} %ffn.1.refs_4_), custom_call_target="tpu_custom_call" | custom-call | flops 5637144576 | bytes 11665408 | tf_op jit(solution)/shard_map/gate_up_grad/pallas_call | solution.py:339
  373.4 3.0 copy-done.1
  376.4 129.7 %gate_up_line.1 = f32[2,28,128,128]{3,2,1,0:T(8,128)} custom-call(bf16[4,2,28,128,128]{4,3,2,1,0:T(8,128)(2,1)} %copy-done.1, bf16[4,2,28,128,128]{4,3,2,1,0:T(8,128)(2,1)} %copy-done), custom_call_target="tpu_custom_call" | custom-call | flops 3670016 | bytes 234881024 | tf_op jit(solution)/shard_map/gate_up_line/pallas_call | solution.py:298
  506.1 4.3 slice_bitcast_fusion
  510.4 3.7 fusion.15
  520.6 41.8 %psum.7 = f32[5636]{0:T(1024)S(1)} all-reduce(f32[5636]{0:T(1024)S(1)} %dynamic_update_slice.11), channel_id=1, replica_groups=mesh['dp'=8,'tensor'=4] {'dp','tensor'}, use_global_device_ids=true, to_apply=%region_17.18 | all-reduce | flops 5636 | bytes 45088 | tf_op jit(solution)/shard_map/psum | solution.py:463
  563.7 2.7 multiply_subtract_fusion
  (67 shorter events, 15.3 us)
Async XLA Ops:
  7.2 13.8 %copy-start.22 = (f32[4]{0:T(128)S(1)}, f32[4]{0:T(128)}, u32[]{:S(2)}) copy-start(f32[4]{0:T(128)} %param.10) | copy-start | bytes 52
  7.2 78.6 %all-gather.6.cloned.1.call-start = ((), (), s32[]{:S(2)}) async-start(), calls=%async_computation.3 | async-start | bytes 8257536 | tf_op jit(solution)/shard_map/all_gather | solution.py:380
  7.9 151.6 %all-gather.4.cloned.1.call-start = ((), (), s32[]{:S(2)}) async-start(), calls=%async_computation.2 | async-start | bytes 8257536 | tf_op jit(solution)/shard_map/all_gather | solution.py:381
  8.7 283.9 %all-gather.8.cloned.1.call-start = ((), (), s32[]{:S(2)}) async-start(), calls=%async_computation.4 | async-start | bytes 8257536 | tf_op jit(solution)/shard_map/all_gather | solution.py:382
  9.4 501.0 %reduce-scatter.5.cloned.1.call-start = ((), (), s32[]{:S(2)}) async-start(), calls=%async_computation.6 | async-start | bytes 1966080 | tf_op jit(solution)/shard_map/reduce_scatter | solution.py:442
  21.5 8.2 %copy-start.21 = (f32[4096]{0:T(1024)S(1)}, f32[4096]{0:T(1024)}, u32[]{:S(2)}) copy-start(f32[4096]{0:T(1024)} %param.12) | copy-start | bytes 49156
  85.8 3.1 copy-start.7
  98.4 1.5 copy-start.10
  99.9 75.2 %copy-start.6 = (bf16[192,4096]{1,0:T(8,128)(2,1)S(1)}, bf16[192,4096]{1,0:T(8,128)(2,1)}, u32[]{:S(2)}) copy-start(bf16[192,4096]{1,0:T(8,128)(2,1)} %refs_1_.1) | copy-start | bytes 4718596
  159.5 1.8 copy-start.11
  173.5 1.6 copy-start.13
  175.1 6.1 %copy-start.15 = (bf16[192,3584]{1,0:T(8,128)(2,1)}, bf16[192,3584]{1,0:T(8,128)(2,1)S(1)}, u32[]{:S(2)}) copy-start(bf16[192,3584]{1,0:T(8,128)(2,1)S(1)} %get-tuple-element.12.refs_1_) | copy-start | bytes 4128772
  181.2 1.9 copy-start.4
  189.2 1.8 copy-start.5
  292.6 1.5 copy-start.2
  294.1 1.8 copy-start.12
  295.8 1.8 copy-start.14
  311.3 3.1 copy-start.8
  329.8 1.1 copy-start.17
  330.9 1.1 copy-start.19
  332.0 231.7 %reduce-scatter.3.cloned.1.call-start = ((), (), s32[]{:S(2)}) async-start(), calls=%async_computation.5 | async-start | bytes 1966080 | tf_op jit(solution)/shard_map/reduce_scatter | solution.py:443
  332.1 3.1 copy-start.9
  335.1 1.3 copy-start.16
  348.3 8.5 %copy-start.18 = (bf16[192,3584]{1,0:T(8,128)(2,1)S(1)}, bf16[192,3584]{1,0:T(8,128)(2,1)}, u32[]{:S(2)}) copy-start(bf16[192,3584]{1,0:T(8,128)(2,1)} %copy-done.17) | copy-start | bytes 4128772
  348.3 8.5 %copy-start.20 = (bf16[192,3584]{1,0:T(8,128)(2,1)S(1)}, bf16[192,3584]{1,0:T(8,128)(2,1)}, u32[]{:S(2)}) copy-start(bf16[192,3584]{1,0:T(8,128)(2,1)} %copy-done.19) | copy-start | bytes 4128772
  363.6 3.0 copy-start
  373.4 3.0 copy-start.1
  510.4 55.9 %copy-start.3 = (f32[1,28,128,128]{3,2,1,0:T(8,128)S(1)}, f32[1,28,128,128]{3,2,1,0:T(8,128)}, u32[]{:S(2)}) copy-start(f32[1,28,128,128]{3,2,1,0:T(8,128)} %down_line.1) | copy-start | bytes 5505028
Sparse Core Ops, SparseCore 0:
  9.7 76.0 all-gather.5
  87.4 71.9 all-gather.3
  161.1 95.9 all-gather.7
  332.1 30.9 reduce-scatter.4
  366.0 30.8 reduce-scatter.2

commit v4 on v3

--- a/solution.py
+++ b/solution.py
@@ -149,7 +149,11 @@
     for_blocks(ids, pl.program_id(0) * n, n, body)
 
 
-def line_sum_kernel(own, other, out, held, below, above, pair_send, pair_recv, up_send, up_recv, down_send, down_recv):
+def line_sum_kernel(
+    own, other, rows_in, gain_in, out, rows_out, gain_out, held, below, above, rows_slots, gain_slots,
+    pair_send, pair_recv, up_send, up_recv, down_send, down_recv,
+    rows_send, rows_recv, gain_send, gain_recv,
+):
     chips, arrays, owned = own.shape[:3]
     dp = lax.axis_index("dp")
     tensor = lax.axis_index("tensor")
@@ -159,18 +163,60 @@
     has_upper, has_lower = chip < chips - 1, chip > 0
     mesh_id = pl.DeviceIdType.MESH
 
+    dp_count, tensor_count = gain_slots.shape[0], rows_slots.shape[0]
+
+    def dp_peer(k):
+        return (lax.rem(dp + k, dp_count), tensor)
+
+    def tensor_peer(k):
+        return (dp, lax.rem(tensor + k, tensor_count))
+
     barrier = pltpu.get_barrier_semaphore()
-    pl.semaphore_signal(barrier, inc=1, device_id=sibling, device_id_type=mesh_id)
-
-    @pl.when(has_upper)
-    def _():
-        pl.semaphore_signal(barrier, inc=1, device_id=upper, device_id_type=mesh_id)
-
-    @pl.when(has_lower)
-    def _():
-        pl.semaphore_signal(barrier, inc=1, device_id=lower, device_id_type=mesh_id)
-
-    pl.semaphore_wait(barrier, 1 + has_upper.astype(jnp.int32) + has_lower.astype(jnp.int32))
+    for k in range(1, dp_count):
+        pl.semaphore_signal(barrier, inc=1, device_id=dp_peer(k), device_id_type=mesh_id)
+    for k in range(1, tensor_count):
+        pl.semaphore_signal(barrier, inc=1, device_id=tensor_peer(k), device_id_type=mesh_id)
+    pl.semaphore_wait(barrier, dp_count + tensor_count - 2)
+
+    def rows_copy(k, slot):
+        return pltpu.make_async_remote_copy(
+            src_ref=rows_in, dst_ref=rows_slots.at[slot],
+            send_sem=rows_send.at[k - 1], recv_sem=rows_recv.at[k - 1],
+            device_id=tensor_peer(k), device_id_type=mesh_id,
+        )
+
+    def gain_copy(k, slot):
+        return pltpu.make_async_remote_copy(
+            src_ref=gain_slots.at[dp], dst_ref=gain_slots.at[slot],
+            send_sem=gain_send.at[k - 1], recv_sem=gain_recv.at[k - 1],
+            device_id=dp_peer(k), device_id_type=mesh_id,
+        )
+
+    def rows_sum():
+        rows_slots[tensor] = rows_in[...]
+        for k in range(1, tensor_count):
+            rows_copy(k, lax.rem(tensor - k + tensor_count, tensor_count)).wait_recv()
+        total = rows_slots[0]
+        for t in range(1, tensor_count):
+            total = total + rows_slots[t]
+        rows_out[...] = total
+        depth_row = gain_in.shape[0] - 8
+        gain_slots[dp] = gain_in[...]
+        gain_slots[dp, depth_row : depth_row + 1, :] = total[0:1, :]
+        for k in range(1, dp_count):
+            gain_copy(k, dp).start()
+
+    def gain_sum():
+        for k in range(1, dp_count):
+            gain_copy(k, lax.rem(dp - k + dp_count, dp_count)).wait_recv()
+        total = gain_slots[0]
+        for d in range(1, dp_count):
+            total = total + gain_slots[d]
+        gain_out[...] = total
+        for k in range(1, dp_count):
+            gain_copy(k, dp).wait_send()
+        for k in range(1, tensor_count):
+            rows_copy(k, tensor).wait_send()
 
     def pair_copy(j, a):
         return pltpu.make_async_remote_copy(
@@ -197,6 +243,9 @@
         j = jnp.where(2 * chip < chips, chips - 1 - k, k)
         for a in range(arrays):
             pair_copy(j, a).start()
+
+    for k in range(1, tensor_count):
+        rows_copy(k, tensor).start()
 
     def add(j, a, arrived):
         def body(b, carry):
@@ -243,7 +292,10 @@
                 step, a, jnp.logical_and(has_lower, chips - 1 - chip <= step), chip == chips - 1,
                 lax.rem(chip + 1 + step, chips), down_copy, above,
             )
-
+        if step == 0:
+            rows_sum()
+
+    gain_sum()
     for a in range(arrays):
         pair_copy(chip, a).wait_recv()
 
@@ -291,34 +343,47 @@
             down_copy(chips - 2, a).wait_send()
 
 
-def line_sum(own, other, collective_id, name):
+def line_sum(own, other, rows, gains):
     chips, arrays = own.shape[:2]
     piece = own.shape[2:]
     line = (chips - 1, arrays)
+    tensor_count, dp_count = lax.axis_size("tensor"), 2 * chips
+    whole = pl.BlockSpec(memory_space=pltpu.VMEM)
+    dma = pltpu.SemaphoreType.DMA
     return pl.pallas_call(
         line_sum_kernel,
-        out_shape=jax.ShapeDtypeStruct(own.shape[1:], F32),
-        in_specs=[pl.BlockSpec(memory_space=pltpu.VMEM)] * 2,
-        out_specs=pl.BlockSpec(memory_space=pltpu.VMEM),
+        out_shape=[
+            jax.ShapeDtypeStruct(own.shape[1:], F32),
+            jax.ShapeDtypeStruct(rows.shape, F32),
+            jax.ShapeDtypeStruct(gains.shape, F32),
+        ],
+        in_specs=[whole] * 4,
+        out_specs=[whole] * 3,
         scratch_shapes=[
             pltpu.VMEM(own.shape, BF16),
             pltpu.VMEM((*line, *piece), BF16),
             pltpu.VMEM((*line, *piece), BF16),
-            pltpu.SemaphoreType.DMA((chips, arrays)),
-            pltpu.SemaphoreType.DMA((chips, arrays)),
-            pltpu.SemaphoreType.DMA(line),
-            pltpu.SemaphoreType.DMA(line),
-            pltpu.SemaphoreType.DMA(line),
-            pltpu.SemaphoreType.DMA(line),
+            pltpu.VMEM((tensor_count, *rows.shape), F32),
+            pltpu.VMEM((dp_count, *gains.shape), F32),
+            dma((chips, arrays)),
+            dma((chips, arrays)),
+            dma(line),
+            dma(line),
+            dma(line),
+            dma(line),
+            dma((tensor_count - 1,)),
+            dma((tensor_count - 1,)),
+            dma((dp_count - 1,)),
+            dma((dp_count - 1,)),
         ],
         compiler_params=pltpu.CompilerParams(
-            collective_id=collective_id, has_side_effects=True, vmem_limit_bytes=56 * 2**20
+            collective_id=0, has_side_effects=True, vmem_limit_bytes=56 * 2**20
         ),
         cost_estimate=pl.CostEstimate(
             flops=own.size, bytes_accessed=64 * own.size, transcendentals=0
         ),
-        name=name,
-    )(own, other)
+        name="gate_up_line",
+    )(own, other, rows, gains)
 
 
 def call(kernel, ids, whole, blocks, outs, flops, steps, acc=None, name=None, after=()):
@@ -346,7 +411,7 @@
             out_specs=out_specs,
             scratch_shapes=[pltpu.VMEM(acc, F32)] if acc else [],
         ),
-        compiler_params=pltpu.CompilerParams(vmem_limit_bytes=40 * 2**20),
+        compiler_params=pltpu.CompilerParams(vmem_limit_bytes=60 * 2**20),
         cost_estimate=pl.CostEstimate(flops=4 * flops, bytes_accessed=moved, transcendentals=0),
         name=name,
     )(ids, *[a for a, _ in order], *after)
@@ -391,8 +456,20 @@
     scale_inv = lax.rsqrt(jnp.mean(mixed * mixed, axis=-1, keepdims=True) + EPSILON)
     normed = (mixed * scale_inv * gain).astype(BF16)
 
+    cubed = scale_inv * scale_inv * scale_inv / width
+    history_share, second = [], []
+    for slot in range(depth_index.shape[0]):
+        earlier = lax.dynamic_index_in_dim(history, depth_index[slot], 0, keepdims=False)
+        history_share.append(share(earlier))
+        second.append(jnp.sum(mixed * earlier.astype(F32), axis=-1) * cubed[:, 0])
+    history_share, second = jnp.stack(history_share), jnp.stack(second)
+    mixed_share = share(mixed)
+
     acts = (tokens, hidden_width)
-    (gate_pre,) = call(gate_kernel, ids, [normed], [gate_all], [(acts, F32, False)], flops, CHUNKS, name="gate")
+    (gate_pre,) = call(
+        gate_kernel, ids, [normed], [gate_all], [(acts, F32, False)], flops, CHUNKS, name="gate",
+        after=[history_share, second, mixed_share],
+    )
     up_pre, hidden = call(
         up_kernel, ids, [normed], [up_all, gate_pre], [(acts, F32, False), (acts, BF16, False)],
         flops, CHUNKS, name="up_hidden",
@@ -405,20 +482,58 @@
 
     other_ids, own_ids = half_ids(1 - core), half_ids(core)
 
-    def down_grads(which):
+    siblings = [(i, i ^ 1) for i in range(dp_count)]
+
+    def down_grads(which, after=()):
         (out,) = call(
             down_grad_kernel, which, [hidden, grad_out], [], [((chips, 1, owned, size, size), BF16, True)],
-            flops // 2, chips, name="down_grad",
+            flops // 2, chips, name="down_grad", after=after,
         )
         return out
 
-    (grad_down,) = line_sum(down_grads(own_ids), down_grads(other_ids), 0, "down_line")
+    def permute_sum(own, received):
+        own = own.reshape(chips, owned, size, size)
+        received = received.reshape(chips, owned, size, size)
+
+        def part(target):
+            target = jnp.clip(target, 0, chips - 1)
+            a = lax.dynamic_index_in_dim(own, target, 0, keepdims=False)
+            b = lax.dynamic_index_in_dim(received, target, 0, keepdims=False)
+            return a.astype(F32) + b.astype(F32)
+
+        from_below = from_above = None
+        for step in range(chips - 1):
+            reach = chips - 1 - step
+            upward, downward = part(chip + reach), part(chip - reach)
+            if step:
+                upward = upward + from_below.astype(F32)
+                downward = downward + from_above.astype(F32)
+            upward, downward = upward.astype(BF16), downward.astype(BF16)
+            pairs = [(z, z + 1) for z in range(step + 1)]
+            up_pairs = [(2 * a + c, 2 * b + c) for a, b in pairs for c in (0, 1)]
+            down_pairs = [
+                (2 * (chips - 1 - a) + c, 2 * (chips - 1 - b) + c) for a, b in pairs for c in (0, 1)
+            ]
+            from_below = lax.ppermute(upward, "dp", up_pairs)
+            from_above = lax.ppermute(downward, "dp", down_pairs)
+            yield [upward, downward]
+        total = part(chip)
+        if from_below is not None:
+            total = total + from_below.astype(F32) + from_above.astype(F32)
+        yield total
+
+    down_other = down_grads(other_ids)
+    down_received = lax.ppermute(down_other, "dp", siblings)
+    down_own = down_grads(own_ids, [down_other])
+    down_line = list(permute_sum(down_own, down_received))
+    grad_down = down_line[-1]
 
     dgate, dup = call(
         hidden_grad_kernel, ids, [grad_out], [down_all, gate_pre, up_pre],
         [(acts, BF16, False), (acts, BF16, False)], flops, CHUNKS, acc=acts, name="hidden_grad",
-        after=[grad_down],
-    )
+        after=down_line[min(1, chips - 2)] if chips > 1 else (),
+    )
+
     rows = (tokens, width)
     (normed_grad,) = call(
         normed_grad_kernel, ids, [dgate, dup], [gate_all, up_all], [(rows, BF16, False)],
@@ -426,7 +541,7 @@
     )
     (ffn,) = call(
         ffn_kernel, ids, [hidden], [down_all], [(rows, BF16, False)], flops, CHUNKS, acc=rows, name="ffn",
-        after=[normed_grad],
+        after=[normed_grad, *(down_line[-2] if chips > 1 else ())],
     )
 
     def gate_up_grads(which):
@@ -437,33 +552,31 @@
         )
         return out
 
-    grad_gate, grad_up = line_sum(gate_up_grads(own_ids), gate_up_grads(other_ids), 1, "gate_up_line")
-
     grad_share = lax.psum_scatter(normed_grad, "tensor", scatter_dimension=1, tiled=True).astype(F32)
     ffn_share = lax.psum_scatter(ffn, "tensor", scatter_dimension=1, tiled=True).astype(F32)
-    mixed_share = share(mixed)
-    layer_out = (mixed_share + ffn_share).astype(BF16)
 
     gain_share = share(gain)
-    cubed = scale_inv * scale_inv * scale_inv / width
     direct = share(grad_out).astype(F32) + scale_inv * gain_share * grad_share
     along_part = jnp.sum(grad_share * gain_share * mixed_share, axis=-1)
     gain_part = jnp.sum(grad_share * mixed_share * scale_inv, axis=0)
-    depth_list = []
-    for slot in range(depth_index.shape[0]):
-        earlier = lax.dynamic_index_in_dim(history, depth_index[slot], 0, keepdims=False).astype(F32)
-        second = jnp.sum(mixed * earlier, axis=-1) * cubed[:, 0]
-        depth_list.append(jnp.sum(direct * share(earlier)) - jnp.sum(along_part * second))
+    depth_part = jnp.sum(direct * history_share.astype(F32), axis=(1, 2)) - jnp.sum(along_part * second, axis=1)
     slots = depth_index.shape[0]
-    sums = jnp.zeros((slots + width + dp_count * tokens,), F32)
-    sums = lax.dynamic_update_slice_in_dim(sums, jnp.stack(depth_list), 0, 0)
-    sums = lax.dynamic_update_slice_in_dim(sums, gain_part, slots + share_start, 0)
-    sums = lax.dynamic_update_slice_in_dim(sums, along_part, slots + width + dp * tokens, 0)
-    sums = lax.optimization_barrier((sums, grad_gate))[0]
-    sums = lax.psum(sums, ("dp", "tensor"))
-    depth_sum = sums[:slots]
-    gain_sum = lax.dynamic_slice_in_dim(sums, slots + share_start, share_width, 0)
-    along = lax.dynamic_slice_in_dim(sums, slots + width + dp * tokens, tokens, 0)[:, None]
+    token_rows, gain_rows = -(-tokens // 128), -(-share_width // 1024) * 8
+    sum_rows = -(-(token_rows + 1) // 8) * 8
+    row_terms = jnp.zeros((sum_rows * 128,), F32)
+    row_terms = lax.dynamic_update_slice_in_dim(row_terms, depth_part, 0, 0)
+    row_terms = lax.dynamic_update_slice_in_dim(row_terms, along_part, 128, 0).reshape(sum_rows, 128)
+    gain_terms = jnp.zeros(((gain_rows + 8) * 128,), F32)
+    gain_terms = lax.dynamic_update_slice_in_dim(gain_terms, gain_part, 0, 0).reshape(gain_rows + 8, 128)
+
+    block_grads, row_sums, gain_sums = line_sum(
+        gate_up_grads(own_ids), gate_up_grads(other_ids), row_terms, gain_terms
+    )
+    grad_gate, grad_up = block_grads
+    depth_sum = gain_sums[gain_rows, :slots]
+    gain_sum = gain_sums.reshape(-1)[:share_width]
+    along = row_sums.reshape(-1)[128 : 128 + tokens][:, None]
+    layer_out = (mixed_share + ffn_share).astype(BF16)
     grad_mixed = direct - mixed_share * cubed * along
     return (layer_out, grad_mixed, grad_gate, grad_up, grad_down, depth_sum, gain_sum)
 

time: 575 us -> 517 us (0.90)
  Pallas kernels: 320 us -> 247 us
  waiting for transfers between devices: 115 us -> 168 us
  blocking collectives: 41.8 us -> 0 us
  local copies, waits for them, and re-layouts: 43.8 us -> 19.4 us
  starting transfers between devices: 0.19 us -> 23.3 us
  other arithmetic: 26.2 us -> 35.4 us
    pallas_call x2 -> x1, Pallas kernels: 231 us -> 131 us  [line_sum(): pl.pallas_call(line_sum_kernel, out_shape=[jax.ShapeDtypeStruct(own.shape...]
    ppermute x0 -> x7, waiting for transfers between devices: none -> 56.7 us  [the longest x3 55.7 us: permute_sum(): from_below = lax.ppermute(upward, 'dp', up_pairs)]
    psum x1 -> x0, blocking collectives: 41.8 us -> none  [per_device(): sums = lax.psum(sums, ('dp', 'tensor'))]
    unnamed x50 -> x49, local copies, waits for them, and re-layouts: 34.5 us -> 3.44 us
    pallas_call x9, Pallas kernels: 88.5 us -> 116 us  [call(): pl.pallas_call(body, out_shape=out_shape, grid_spec=pltpu.PrefetchScalarG...]
    ppermute x0 -> x7, starting transfers between devices: none -> 23.1 us  [the longest x3 18.1 us: permute_sum(): from_below = lax.ppermute(upward, 'dp', up_pairs)]
    convert_element_type x1 -> x3, other arithmetic: 8.46 us -> 14.8 us  [permute_sum(): upward, downward = (upward.astype(BF16), downward.astype(BF16))]
    reduce_sum x3 -> x4, other arithmetic: 12.7 us -> 10.1 us  [the longest x1 7.77 us: per_device(): second.append(jnp.sum(mixed * earlier.astype(F32), axis=-1) * cubed[:, 0])]
  transfers between devices with their start and end apart: 5 -> 12, of which waited for: 2 -> 5; matrix products, arithmetic and copies ran while one was open for 6% -> 10% of each run, Pallas kernels for 51% -> 41%
where the time goes in v4:
time: 517 us; the launch traced here: 515 us
  Pallas kernels  247 us (48%)
  waiting for transfers between devices  168 us (32%)
  other arithmetic  35.4 us (7%)
  starting transfers between devices  23.3 us (5%)
  between operations  21.9 us (4%)
  local copies, waits for them, and re-layouts  19.4 us (4%)
    pallas_call x1, Pallas kernels, line_sum(): pl.pallas_call(line_sum_kernel, out_shape=[jax.ShapeDtypeStruct(own.shape...  131 us
    pallas_call x9, Pallas kernels, call(): pl.pallas_call(body, out_shape=out_shape, grid_spec=pltpu.PrefetchScalarG...  116 us
    all_gather x1, waiting for transfers between devices, per_device(): up_all = lax.all_gather(up_blocks, 'dp', axis=0, tiled=True)  60.4 us
    ppermute x3, waiting for transfers between devices, permute_sum(): from_below = lax.ppermute(upward, 'dp', up_pairs)  55.7 us
    all_gather x1, waiting for transfers between devices, per_device(): gate_all = lax.all_gather(gate_blocks, 'dp', axis=0, tiled=True)  48.9 us
    ppermute x3, starting transfers between devices, permute_sum(): from_below = lax.ppermute(upward, 'dp', up_pairs)  18.1 us
    convert_element_type x3, other arithmetic, permute_sum(): upward, downward = (upward.astype(BF16), downward.astype(BF16))  14.8 us
  transfers between devices with their start and end apart: 12, of which 5 were waited for; matrix products, arithmetic and copies ran while one was open for 10% of the time, Pallas kernels for 41%

profile of v4, /device:TPU:0, one launch (start us, length us, event | category | flops | bytes accessed | tf_op | source)
XLA Modules:
  0.0 515.5 jit_solution(10403159036122225815)
XLA Ops:
  20.8 7.8 %fusion.3 = (f32[192]{0:T(256)S(1)}, f32[192]{0:T(256)S(1)}, f32[192]{0:T(256)S(1)}, f32[192]{0:T(256)S(1)}, f32[192]{0:T(256)S(1)}, /*index=5*/f32[192,4096]{1,0:T(8,128)S(1)}) fusion(bf16[4,192,4096]{2,1,0:T(8,128)(2,1)} %param.9, s32[]{:T(128)S(6)} %select_n.69, s32[]{:T(128)S(6)} %select_n.72, s32[]{:T(128)S(6)} %select_n.71, s32[]{:T(128)S(6)} %select_n.70, ...), kind=kLoop, calls=%fused_computation.11 | loop fusion | flops 16514112 | bytes 9441056 | tf_op jit(solution)/shard_map/reduce_sum | solution.py:464
  30.8 2.1 constant_dynamic-slice_fusion.5
  35.3 1.6 multiply_convert_fusion.refs_1_
  36.9 48.9 %all-gather.6.cloned.1.call-done.refs_2_.refs_3_ = bf16[224,128,128]{2,1,0:T(8,128)(2,1)} async-done(((bf16[28,128,128]{2,1,0:T(8,128)(2,1)}), bf16[224,128,128]{2,1,0:T(8,128)(2,1)}) %all-gather.6.cloned.1.call-update) | async-done | bytes 7340048 | tf_op jit(solution)/shard_map/all_gather | solution.py:445
  85.8 13.3 %gate.1.refs_3_ = f32[192,3584]{1,0:T(8,128)} custom-call(s32[448]{0:T(512)} %reshape.196.refs_0_, bf16[192,4096]{1,0:T(8,128)(2,1)} %multiply_convert_fusion.refs_1_, bf16[224,128,128]{2,1,0:T(8,128)(2,1)} %all-gather.6.cloned.1.call-done.refs_2_.refs_3_, bf16[4,192,1024]{2,1,0:T(8,128)(2,1)} %pad_maximum_fusion.refs_3_, ...), custom_call_target="tpu_custom_call" | custom-call | flops 5637144576 | bytes 11665408 | tf_op jit(solution)/shard_map/gate/pallas_call | solution.py:404
  99.1 60.4 %all-gather.4.cloned.1.call-done.refs_2_.refs_4_ = bf16[224,128,128]{2,1,0:T(8,128)(2,1)} async-done(((bf16[28,128,128]{2,1,0:T(8,128)(2,1)}), bf16[224,128,128]{2,1,0:T(8,128)(2,1)}) %all-gather.4.cloned.1.call-update) | async-done | bytes 7340048 | tf_op jit(solution)/shard_map/all_gather | solution.py:446
  159.5 15.8 %up_hidden.1 = (f32[192,3584]{1,0:T(8,128)}, bf16[192,3584]{1,0:T(8,128)(2,1)}) custom-call(s32[448]{0:T(512)} %reshape.196.refs_0_, bf16[192,4096]{1,0:T(8,128)(2,1)} %multiply_convert_fusion.refs_1_, bf16[224,128,128]{2,1,0:T(8,128)(2,1)} %all-gather.4.cloned.1.call-done.refs_2_.refs_4_, f32[192,3584]{1,0:T(8,128)} %gate.1.refs_3_), custom_call_target="tpu_custom_call" | custom-call | flops 5637144576 | bytes 15794176 | tf_op jit(solution)/shard_map/up_hidden/pallas_call | solution.py:404
  175.2 9.1 %down_grad.2.refs_3_ = bf16[4,1,28,128,128]{4,3,2,1,0:T(8,128)(2,1)} custom-call(s32[224]{0:T(256)} %reshape.199.refs_0_, bf16[192,3584]{1,0:T(8,128)(2,1)} %get-tuple-element.14.refs_1_, bf16[192,4096]{1,0:T(8,128)(2,1)} %refs_1_.1), custom_call_target="tpu_custom_call" | custom-call | flops 2818572288 | bytes 6619136 | tf_op jit(solution)/shard_map/down_grad/pallas_call | solution.py:404
  184.6 1.4 copy.22
  186.0 1.5 reshape.198.refs_0_
  187.6 9.1 %down_grad.3 = bf16[4,1,28,128,128]{4,3,2,1,0:T(8,128)(2,1)} custom-call(s32[224]{0:T(256)} %reshape.198.refs_0_, bf16[192,3584]{1,0:T(8,128)(2,1)} %get-tuple-element.14.refs_1_, bf16[192,4096]{1,0:T(8,128)(2,1)} %refs_1_.1, bf16[4,1,28,128,128]{4,3,2,1,0:T(8,128)(2,1)} %down_grad.2.refs_3_), custom_call_target="tpu_custom_call" | custom-call | flops 2818572288 | bytes 6619136 | tf_op jit(solution)/shard_map/down_grad/pallas_call | solution.py:404
  196.7 4.2 fusion.13
  200.9 2.2 collective-permute-start.1
  203.1 1.7 collective-permute-start.2
  204.8 37.9 %collective-permute-done.1 = bf16[28,128,128]{2,1,0:T(8,128)(2,1)} collective-permute-done((bf16[28,128,128]{2,1,0:T(8,128)(2,1)}, bf16[28,128,128]{2,1,0:T(8,128)(2,1)}, u32[]{:S(2)}, u32[]{:S(2)}) %collective-permute-start.1) | collective-permute-done | bytes 917536 | tf_op jit(solution)/shard_map/ppermute | solution.py:517
  242.7 5.1 fusion.10
  247.9 17.7 %hidden_grad.1 = (bf16[192,3584]{1,0:T(8,128)(2,1)}, bf16[192,3584]{1,0:T(8,128)(2,1)}) custom-call(s32[448]{0:T(512)} %reshape.196.refs_0_, bf16[192,4096]{1,0:T(8,128)(2,1)} %refs_1_.1, bf16[224,128,128]{2,1,0:T(8,128)(2,1)} %all-gather.8.cloned.1.call-done.refs_2_, f32[192,3584]{1,0:T(8,128)} %gate.1.refs_3_, f32[192,3584]{1,0:T(8,128)} %get-tuple-element.15.refs_4_, ...), custom_call_target="tpu_custom_call" | custom-call | flops 5637144576 | bytes 17170432 | tf_op jit(solution)/shard_map/hidden_grad/pallas_call | solution.py:404
  265.5 16.7 %normed_grad.1.refs_3_ = bf16[192,4096]{1,0:T(8,128)(2,1)} custom-call(s32[448]{0:T(512)} %reshape.196.refs_0_, bf16[192,3584]{1,0:T(8,128)(2,1)} %get-tuple-element.16.refs_1_.refs_2_, bf16[192,3584]{1,0:T(8,128)(2,1)} %get-tuple-element.17.refs_2_.refs_3_, bf16[224,128,128]{2,1,0:T(8,128)(2,1)} %all-gather.6.cloned.1.call-done.refs_2_.refs_3_, ...), custom_call_target="tpu_custom_call" | custom-call | flops 11274289152 | bytes 19005440 | tf_op jit(solution)/shard_map/normed_grad/pallas_call | solution.py:404
  282.3 6.5 %collective-permute-start.3 = (bf16[28,128,128]{2,1,0:T(8,128)(2,1)}, bf16[28,128,128]{2,1,0:T(8,128)(2,1)}, u32[]{:S(2)}, u32[]{:S(2)}) collective-permute-start(bf16[28,128,128]{2,1,0:T(8,128)(2,1)} %get-tuple-element.32.refs_5_), channel_id=1, source_target_pairs={{0,8},{4,12},{8,16},{12,20},{1,9},{5,13},{9,17},{13,21},{2,10},{6,... | collective-permute-start | bytes 2752520 | tf_op jit(solution)/shard_map/ppermute | solution.py:517
  288.8 1.6 collective-permute-start.4
  290.4 17.8 %collective-permute-done.3 = bf16[28,128,128]{2,1,0:T(8,128)(2,1)} collective-permute-done((bf16[28,128,128]{2,1,0:T(8,128)(2,1)}, bf16[28,128,128]{2,1,0:T(8,128)(2,1)}, u32[]{:S(2)}, u32[]{:S(2)}) %collective-permute-start.3) | collective-permute-done | bytes 917536 | tf_op jit(solution)/shard_map/ppermute | solution.py:517
  308.2 5.4 %fusion.8 = (bf16[28,128,128]{2,1,0:T(8,128)(2,1)}, bf16[28,128,128]{2,1,0:T(8,128)(2,1)}) fusion(bf16[28,128,128]{2,1,0:T(8,128)(2,1)} %collective-permute-done.4, bf16[4,1,28,128,128]{4,3,2,1,0:T(8,128)(2,1)} %collective-permute-done, s32[]{:T(128)S(6)} %min.27, bf16[4,1,28,128,128]{4,3,2,1,0:T(8,128)(2,1)} %down_grad.3, ...), kind=kLoop, calls=%fused_computation.21 | loop fusion | flops 5505024 | bytes 7340040 | tf_op jit(solution)/shard_map/convert_element_type | solution.py:511
  313.6 13.6 %ffn.1.refs_4_ = bf16[192,4096]{1,0:T(8,128)(2,1)} custom-call(s32[448]{0:T(512)} %reshape.196.refs_0_, bf16[192,3584]{1,0:T(8,128)(2,1)} %get-tuple-element.14.refs_1_, bf16[224,128,128]{2,1,0:T(8,128)(2,1)} %all-gather.8.cloned.1.call-done.refs_2_, bf16[192,4096]{1,0:T(8,128)(2,1)} %normed_grad.1.refs_3_, bf16[28,128,128]{2,1,0:T(8,128)(2,1)} %get-tuple-element.30.refs_4_, ...), custom_call_target="tpu_custom_call" | custom-call | flops 5637144576 | bytes 10289152 | tf_op jit(solution)/shard_map/ffn/pallas_call | solution.py:404
  327.3 9.4 %collective-permute-start.5 = (bf16[28,128,128]{2,1,0:T(8,128)(2,1)}, bf16[28,128,128]{2,1,0:T(8,128)(2,1)}, u32[]{:S(2)}, u32[]{:S(2)}) collective-permute-start(bf16[28,128,128]{2,1,0:T(8,128)(2,1)} %get-tuple-element.30.refs_4_), channel_id=1, source_target_pairs={{0,8},{4,12},{8,16},{12,20},{16,24},{20,28},{1,9},{5,13},{9,17},{1... | collective-permute-start | bytes 2752520 | tf_op jit(solution)/shard_map/ppermute | solution.py:517
  336.7 1.5 collective-permute-start.6
  338.1 10.4 %gate_up_grad.3.other = bf16[4,2,28,128,128]{4,3,2,1,0:T(8,128)(2,1)} custom-call(s32[224]{0:T(256)} %reshape.199.refs_0_, bf16[192,4096]{1,0:T(8,128)(2,1)} %multiply_convert_fusion.refs_1_, bf16[192,3584]{1,0:T(8,128)(2,1)} %get-tuple-element.16.refs_1_.refs_2_, bf16[192,3584]{1,0:T(8,128)(2,1)} %get-tuple-element.17.refs_2_.refs_3_, ...), custom_call_target="tpu_custom_call" | custom-call | flops 5637144576 | bytes 11665408 | tf_op jit(solution)/shard_map/gate_up_grad/pallas_call | solution.py:404
  348.5 10.4 %gate_up_grad.2.own = bf16[4,2,28,128,128]{4,3,2,1,0:T(8,128)(2,1)} custom-call(s32[224]{0:T(256)} %reshape.198.refs_0_, bf16[192,4096]{1,0:T(8,128)(2,1)} %multiply_convert_fusion.refs_1_, bf16[192,3584]{1,0:T(8,128)(2,1)} %get-tuple-element.16.refs_1_.refs_2_, bf16[192,3584]{1,0:T(8,128)(2,1)} %get-tuple-element.17.refs_2_.refs_3_, ...), custom_call_target="tpu_custom_call" | custom-call | flops 5637144576 | bytes 11665408 | tf_op jit(solution)/shard_map/gate_up_grad/pallas_call | solution.py:404
  360.0 3.9 fusion.7
  363.9 1.6 fusion.18
  367.6 131.4 %gate_up_line.1 = (f32[2,28,128,128]{3,2,1,0:T(8,128)}, f32[8,128]{1,0:T(8,128)}, f32[16,128]{1,0:T(8,128)}) custom-call(bf16[4,2,28,128,128]{4,3,2,1,0:T(8,128)(2,1)} %gate_up_grad.2.own, bf16[4,2,28,128,128]{4,3,2,1,0:T(8,128)(2,1)} %gate_up_grad.3.other, f32[8,128]{1,0:T(8,128)} %bitcast.76, f32[16,128]{1,0:T(8,128)} %pad_bitcast_fusion.gain_in), custom_call_target="tpu_custom_call" | custom-call | flops 3670016 | bytes 234881024 | tf_op jit(solution)/shard_map/gate_up_line/pallas_call | solution.py:353
  502.2 4.3 slice_bitcast_fusion
  506.5 2.5 multiply_subtract_fusion
  (89 shorter events, 16.9 us)
Async XLA Ops:
  7.2 2.3 copy-start.20
  7.2 8.1 %copy-start.19 = (s32[224,2]{0,1:T(2,128)S(1)}, s32[224,2]{0,1:T(2,128)}, u32[]{:S(2)}) copy-start(s32[224,2]{0,1:T(2,128)} %param.16) | copy-start | bytes 5380
  7.2 13.0 %copy-start.21 = (f32[4]{0:T(128)S(1)}, f32[4]{0:T(128)}, u32[]{:S(2)}) copy-start(f32[4]{0:T(128)} %param.10) | copy-start | bytes 52
  7.2 78.6 %all-gather.6.cloned.1.call-start = ((), (), s32[]{:S(2)}) async-start(), calls=%async_computation.3 | async-start | bytes 8257536 | tf_op jit(solution)/shard_map/all_gather | solution.py:445
  7.9 151.5 %all-gather.4.cloned.1.call-start = ((), (), s32[]{:S(2)}) async-start(), calls=%async_computation.2 | async-start | bytes 8257536 | tf_op jit(solution)/shard_map/all_gather | solution.py:446
  8.7 239.2 %all-gather.8.cloned.1.call-start = ((), (), s32[]{:S(2)}) async-start(), calls=%async_computation.4 | async-start | bytes 8257536 | tf_op jit(solution)/shard_map/all_gather | solution.py:447
  9.4 354.4 %reduce-scatter.5.cloned.1.call-start = ((), (), s32[]{:S(2)}) async-start(), calls=%async_computation.6 | async-start | bytes 1966080 | tf_op jit(solution)/shard_map/reduce_scatter | solution.py:555
  29.2 6.1 %copy-start.8 = (f32[192]{0:T(256)}, f32[192]{0:T(256)S(1)}, u32[]{:S(2)}) copy-start(f32[192]{0:T(256)S(1)} %get-tuple-element.47) | copy-start | bytes 2308
  29.2 0.6 copy-start.11
  32.9 0.8 copy-start.1
  33.0 0.9 copy-start.3
  33.0 1.0 copy-start.5
  33.0 2.3 copy-start.7
  184.3 12.4 %collective-permute-start = (bf16[4,1,28,128,128]{4,3,2,1,0:T(8,128)(2,1)}, bf16[4,1,28,128,128]{4,3,2,1,0:T(8,128)(2,1)}, u32[]{:S(2)}, u32[]{:S(2)}) collective-permute-start(bf16[4,1,28,128,128]{4,3,2,1,0:T(8,128)(2,1)} %down_grad.2.refs_3_), channel_id=1, source_target_pairs={{0,4},{4,0},{8,12},{12,8},{16,20},{20,16},{24,28},{28,24},{1,5},{5... | collective-permute-start | bytes 11010056 | tf_op jit(solution)/shard_map/ppermute | solution.py:526
  200.9 41.8 %collective-permute-start.1 = (bf16[28,128,128]{2,1,0:T(8,128)(2,1)}, bf16[28,128,128]{2,1,0:T(8,128)(2,1)}, u32[]{:S(2)}, u32[]{:S(2)}) collective-permute-start(bf16[28,128,128]{2,1,0:T(8,128)(2,1)} %get-tuple-element.34), channel_id=1, source_target_pairs={{0,8},{4,12},{1,9},{5,13},{2,10},{6,14},{3,11},{7,15}} | collective-permute-start | bytes 2752520 | tf_op jit(solution)/shard_map/ppermute | solution.py:517
  203.1 39.6 %collective-permute-start.2 = (bf16[28,128,128]{2,1,0:T(8,128)(2,1)}, bf16[28,128,128]{2,1,0:T(8,128)(2,1)}, u32[]{:S(2)}, u32[]{:S(2)}) collective-permute-start(bf16[28,128,128]{2,1,0:T(8,128)(2,1)} %get-tuple-element.33), channel_id=1, source_target_pairs={{24,16},{28,20},{25,17},{29,21},{26,18},{30,22},{27,19},{31,23}} | collective-permute-start | bytes 2752520 | tf_op jit(solution)/shard_map/ppermute | solution.py:518
  282.2 224.3 %reduce-scatter.3.cloned.1.call-start = ((), (), s32[]{:S(2)}) async-start(), calls=%async_computation.5 | async-start | bytes 1966080 | tf_op jit(solution)/shard_map/reduce_scatter | solution.py:556
  282.3 25.9 %collective-permute-start.3 = (bf16[28,128,128]{2,1,0:T(8,128)(2,1)}, bf16[28,128,128]{2,1,0:T(8,128)(2,1)}, u32[]{:S(2)}, u32[]{:S(2)}) collective-permute-start(bf16[28,128,128]{2,1,0:T(8,128)(2,1)} %get-tuple-element.32.refs_5_), channel_id=1, source_target_pairs={{0,8},{4,12},{8,16},{12,20},{1,9},{5,13},{9,17},{13,21},{2,10},{6,... | collective-permute-start | bytes 2752520 | tf_op jit(solution)/shard_map/ppermute | solution.py:517
  288.8 19.4 %collective-permute-start.4 = (bf16[28,128,128]{2,1,0:T(8,128)(2,1)}, bf16[28,128,128]{2,1,0:T(8,128)(2,1)}, u32[]{:S(2)}, u32[]{:S(2)}) collective-permute-start(bf16[28,128,128]{2,1,0:T(8,128)(2,1)} %get-tuple-element.31.refs_6_), channel_id=1, source_target_pairs={{24,16},{28,20},{16,8},{20,12},{25,17},{29,21},{17,9},{21,13},{26,... | collective-permute-start | bytes 2752520 | tf_op jit(solution)/shard_map/ppermute | solution.py:518
  327.3 31.7 %collective-permute-start.5 = (bf16[28,128,128]{2,1,0:T(8,128)(2,1)}, bf16[28,128,128]{2,1,0:T(8,128)(2,1)}, u32[]{:S(2)}, u32[]{:S(2)}) collective-permute-start(bf16[28,128,128]{2,1,0:T(8,128)(2,1)} %get-tuple-element.30.refs_4_), channel_id=1, source_target_pairs={{0,8},{4,12},{8,16},{12,20},{16,24},{20,28},{1,9},{5,13},{9,17},{1... | collective-permute-start | bytes 2752520 | tf_op jit(solution)/shard_map/ppermute | solution.py:517
  336.7 23.3 %collective-permute-start.6 = (bf16[28,128,128]{2,1,0:T(8,128)(2,1)}, bf16[28,128,128]{2,1,0:T(8,128)(2,1)}, u32[]{:S(2)}, u32[]{:S(2)}) collective-permute-start(bf16[28,128,128]{2,1,0:T(8,128)(2,1)} %get-tuple-element.29.refs_5_), channel_id=1, source_target_pairs={{24,16},{28,20},{16,8},{20,12},{8,0},{12,4},{25,17},{29,21},{17,9}... | collective-permute-start | bytes 2752520 | tf_op jit(solution)/shard_map/ppermute | solution.py:518
  358.9 4.9 dynamic-slice-start
  358.9 4.9 copy-start.9
  363.8 1.7 copy-start.12
  363.8 1.7 copy-start.14
  363.9 1.7 copy-start.16
  363.9 1.7 copy-start.18
  363.9 2.5 copy-start.2
  363.9 2.5 copy-start.4
  363.9 2.5 copy-start.6
  365.5 0.9 copy-start
  502.2 4.3 copy-start.22
  (4 other events, 2.5 us)
Sparse Core Ops, SparseCore 0:
  9.7 76.0 all-gather.5
  87.4 71.9 all-gather.3
  161.1 86.3 all-gather.7
  282.3 34.2 reduce-scatter.4
  327.4 35.0 reduce-scatter.2

commit v5 on v4

--- a/solution.py
+++ b/solution.py
@@ -150,7 +150,7 @@
 
 
 def line_sum_kernel(
-    own, other, rows_in, gain_in, out, rows_out, gain_out, held, below, above, rows_slots, gain_slots,
+    own, other, rows_in, gain_in, out_gate, out_up, rows_out, gain_out, held, below, above, rows_slots, gain_slots,
     pair_send, pair_recv, up_send, up_recv, down_send, down_recv,
     rows_send, rows_recv, gain_send, gain_recv,
 ):
@@ -312,7 +312,7 @@
 
         def each(value):
             def body(b, carry):
-                out[a, b] = value(b)
+                (out_gate, out_up)[a][b] = value(b)
                 return carry
 
             lax.fori_loop(0, owned, body, 0)
@@ -353,12 +353,13 @@
     return pl.pallas_call(
         line_sum_kernel,
         out_shape=[
-            jax.ShapeDtypeStruct(own.shape[1:], F32),
+            jax.ShapeDtypeStruct(piece, F32),
+            jax.ShapeDtypeStruct(piece, F32),
             jax.ShapeDtypeStruct(rows.shape, F32),
             jax.ShapeDtypeStruct(gains.shape, F32),
         ],
         in_specs=[whole] * 4,
-        out_specs=[whole] * 3,
+        out_specs=[whole] * 4,
         scratch_shapes=[
             pltpu.VMEM(own.shape, BF16),
             pltpu.VMEM((*line, *piece), BF16),
@@ -411,7 +412,7 @@
             out_specs=out_specs,
             scratch_shapes=[pltpu.VMEM(acc, F32)] if acc else [],
         ),
-        compiler_params=pltpu.CompilerParams(vmem_limit_bytes=60 * 2**20),
+        compiler_params=pltpu.CompilerParams(vmem_limit_bytes=40 * 2**20),
         cost_estimate=pl.CostEstimate(flops=4 * flops, bytes_accessed=moved, transcendentals=0),
         name=name,
     )(ids, *[a for a, _ in order], *after)
@@ -541,7 +542,7 @@
     )
     (ffn,) = call(
         ffn_kernel, ids, [hidden], [down_all], [(rows, BF16, False)], flops, CHUNKS, acc=rows, name="ffn",
-        after=[normed_grad, *(down_line[-2] if chips > 1 else ())],
+        after=[normed_grad],
     )
 
     def gate_up_grads(which):
@@ -569,10 +570,9 @@
     gain_terms = jnp.zeros(((gain_rows + 8) * 128,), F32)
     gain_terms = lax.dynamic_update_slice_in_dim(gain_terms, gain_part, 0, 0).reshape(gain_rows + 8, 128)
 
-    block_grads, row_sums, gain_sums = line_sum(
+    grad_gate, grad_up, row_sums, gain_sums = line_sum(
         gate_up_grads(own_ids), gate_up_grads(other_ids), row_terms, gain_terms
     )
-    grad_gate, grad_up = block_grads
     depth_sum = gain_sums[gain_rows, :slots]
     gain_sum = gain_sums.reshape(-1)[:share_width]
     along = row_sums.reshape(-1)[128 : 128 + tokens][:, None]

time: 517 us -> 503 us (0.973)
  Pallas kernels: 247 us -> 219 us
  local copies, waits for them, and re-layouts: 19.4 us -> 46.1 us
  other arithmetic: 35.4 us -> 29.1 us
  waiting for transfers between devices: 168 us -> 162 us
    unnamed x49 -> x81, local copies, waits for them, and re-layouts: 3.44 us -> 37.1 us
    pallas_call x9, Pallas kernels: 116 us -> 89.5 us  [call(): pl.pallas_call(body, out_shape=out_shape, grid_spec=pltpu.PrefetchScalarG...]
    ppermute x3, waiting for transfers between devices: 55.7 us -> 39.7 us  [permute_sum(): from_below = lax.ppermute(upward, 'dp', up_pairs)]
    all_gather x1, waiting for transfers between devices: 0.01 us -> 6.41 us  [per_device(): down_all = lax.all_gather(down_blocks, 'dp', axis=0, tiled=True)]
  transfers between devices with their start and end apart: 12 -> 12, of which waited for: 5 -> 6; matrix products, arithmetic and copies ran while one was open for 10% -> 7% of each run, Pallas kernels for 41% -> 38%
where the time goes in v5:
time: 503 us; the launch traced here: 501 us
  Pallas kernels  219 us (44%)
  waiting for transfers between devices  162 us (32%)
  local copies, waits for them, and re-layouts  46.1 us (9%)
  other arithmetic  29.1 us (6%)
  between operations  22.1 us (4%)
  starting transfers between devices  22 us (4%)
    pallas_call x1, Pallas kernels, line_sum(): pl.pallas_call(line_sum_kernel, out_shape=[jax.ShapeDtypeStruct(piece, F3...  130 us
    pallas_call x9, Pallas kernels, call(): pl.pallas_call(body, out_shape=out_shape, grid_spec=pltpu.PrefetchScalarG...  89.5 us
    all_gather x1, waiting for transfers between devices, per_device(): up_all = lax.all_gather(up_blocks, 'dp', axis=0, tiled=True)  58.4 us
    all_gather x1, waiting for transfers between devices, per_device(): gate_all = lax.all_gather(gate_blocks, 'dp', axis=0, tiled=True)  53.5 us
    ppermute x3, waiting for transfers between devices, permute_sum(): from_below = lax.ppermute(upward, 'dp', up_pairs)  39.7 us
    unnamed x81, local copies, waits for them, and re-layouts  37.1 us
    ppermute x3, starting transfers between devices, permute_sum(): from_below = lax.ppermute(upward, 'dp', up_pairs)  16.9 us
    convert_element_type x3, other arithmetic, permute_sum(): upward, downward = (upward.astype(BF16), downward.astype(BF16))  12.2 us
  transfers between devices with their start and end apart: 12, of which 6 were waited for; matrix products, arithmetic and copies ran while one was open for 7% of the time, Pallas kernels for 38%

profile of v5, /device:TPU:0, one launch (start us, length us, event | category | flops | bytes accessed | tf_op | source)
XLA Modules:
  0.0 500.7 jit_solution(1791880326683818589)
XLA Ops:
  19.2 7.9 %fusion.3 = (f32[192]{0:T(256)S(1)}, f32[192]{0:T(256)S(1)}, f32[192]{0:T(256)S(1)}, f32[192]{0:T(256)S(1)}, f32[192]{0:T(256)S(1)}, /*index=5*/f32[192,4096]{1,0:T(8,128)S(1)}) fusion(bf16[4,192,4096]{2,1,0:T(8,128)(2,1)} %param.9, s32[]{:T(128)S(6)} %select_n.69, s32[]{:T(128)S(6)} %select_n.72, s32[]{:T(128)S(6)} %select_n.71, s32[]{:T(128)S(6)} %select_n.70, ...), kind=kLoop, calls=%fused_computation.11 | loop fusion | flops 16514112 | bytes 9441056 | tf_op jit(solution)/shard_map/reduce_sum | solution.py:465
  28.2 2.4 constant_dynamic-slice_fusion.5
  32.3 53.5 %all-gather.6.cloned.1.call-done.refs_2_.refs_3_ = bf16[224,128,128]{2,1,0:T(8,128)(2,1)} async-done(((bf16[28,128,128]{2,1,0:T(8,128)(2,1)}), bf16[224,128,128]{2,1,0:T(8,128)(2,1)}) %all-gather.6.cloned.1.call-update) | async-done | bytes 7340048 | tf_op jit(solution)/shard_map/all_gather | solution.py:446
  86.9 3.1 copy-done.7
  90.0 9.5 %gate.1.refs_3_ = f32[192,3584]{1,0:T(8,128)S(1)} custom-call(s32[448]{0:T(512)S(1)} %reshape.196.refs_0_, bf16[192,4096]{1,0:T(8,128)(2,1)S(1)} %multiply_convert_fusion.refs_1_, bf16[224,128,128]{2,1,0:T(8,128)(2,1)S(1)} %copy-done.7, bf16[4,192,1024]{2,1,0:T(8,128)(2,1)S(1)} %pad_maximum_fusion.refs_3_, f32[4,192]{1,0:T(4,128)S(1)} %pad_maximum_fusion.1.refs_4_, ...), custom_call_target="tpu_custom_call" | custom-call | flops 5637144576 | bytes 11665408 | tf_op jit(solution)/shard_map/gate/pallas_call | solution.py:405
  101.1 58.4 %all-gather.4.cloned.1.call-done.refs_2_.refs_4_ = bf16[224,128,128]{2,1,0:T(8,128)(2,1)} async-done(((bf16[28,128,128]{2,1,0:T(8,128)(2,1)}), bf16[224,128,128]{2,1,0:T(8,128)(2,1)}) %all-gather.4.cloned.1.call-update) | async-done | bytes 7340048 | tf_op jit(solution)/shard_map/all_gather | solution.py:447
  159.5 1.8 copy-done.13
  161.3 12.3 %up_hidden.1 = (f32[192,3584]{1,0:T(8,128)S(1)}, bf16[192,3584]{1,0:T(8,128)(2,1)S(1)}) custom-call(s32[448]{0:T(512)S(1)} %reshape.196.refs_0_, bf16[192,4096]{1,0:T(8,128)(2,1)S(1)} %multiply_convert_fusion.refs_1_, bf16[224,128,128]{2,1,0:T(8,128)(2,1)} %all-gather.4.cloned.1.call-done.refs_2_.refs_4_, f32[192,3584]{1,0:T(8,128)S(1)} %copy-done.13), custom_call_target="tpu_custom_call" | custom-call | flops 5637144576 | bytes 15794176 | tf_op jit(solution)/shard_map/up_hidden/pallas_call | solution.py:405
  175.1 7.1 %down_grad.2.refs_3_ = bf16[4,1,28,128,128]{4,3,2,1,0:T(8,128)(2,1)} custom-call(s32[224]{0:T(256)S(1)} %reshape.199.refs_0_, bf16[192,3584]{1,0:T(8,128)(2,1)S(1)} %get-tuple-element.15.refs_1_, bf16[192,4096]{1,0:T(8,128)(2,1)S(1)} %copy-done.4), custom_call_target="tpu_custom_call" | custom-call | flops 2818572288 | bytes 6619136 | tf_op jit(solution)/shard_map/down_grad/pallas_call | solution.py:405
  184.1 6.1 %down_grad.3 = bf16[4,1,28,128,128]{4,3,2,1,0:T(8,128)(2,1)S(1)} custom-call(s32[224]{0:T(256)S(1)} %reshape.198.refs_0_, bf16[192,3584]{1,0:T(8,128)(2,1)S(1)} %copy-done.10, bf16[192,4096]{1,0:T(8,128)(2,1)S(1)} %copy-done.4, bf16[4,1,28,128,128]{4,3,2,1,0:T(8,128)(2,1)} %down_grad.2.refs_3_), custom_call_target="tpu_custom_call" | custom-call | flops 2818572288 | bytes 6619136 | tf_op jit(solution)/shard_map/down_grad/pallas_call | solution.py:405
  190.3 4.5 fusion.13
  197.7 38.9 %collective-permute-done.1 = bf16[28,128,128]{2,1,0:T(8,128)(2,1)S(1)} collective-permute-done((bf16[28,128,128]{2,1,0:T(8,128)(2,1)}, bf16[28,128,128]{2,1,0:T(8,128)(2,1)S(1)}, u32[]{:S(2)}, u32[]{:S(2)}) %collective-permute-start.1) | collective-permute-done | bytes 917536 | tf_op jit(solution)/shard_map/ppermute | solution.py:518
  237.5 3.5 fusion.10
  241.0 6.4 %all-gather.8.cloned.1.call-done.refs_2_ = bf16[224,128,128]{2,1,0:T(8,128)(2,1)} async-done(((bf16[28,128,128]{2,1,0:T(8,128)(2,1)}), bf16[224,128,128]{2,1,0:T(8,128)(2,1)}) %all-gather.8.cloned.1.call-update) | async-done | bytes 7340048 | tf_op jit(solution)/shard_map/all_gather | solution.py:448
  250.6 1.8 copy-done.16
  252.4 13.7 %hidden_grad.1 = (bf16[192,3584]{1,0:T(8,128)(2,1)S(1)}, bf16[192,3584]{1,0:T(8,128)(2,1)S(1)}) custom-call(s32[448]{0:T(512)S(1)} %reshape.196.refs_0_, bf16[192,4096]{1,0:T(8,128)(2,1)S(1)} %copy-done.5, bf16[224,128,128]{2,1,0:T(8,128)(2,1)} %all-gather.8.cloned.1.call-done.refs_2_, f32[192,3584]{1,0:T(8,128)S(1)} %copy-done.14, ...), custom_call_target="tpu_custom_call" | custom-call | flops 5637144576 | bytes 17170432 | tf_op jit(solution)/shard_map/hidden_grad/pallas_call | solution.py:405
  266.1 3.1 copy-done.8
  269.2 15.4 %normed_grad.1.refs_3_ = bf16[192,4096]{1,0:T(8,128)(2,1)} custom-call(s32[448]{0:T(512)S(1)} %reshape.196.refs_0_, bf16[192,3584]{1,0:T(8,128)(2,1)S(1)} %get-tuple-element.17.refs_1_.refs_2_, bf16[192,3584]{1,0:T(8,128)(2,1)S(1)} %get-tuple-element.18.refs_2_.refs_3_, bf16[224,128,128]{2,1,0:T(8,128)(2,1)S(1)} %copy-done.8, ...), custom_call_target="tpu_custom_call" | custom-call | flops 11274289152 | bytes 19005440 | tf_op jit(solution)/shard_map/normed_grad/pallas_call | solution.py:405
  286.9 6.9 %collective-permute-start.3 = (bf16[28,128,128]{2,1,0:T(8,128)(2,1)S(1)}, bf16[28,128,128]{2,1,0:T(8,128)(2,1)}, u32[]{:S(2)}, u32[]{:S(2)}) collective-permute-start(bf16[28,128,128]{2,1,0:T(8,128)(2,1)S(1)} %get-tuple-element.34.refs_5_), channel_id=1, source_target_pairs={{0,8},{4,12},{8,16},{12,20},{1,9},{5,13},{9,17},{13,21},{2,10},{6,... | collective-permute-start | bytes 2752520 | tf_op jit(solution)/shard_map/ppermute | solution.py:518
  295.5 3.3 copy-done.6
  300.1 11.8 %ffn.1.refs_4_ = bf16[192,4096]{1,0:T(8,128)(2,1)} custom-call(s32[448]{0:T(512)S(1)} %reshape.196.refs_0_, bf16[192,3584]{1,0:T(8,128)(2,1)S(1)} %copy-done.11, bf16[224,128,128]{2,1,0:T(8,128)(2,1)S(1)} %copy-done.6, bf16[192,4096]{1,0:T(8,128)(2,1)} %normed_grad.1.refs_3_), custom_call_target="tpu_custom_call" | custom-call | flops 5637144576 | bytes 10289152 | tf_op jit(solution)/shard_map/ffn/pallas_call | solution.py:405
  312.8 4.2 fusion.8
  317.0 8.6 %collective-permute-start.4 = (bf16[28,128,128]{2,1,0:T(8,128)(2,1)S(1)}, bf16[28,128,128]{2,1,0:T(8,128)(2,1)S(1)}, u32[]{:S(2)}, u32[]{:S(2)}) collective-permute-start(bf16[28,128,128]{2,1,0:T(8,128)(2,1)S(1)} %get-tuple-element.31), channel_id=1, source_target_pairs={{0,8},{4,12},{8,16},{12,20},{16,24},{20,28},{1,9},{5,13},{9,17},{1... | collective-permute-start | bytes 2752520 | tf_op jit(solution)/shard_map/ppermute | solution.py:518
  327.2 6.8 %gate_up_grad.3.other = bf16[4,2,28,128,128]{4,3,2,1,0:T(8,128)(2,1)S(1)} custom-call(s32[224]{0:T(256)S(1)} %reshape.199.refs_0_, bf16[192,4096]{1,0:T(8,128)(2,1)S(1)} %multiply_convert_fusion.refs_1_, bf16[192,3584]{1,0:T(8,128)(2,1)S(1)} %copy-done.18, bf16[192,3584]{1,0:T(8,128)(2,1)S(1)} %copy-done.20, bf16[192,4096]{1,0:T(8,128)(2,1)} %ffn.1.refs_4_), custom_call_target="tpu_custom_call" | custom-call | flops 5637144576 | bytes 11665408 | tf_op jit(solution)/shard_map/gate_up_grad/pallas_call | solution.py:405
  334.0 3.0 copy-done.1
  336.9 6.8 %gate_up_grad.2.own = bf16[4,2,28,128,128]{4,3,2,1,0:T(8,128)(2,1)S(1)} custom-call(s32[224]{0:T(256)S(1)} %reshape.198.refs_0_, bf16[192,4096]{1,0:T(8,128)(2,1)S(1)} %multiply_convert_fusion.refs_1_, bf16[192,3584]{1,0:T(8,128)(2,1)S(1)} %copy-done.18, bf16[192,3584]{1,0:T(8,128)(2,1)S(1)} %copy-done.20, bf16[192,4096]{1,0:T(8,128)(2,1)} %ffn.1.refs_4_), custom_call_target="tpu_custom_call" | custom-call | flops 5637144576 | bytes 11665408 | tf_op jit(solution)/shard_map/gate_up_grad/pallas_call | solution.py:405
  343.7 2.9 copy-done.2
  346.6 2.0 collective-permute-done.6
  348.6 3.3 fusion.9
  352.0 1.9 fusion.18
  355.3 129.7 %gate_up_line.1 = (f32[28,128,128]{2,1,0:T(8,128)}, f32[28,128,128]{2,1,0:T(8,128)}, f32[8,128]{1,0:T(8,128)}, f32[16,128]{1,0:T(8,128)}) custom-call(bf16[4,2,28,128,128]{4,3,2,1,0:T(8,128)(2,1)} %copy-done.2, bf16[4,2,28,128,128]{4,3,2,1,0:T(8,128)(2,1)} %copy-done.1, f32[8,128]{1,0:T(8,128)} %bitcast.72, f32[16,128]{1,0:T(8,128)} %pad_bitcast_fusion.gain_in), custom_call_target="tpu_custom_call" | custom-call | flops 3670016 | bytes 234881024 | tf_op jit(solution)/shard_map/gate_up_line/pallas_call | solution.py:353
  488.3 2.5 multiply_subtract_fusion
  (120 shorter events, 35.6 us)
Async XLA Ops:
  7.2 2.3 copy-start.36
  7.2 8.1 %copy-start.35 = (s32[224,2]{0,1:T(2,128)S(1)}, s32[224,2]{0,1:T(2,128)}, u32[]{:S(2)}) copy-start(s32[224,2]{0,1:T(2,128)} %param.16) | copy-start | bytes 5380
  7.2 11.4 %copy-start.37 = (f32[4]{0:T(128)S(1)}, f32[4]{0:T(128)}, u32[]{:S(2)}) copy-start(f32[4]{0:T(128)} %param.10) | copy-start | bytes 52
  7.2 78.6 %all-gather.6.cloned.1.call-start = ((), (), s32[]{:S(2)}) async-start(), calls=%async_computation.3 | async-start | bytes 8257536 | tf_op jit(solution)/shard_map/all_gather | solution.py:446
  7.9 151.5 %all-gather.4.cloned.1.call-start = ((), (), s32[]{:S(2)}) async-start(), calls=%async_computation.2 | async-start | bytes 8257536 | tf_op jit(solution)/shard_map/all_gather | solution.py:447
  8.7 238.8 %all-gather.8.cloned.1.call-start = ((), (), s32[]{:S(2)}) async-start(), calls=%async_computation.4 | async-start | bytes 8257536 | tf_op jit(solution)/shard_map/all_gather | solution.py:448
  9.4 342.6 %reduce-scatter.5.cloned.1.call-start = ((), (), s32[]{:S(2)}) async-start(), calls=%async_computation.6 | async-start | bytes 1966080 | tf_op jit(solution)/shard_map/reduce_scatter | solution.py:556
  27.0 4.8 copy-start.21
  86.9 3.1 copy-start.7
  101.1 74.1 %copy-start.4 = (bf16[192,4096]{1,0:T(8,128)(2,1)S(1)}, bf16[192,4096]{1,0:T(8,128)(2,1)}, u32[]{:S(2)}) copy-start(bf16[192,4096]{1,0:T(8,128)(2,1)} %refs_1_.1) | copy-start | bytes 4718596
  175.1 7.1 %copy-start.9 = (bf16[192,3584]{1,0:T(8,128)(2,1)}, bf16[192,3584]{1,0:T(8,128)(2,1)S(1)}, u32[]{:S(2)}) copy-start(bf16[192,3584]{1,0:T(8,128)(2,1)S(1)} %get-tuple-element.15.refs_1_) | copy-start | bytes 4128772
  182.2 8.0 %collective-permute-start = (bf16[4,1,28,128,128]{4,3,2,1,0:T(8,128)(2,1)}, bf16[4,1,28,128,128]{4,3,2,1,0:T(8,128)(2,1)}, u32[]{:S(2)}, u32[]{:S(2)}) collective-permute-start(bf16[4,1,28,128,128]{4,3,2,1,0:T(8,128)(2,1)} %down_grad.2.refs_3_), channel_id=1, source_target_pairs={{0,4},{4,0},{8,12},{12,8},{16,20},{20,16},{24,28},{28,24},{1,5},{5... | collective-permute-start | bytes 11010056 | tf_op jit(solution)/shard_map/ppermute | solution.py:527
  190.3 4.5 copy-start
  194.8 41.8 %collective-permute-start.1 = (bf16[28,128,128]{2,1,0:T(8,128)(2,1)}, bf16[28,128,128]{2,1,0:T(8,128)(2,1)S(1)}, u32[]{:S(2)}, u32[]{:S(2)}) collective-permute-start(bf16[28,128,128]{2,1,0:T(8,128)(2,1)} %get-tuple-element.36), channel_id=1, source_target_pairs={{0,8},{4,12},{1,9},{5,13},{2,10},{6,14},{3,11},{7,15}} | collective-permute-start | bytes 2752520 | tf_op jit(solution)/shard_map/ppermute | solution.py:518
  196.1 41.4 %collective-permute-start.2 = (bf16[28,128,128]{2,1,0:T(8,128)(2,1)S(1)}, bf16[28,128,128]{2,1,0:T(8,128)(2,1)}, u32[]{:S(2)}, u32[]{:S(2)}) collective-permute-start(bf16[28,128,128]{2,1,0:T(8,128)(2,1)S(1)} %get-tuple-element.35), channel_id=1, source_target_pairs={{24,16},{28,20},{25,17},{29,21},{26,18},{30,22},{27,19},{31,23}} | collective-permute-start | bytes 2752520 | tf_op jit(solution)/shard_map/ppermute | solution.py:519
  266.1 3.1 copy-start.8
  286.8 201.4 %reduce-scatter.3.cloned.1.call-start = ((), (), s32[]{:S(2)}) async-start(), calls=%async_computation.5 | async-start | bytes 1966080 | tf_op jit(solution)/shard_map/reduce_scatter | solution.py:557
  286.9 25.9 %collective-permute-start.3 = (bf16[28,128,128]{2,1,0:T(8,128)(2,1)S(1)}, bf16[28,128,128]{2,1,0:T(8,128)(2,1)}, u32[]{:S(2)}, u32[]{:S(2)}) collective-permute-start(bf16[28,128,128]{2,1,0:T(8,128)(2,1)S(1)} %get-tuple-element.34.refs_5_), channel_id=1, source_target_pairs={{0,8},{4,12},{8,16},{12,20},{1,9},{5,13},{9,17},{13,21},{2,10},{6,... | collective-permute-start | bytes 2752520 | tf_op jit(solution)/shard_map/ppermute | solution.py:518
  293.8 19.1 %collective-permute-start.5 = (bf16[28,128,128]{2,1,0:T(8,128)(2,1)S(1)}, bf16[28,128,128]{2,1,0:T(8,128)(2,1)}, u32[]{:S(2)}, u32[]{:S(2)}) collective-permute-start(bf16[28,128,128]{2,1,0:T(8,128)(2,1)S(1)} %get-tuple-element.33.refs_6_), channel_id=1, source_target_pairs={{24,16},{28,20},{16,8},{20,12},{25,17},{29,21},{17,9},{21,13},{26,... | collective-permute-start | bytes 2752520 | tf_op jit(solution)/shard_map/ppermute | solution.py:519
  295.4 3.3 copy-start.6
  312.0 15.2 %copy-start.18 = (bf16[192,3584]{1,0:T(8,128)(2,1)S(1)}, bf16[192,3584]{1,0:T(8,128)(2,1)}, u32[]{:S(2)}) copy-start(bf16[192,3584]{1,0:T(8,128)(2,1)} %copy-done.17) | copy-start | bytes 4128772
  312.0 15.2 %copy-start.20 = (bf16[192,3584]{1,0:T(8,128)(2,1)S(1)}, bf16[192,3584]{1,0:T(8,128)(2,1)}, u32[]{:S(2)}) copy-start(bf16[192,3584]{1,0:T(8,128)(2,1)} %copy-done.19) | copy-start | bytes 4128772
  317.0 29.6 %collective-permute-start.4 = (bf16[28,128,128]{2,1,0:T(8,128)(2,1)S(1)}, bf16[28,128,128]{2,1,0:T(8,128)(2,1)S(1)}, u32[]{:S(2)}, u32[]{:S(2)}) collective-permute-start(bf16[28,128,128]{2,1,0:T(8,128)(2,1)S(1)} %get-tuple-element.31), channel_id=1, source_target_pairs={{0,8},{4,12},{8,16},{12,20},{16,24},{20,28},{1,9},{5,13},{9,17},{1... | collective-permute-start | bytes 2752520 | tf_op jit(solution)/shard_map/ppermute | solution.py:518
  325.7 23.0 %collective-permute-start.6 = (bf16[28,128,128]{2,1,0:T(8,128)(2,1)S(1)}, bf16[28,128,128]{2,1,0:T(8,128)(2,1)S(1)}, u32[]{:S(2)}, u32[]{:S(2)}) collective-permute-start(bf16[28,128,128]{2,1,0:T(8,128)(2,1)S(1)} %get-tuple-element.32), channel_id=1, source_target_pairs={{24,16},{28,20},{16,8},{20,12},{8,0},{12,4},{25,17},{29,21},{17,9}... | collective-permute-start | bytes 2752520 | tf_op jit(solution)/shard_map/ppermute | solution.py:519
  333.9 3.0 copy-start.1
  343.7 2.9 copy-start.2
  346.6 5.4 %dynamic-slice-start = ((f32[4096]{0:T(1024)}, s32[]{:T(128)}), f32[1024]{0:T(1024)S(1)}, s32[]{:S(2)}) async-start(f32[4096]{0:T(1024)} %param.12, s32[]{:T(128)} %select_n.73), calls=%async_computation.7 | async-start | bytes 8704 | tf_op jit(solution)/shard_map/dynamic_slice | solution.py:451
  352.0 2.1 copy-start.25
  352.0 2.1 copy-start.27
  352.0 2.1 copy-start.29
  485.0 5.8 %copy-start.31 = (f32[28,128,128]{2,1,0:T(8,128)S(1)}, f32[28,128,128]{2,1,0:T(8,128)}, u32[]{:S(2)}) copy-start(f32[28,128,128]{2,1,0:T(8,128)} %get-tuple-element.69) | copy-start | bytes 5505028
  490.7 2.2 copy-start.30
  (19 other events, 24.5 us)
Sparse Core Ops, SparseCore 0:
  9.7 76.0 all-gather.5
  87.4 71.9 all-gather.3
  161.1 86.2 all-gather.7
  287.0 34.6 reduce-scatter.4
  325.1 30.9 reduce-scatter.2
